TPU v7x, 32 devices: a whole 2x2x4 slice. The times are simulated.
32 devices in a mesh: ctx: 8 (over z, core), exp: 4 (over y, x).
Axes of the slice: x: 2, y: 2, z: 4, core: 2. Of those that a mesh axis runs over, the one named last changes fastest.
Arguments:
- tokens: bfloat16 [4, 2048, 1536], P('exp', 'ctx'), may hold values from -6 to 6
- cotangent: bfloat16 [4, 2048, 1536], P('exp', 'ctx'), may hold values from -6 to 6
- routes: int32 [4, 2048, 2], P('exp', 'ctx'), may hold values from 0 to 15, all different within a row; in each aligned block of 256 rows (0 to 255, 256 to 511, ..., all dimensions but the last counted through in order) at most 48 rows name the same one
- lengths: int32 [4, 3], P('exp'), may hold values from 1 to 1024, 2048 in all within a row
- block_order: int32 [4, 16], P('exp'), may hold values from 0 to 15, each once within a row
- gain_attn: float32 [1536], P(('ctx', 'exp')), may hold values from 0.5 to 1.5
- qkv_weight: float32 [1536, 2560], P(('ctx', 'exp')), may hold values from -0.15625 to 0.15625
- out_weight: float32 [1536, 1536], P(('ctx', 'exp')), may hold values from -1.5 to 1.5
- gain_moe: float32 [1536], P(('ctx', 'exp')), may hold values from 0.5 to 1.5
- router_weight: float32 [1536, 16], P(('ctx', 'exp')), may hold values from -0.109375 to 0.109375
- expert_in: float32 [16, 1536, 2048], P('exp', 'ctx'), may hold values from -0.15625 to 0.15625
- expert_out: float32 [16, 1024, 1536], P('exp', 'ctx'), may hold values from -0.375 to 0.375
Outputs:
- block_out: bfloat16 [4, 2048, 1536], P('exp', 'ctx')
- d_tokens: bfloat16 [4, 2048, 1536], P('exp', 'ctx')
- d_gain_attn: float32 [1536], P(('ctx', 'exp'))
- d_qkv_weight: float32 [1536, 2560], P(('ctx', 'exp'))
- d_out_weight: float32 [1536, 1536], P(('ctx', 'exp'))
- d_gain_moe: float32 [1536], P(('ctx', 'exp'))
- d_router_weight: float32 [1536, 16], P(('ctx', 'exp'))
- d_expert_in: float32 [16, 1536, 2048], P('exp', 'ctx')
- d_expert_out: float32 [16, 1024, 1536], P('exp', 'ctx')
Inputs may be any that keep to these rules, and one draw needn't show every extreme that they name: `routes`: among the rows of one device no expert is named more than 48 times; the two experts of a row differ. The lengths of a pack sum to 2048; the longest is 1024. `block_order`: each row is a permutation.
All inputs are finite; a program needn't handle non-finite values.
Results may differ from a plain program's by a relative error of at most 0.025.
Values may be sent and summed in bfloat16 or wider, within the bound.
A program may use at most 256 MiB of HBM per device.

v0:
```python
import math

import jax
import jax.numpy as jnp
from jax import lax
from jax.sharding import PartitionSpec as P

D = 1536
HEADS = 24
KV_HEADS = 8
HEAD = 64
FF = 1024
EXPERTS = 16
BLK = 128
CAP = 48


epsilon = 1e-05
far_negative = -1e30


def norm_scale(values):
    return lax.rsqrt(jnp.mean(values * values, axis=-1, keepdims=True) + epsilon)


def pack_layout(lengths, block_ids):
    offsets = jnp.arange(BLK, dtype=jnp.int32)
    position = (block_ids[:, None] * BLK + offsets[None, :]).reshape(block_ids.shape[0] * BLK)
    bounds = jnp.cumsum(lengths)
    document = jnp.sum((position[:, None] >= bounds[None, :]).astype(jnp.int32), axis=1)
    return (position, document)


def visible_mask(query_pos, query_doc, key_pos, key_doc):
    return (query_doc[:, None] == key_doc[None, :]) & (key_pos[None, :] <= query_pos[:, None])


def online_block(softmax_state, queries, key_block, value_block, visible):
    running_max, denominator, summed = softmax_state
    scores = jnp.einsum(
        "tkgd,nkd->kgtn", queries, key_block, preferred_element_type=jnp.float32
    ) * HEAD ** (-0.5)
    scores = jnp.where(visible[None, None], scores, far_negative)
    new_max = jnp.maximum(running_max, jnp.max(scores, axis=-1))
    weights = jnp.where(visible[None, None], jnp.exp(scores - new_max[..., None]), 0.0)
    factor = jnp.exp(running_max - new_max)
    denominator = denominator * factor + jnp.sum(weights, axis=-1)
    summed = summed * factor[..., None] + jnp.einsum(
        "kgtn,nkd->kgtd",
        weights.astype(jnp.bfloat16),
        value_block,
        preferred_element_type=jnp.float32,
    )
    return (new_max, denominator, summed)


def fold_keys(softmax_state, key_piece, first_row, queries, query_pos, query_doc, all_pos, all_doc):
    key_rows, value_rows = key_piece
    piece_rows = key_rows.shape[0]
    step_rows = math.gcd(piece_rows, queries.shape[0])
    block_count = piece_rows // step_rows
    key_blocks = key_rows.reshape(block_count, step_rows, KV_HEADS, HEAD)
    value_blocks = value_rows.reshape(block_count, step_rows, KV_HEADS, HEAD)
    offsets = first_row + jnp.arange(block_count, dtype=jnp.int32) * step_rows

    def advance(running, block_item):
        key_block, value_block, offset = block_item
        key_pos = lax.dynamic_slice_in_dim(all_pos, offset, step_rows)
        key_doc = lax.dynamic_slice_in_dim(all_doc, offset, step_rows)
        visible = visible_mask(query_pos, query_doc, key_pos, key_doc)
        return (online_block(running, queries, key_block, value_block, visible), None)

    softmax_state, _ = lax.scan(advance, softmax_state, (key_blocks, value_blocks, offsets))
    return softmax_state


def backward_block(
    grad_queries, block_item, queries, grad_attended, logsum, delta, query_pos, query_doc
):
    key_block, value_block, key_pos, key_doc = block_item
    scale = HEAD ** (-0.5)
    visible = visible_mask(query_pos, query_doc, key_pos, key_doc)[None, None]
    scores = (
        jnp.einsum("tkgd,nkd->kgtn", queries, key_block, preferred_element_type=jnp.float32) * scale
    )
    scores = jnp.where(visible, scores, far_negative)
    probs = jnp.where(visible, jnp.exp(scores - logsum[..., None]), 0.0)
    grad_probs = jnp.einsum(
        "tkgd,nkd->kgtn", grad_attended, value_block, preferred_element_type=jnp.float32
    )
    grad_scores = (probs * (grad_probs - delta[..., None])).astype(jnp.bfloat16)
    grad_queries = (
        grad_queries
        + jnp.einsum("kgtn,nkd->tkgd", grad_scores, key_block, preferred_element_type=jnp.float32)
        * scale
    )
    grad_keys = (
        jnp.einsum("kgtn,tkgd->nkd", grad_scores, queries, preferred_element_type=jnp.float32)
        * scale
    )
    grad_values = jnp.einsum(
        "kgtn,tkgd->nkd",
        probs.astype(jnp.bfloat16),
        grad_attended,
        preferred_element_type=jnp.float32,
    )
    block_rows = key_block.shape[0]
    return (
        grad_queries,
        jnp.concatenate(
            [
                grad_keys.reshape(block_rows, KV_HEADS * HEAD),
                grad_values.reshape(block_rows, KV_HEADS * HEAD),
            ],
            axis=1,
        ),
    )


def on_device(
    tokens,
    cotangent,
    routes,
    lengths,
    block_order,
    gain_attn,
    qkv_weight,
    out_weight,
    gain_moe,
    router_weight,
    expert_in,
    expert_out,
):
    tok_rows = tokens.shape[1]
    group_size = HEADS // KV_HEADS
    head_width = HEADS * HEAD
    kv_width = KV_HEADS * HEAD
    exp_local = expert_in.shape[0]
    owner_count = EXPERTS // exp_local
    gain_first, w_qkv, w_attn_out, gain_second, w_router = (
        lax.all_gather(gain_attn.astype(jnp.bfloat16), ("ctx", "exp"), axis=0, tiled=True),
        lax.all_gather(qkv_weight.astype(jnp.bfloat16), ("ctx", "exp"), axis=0, tiled=True),
        lax.all_gather(out_weight.astype(jnp.bfloat16), ("ctx", "exp"), axis=0, tiled=True),
        lax.all_gather(gain_moe.astype(jnp.bfloat16), ("ctx", "exp"), axis=0, tiled=True),
        lax.all_gather(router_weight.astype(jnp.bfloat16), ("ctx", "exp"), axis=0, tiled=True),
    )
    w_in, w_down = (
        lax.all_gather(expert_in.astype(jnp.bfloat16), "ctx", axis=1, tiled=True),
        lax.all_gather(expert_out.astype(jnp.bfloat16), "ctx", axis=1, tiled=True),
    )
    inputs = tokens[0].astype(jnp.float32)
    all_pos, all_doc = pack_layout(lengths[0], block_order[0])
    pack_rows = all_pos.shape[0]
    row_start = lax.axis_index("ctx") * tok_rows
    query_pos = lax.dynamic_slice_in_dim(all_pos, row_start, tok_rows)
    query_doc = lax.dynamic_slice_in_dim(all_doc, row_start, tok_rows)
    scale_first = norm_scale(inputs)
    norm_first = inputs * scale_first
    first = (norm_first * gain_first.astype(jnp.float32)).astype(jnp.bfloat16)
    projected = jnp.dot(first, w_qkv, preferred_element_type=jnp.float32).astype(jnp.bfloat16)
    queries = projected[:, :head_width].reshape(tok_rows, KV_HEADS, group_size, HEAD)
    keys = projected[:, head_width : head_width + kv_width]
    values = projected[:, head_width + kv_width :]
    start_state = (
        jnp.full((KV_HEADS, group_size, tok_rows), far_negative, jnp.float32),
        jnp.zeros((KV_HEADS, group_size, tok_rows), jnp.float32),
        jnp.zeros((KV_HEADS, group_size, tok_rows, HEAD), jnp.float32),
    )
    keys_all, values_all = (
        lax.all_gather(keys, "ctx", axis=0, tiled=True),
        lax.all_gather(values, "ctx", axis=0, tiled=True),
    )
    final_state = fold_keys(
        start_state, (keys_all, values_all), 0, queries, query_pos, query_doc, all_pos, all_doc
    )
    running_max, denominator, summed = final_state
    attn_exact = summed / denominator[..., None]
    logsum = running_max + jnp.log(denominator)
    attended = (
        jnp.transpose(attn_exact, (2, 0, 1, 3)).reshape(tok_rows, head_width).astype(jnp.bfloat16)
    )
    middle = inputs + jnp.dot(attended, w_attn_out, preferred_element_type=jnp.float32)
    scale_second = norm_scale(middle)
    norm_second = middle * scale_second
    second = (norm_second * gain_second.astype(jnp.float32)).astype(jnp.bfloat16)
    logits = jnp.dot(second, w_router, preferred_element_type=jnp.float32)
    route_hot = (
        routes[0][:, :, None] == jnp.arange(EXPERTS, dtype=jnp.int32)[None, None, :]
    ).astype(jnp.float32)
    chosen = jnp.sum(route_hot * logits[:, None, :], axis=-1)
    gates = jax.nn.softmax(chosen, axis=-1)
    flat_hot = route_hot.reshape(tok_rows * 2, EXPERTS)
    ranks = jnp.cumsum(flat_hot, axis=0) - 1.0
    slot_index = jnp.sum(ranks * flat_hot, axis=1).astype(jnp.int32)
    target = routes[0].reshape(tok_rows * 2) * CAP + slot_index
    send_rows = (
        jnp.zeros((EXPERTS * CAP, D), jnp.bfloat16).at[target].set(jnp.repeat(second, 2, axis=0))
    )
    received = lax.all_to_all(
        send_rows.reshape(owner_count, exp_local, CAP, D),
        "exp",
        split_axis=0,
        concat_axis=2,
        tiled=True,
    )[0]
    gate_up = jnp.einsum("ecd,edf->ecf", received, w_in, preferred_element_type=jnp.float32)
    gate_part = gate_up[..., :FF]
    up_part = gate_up[..., FF:]
    sigmoid_gate = jax.nn.sigmoid(gate_part)
    silu_gate = gate_part * sigmoid_gate
    hidden = (silu_gate * up_part).astype(jnp.bfloat16)
    expert_rows = jnp.einsum(
        "ecf,efd->ecd", hidden, w_down, preferred_element_type=jnp.float32
    ).astype(jnp.bfloat16)
    returned = lax.all_to_all(expert_rows[None], "exp", split_axis=2, concat_axis=0, tiled=True)
    picked = returned.reshape(EXPERTS * CAP, D)[target].reshape(tok_rows, 2, D).astype(jnp.float32)
    block_out = (middle + jnp.sum(gates[:, :, None] * picked, axis=1)).astype(jnp.bfloat16)
    gain_first, w_qkv, w_attn_out, gain_second, w_router = (
        lax.all_gather(gain_attn.astype(jnp.bfloat16), ("ctx", "exp"), axis=0, tiled=True),
        lax.all_gather(qkv_weight.astype(jnp.bfloat16), ("ctx", "exp"), axis=0, tiled=True),
        lax.all_gather(out_weight.astype(jnp.bfloat16), ("ctx", "exp"), axis=0, tiled=True),
        lax.all_gather(gain_moe.astype(jnp.bfloat16), ("ctx", "exp"), axis=0, tiled=True),
        lax.all_gather(router_weight.astype(jnp.bfloat16), ("ctx", "exp"), axis=0, tiled=True),
    )
    w_in, w_down = (
        lax.all_gather(expert_in.astype(jnp.bfloat16), "ctx", axis=1, tiled=True),
        lax.all_gather(expert_out.astype(jnp.bfloat16), "ctx", axis=1, tiled=True),
    )
    grad_y = cotangent[0].astype(jnp.float32)
    grad_gates = jnp.sum(grad_y[:, None, :] * picked, axis=-1)
    grad_rows = (
        (gates[:, :, None] * grad_y[:, None, :]).astype(jnp.bfloat16).reshape(tok_rows * 2, D)
    )
    grad_send = jnp.zeros((EXPERTS * CAP, D), jnp.bfloat16).at[target].set(grad_rows)
    grad_received = lax.all_to_all(
        grad_send.reshape(owner_count, exp_local, CAP, D),
        "exp",
        split_axis=0,
        concat_axis=2,
        tiled=True,
    )[0]
    grad_hidden = jnp.einsum(
        "ecd,efd->ecf", grad_received, w_down, preferred_element_type=jnp.float32
    )
    grad_down = jnp.einsum(
        "ecf,ecd->efd", hidden, grad_received, preferred_element_type=jnp.float32
    )
    grad_gate = grad_hidden * up_part * sigmoid_gate * (1.0 + gate_part * (1.0 - sigmoid_gate))
    grad_up = grad_hidden * silu_gate
    grad_gate_up = jnp.concatenate([grad_gate, grad_up], axis=-1).astype(jnp.bfloat16)
    grad_in = jnp.einsum("ecd,ecf->edf", received, grad_gate_up, preferred_element_type=jnp.float32)
    grad_back = jnp.einsum(
        "ecf,edf->ecd", grad_gate_up, w_in, preferred_element_type=jnp.float32
    ).astype(jnp.bfloat16)
    grad_returned = lax.all_to_all(grad_back[None], "exp", split_axis=2, concat_axis=0, tiled=True)
    grad_second = jnp.sum(
        grad_returned.reshape(EXPERTS * CAP, D)[target].reshape(tok_rows, 2, D).astype(jnp.float32),
        axis=1,
    )
    grad_chosen = gates * (grad_gates - jnp.sum(gates * grad_gates, axis=-1, keepdims=True))
    grad_logits = jnp.sum(grad_chosen[:, :, None] * route_hot, axis=1).astype(jnp.bfloat16)
    grad_router = jnp.einsum("td,te->de", second, grad_logits, preferred_element_type=jnp.float32)
    grad_second = grad_second + jnp.einsum(
        "te,de->td", grad_logits, w_router, preferred_element_type=jnp.float32
    )
    grad_gain_second = jnp.sum(grad_second * norm_second, axis=0)
    grad_norm_second = grad_second * gain_second.astype(jnp.float32)
    grad_middle = grad_y + scale_second * (
        grad_norm_second
        - norm_second * jnp.mean(grad_norm_second * norm_second, axis=-1, keepdims=True)
    )
    grad_branch = grad_middle.astype(jnp.bfloat16)
    grad_attn_out = jnp.einsum(
        "th,td->hd", attended, grad_branch, preferred_element_type=jnp.float32
    )
    grad_attended = (
        jnp.einsum("td,hd->th", grad_branch, w_attn_out, preferred_element_type=jnp.float32)
        .astype(jnp.bfloat16)
        .reshape(tok_rows, KV_HEADS, group_size, HEAD)
    )
    delta = jnp.einsum("tkgd,kgtd->kgt", grad_attended.astype(jnp.float32), attn_exact)
    block_count = pack_rows // tok_rows

    def back_step(grad_queries, block_item):
        return backward_block(
            grad_queries, block_item, queries, grad_attended, logsum, delta, query_pos, query_doc
        )

    grad_queries, grad_kv_blocks = lax.scan(
        back_step,
        jnp.zeros((tok_rows, KV_HEADS, group_size, HEAD), jnp.float32),
        (
            keys_all.reshape(block_count, tok_rows, KV_HEADS, HEAD),
            values_all.reshape(block_count, tok_rows, KV_HEADS, HEAD),
            all_pos.reshape(block_count, tok_rows),
            all_doc.reshape(block_count, tok_rows),
        ),
    )
    grad_kv = lax.psum_scatter(
        grad_kv_blocks.reshape(pack_rows, 2 * kv_width).astype(jnp.bfloat16),
        "ctx",
        scatter_dimension=0,
        tiled=True,
    ).astype(jnp.float32)
    grad_projected = jnp.concatenate(
        [grad_queries.reshape(tok_rows, head_width), grad_kv], axis=1
    ).astype(jnp.bfloat16)
    grad_qkv = jnp.einsum("td,tc->dc", first, grad_projected, preferred_element_type=jnp.float32)
    grad_first = jnp.einsum("tc,dc->td", grad_projected, w_qkv, preferred_element_type=jnp.float32)
    grad_gain_first = jnp.sum(grad_first * norm_first, axis=0)
    grad_norm_first = grad_first * gain_first.astype(jnp.float32)
    grad_inputs = grad_middle + scale_first * (
        grad_norm_first
        - norm_first * jnp.mean(grad_norm_first * norm_first, axis=-1, keepdims=True)
    )
    sum_gain_first, sum_qkv, sum_attn_out, sum_gain_second, sum_router = (
        lax.psum_scatter(grad_gain_first, ("ctx", "exp"), scatter_dimension=0, tiled=True),
        lax.psum_scatter(grad_qkv, ("ctx", "exp"), scatter_dimension=0, tiled=True),
        lax.psum_scatter(grad_attn_out, ("ctx", "exp"), scatter_dimension=0, tiled=True),
        lax.psum_scatter(grad_gain_second, ("ctx", "exp"), scatter_dimension=0, tiled=True),
        lax.psum_scatter(grad_router, ("ctx", "exp"), scatter_dimension=0, tiled=True),
    )
    sum_in, sum_down = (
        lax.psum_scatter(
            grad_in.astype(jnp.bfloat16), "ctx", scatter_dimension=1, tiled=True
        ).astype(jnp.float32),
        lax.psum_scatter(
            grad_down.astype(jnp.bfloat16), "ctx", scatter_dimension=1, tiled=True
        ).astype(jnp.float32),
    )
    return (
        block_out[None],
        grad_inputs.astype(jnp.bfloat16)[None],
        sum_gain_first,
        sum_qkv,
        sum_attn_out,
        sum_gain_second,
        sum_router,
        sum_in,
        sum_down,
    )


def solution(mesh):
    return jax.shard_map(
        on_device,
        mesh=mesh,
        in_specs=(
            P("exp", "ctx", None),
            P("exp", "ctx", None),
            P("exp", "ctx", None),
            P("exp", None),
            P("exp", None),
            P(("ctx", "exp")),
            P(("ctx", "exp"), None),
            P(("ctx", "exp"), None),
            P(("ctx", "exp")),
            P(("ctx", "exp"), None),
            P("exp", "ctx", None),
            P("exp", "ctx", None),
        ),
        out_specs=(
            P("exp", "ctx", None),
            P("exp", "ctx", None),
            P(("ctx", "exp")),
            P(("ctx", "exp"), None),
            P(("ctx", "exp"), None),
            P(("ctx", "exp")),
            P(("ctx", "exp"), None),
            P("exp", "ctx", None),
            P("exp", "ctx", None),
        ),
        check_vma=False,
    )
```

profile of v0, /device:TPU:8, one launch (start us, length us, event | category | flops | bytes accessed | tf_op | source)
XLA Modules:
  0.0 1679.4 jit_solution(8121719508180482363)
XLA Ops:
  10.8 41.0 %all-reduce.5 = (bf16[1536]{0:T(1024)(128)(2,1)S(1)}, bf16[1536]{0:T(1024)(128)(2,1)S(1)}) all-reduce(bf16[1536]{0:T(1024)(128)(2,1)S(1)} %dynamic-update-slice, bf16[1536]{0:T(1024)(128)(2,1)S(1)} %dynamic-update-slice.1), channel_id=1, replica_groups=mesh['ctx'=8,'exp'=4] {'ctx','exp'}, use_global_device_ids=true, to_apply=%add | all-reduce | flops 3072 | bytes 12288
  53.2 35.2 %all-gather.8.cloned.1.call-done = bf16[1536,2560]{1,0:T(8,128)(2,1)} async-done(((bf16[48,2560]{1,0:T(8,128)(2,1)}), bf16[1536,2560]{1,0:T(8,128)(2,1)}) %all-gather.8.cloned.1.call-update) | async-done | bytes 7864336 | tf_op jit(solution)/shard_map/all_gather | solution.py:142
  109.1 14.8 all-gather.10.cloned.1.call-done
  123.8 6.1 reshape.511
  135.1 19.5 %all-gather.12.cloned.1.call-done = bf16[2048,512]{1,0:T(8,128)(2,1)} async-done(((bf16[256,512]{1,0:T(8,128)(2,1)}), bf16[2048,512]{1,0:T(8,128)(2,1)}) %all-gather.12.cloned.1.call-update) | async-done | bytes 2097168 | tf_op jit(solution)/shard_map/all_gather | solution.py:171
  154.6 6.1 reshape.512
  165.9 132.6 %while.28 = (s32[]{:T(128)}, f32[8,3,256]{2,1,0:T(4,128)S(1)}, f32[8,3,256]{2,1,0:T(4,128)S(1)}, f32[8,3,256,64]{2,3,1,0:T(8,128)}, s32[256]{0:T(256)S(1)}, /*in...) while((s32[]{:T(128)}, f32[8,3,256]{2,1,0:T(4,128)S(1)}, ...), condition=%wide.region_6.7_spmd.clone, body=%wide.region_3.6_spmd.clone.sunk | while | flops 424507392 | bytes 49160440 | solution.py:73
  308.0 5.9 scatter_custom_fusion
  328.0 83.1 %all-gather = bf16[32,48,16]{1,2,0:T(8,128)(2,1)S(1)} all-gather(bf16[1,48,16]{1,2,0:T(8,128)(2,1)S(1)} %convert_bitcast_fusion), channel_id=1, replica_groups=mesh['ctx'=8,'exp'=4] {'ctx','exp'}, dimensions={0}, use_global_device_ids=true | all-gather | bytes 50688 | tf_op jit(solution)/shard_map/all_gather | solution.py:145
  412.1 6.1 scatter_custom_fusion.1
  424.7 24.8 %all-to-all-done.2 = bf16[4,4,48,1536]{3,2,1,0:T(8,128)(2,1)} async-done(((bf16[4,4,48,1536]{3,2,1,0:T(8,128)(2,1)}), bf16[4,4,48,1536]{3,2,1,0:T(8,128)(2,1)}, u32[]{:S(2)}, u32[]{:S(2)}) %all-to-all-start.2) | async-done | bytes 2359328 | tf_op jit(solution)/shard_map/all_to_all | solution.py:235
  453.0 14.3 fusion.88
  467.3 88.6 %all-gather.18.cloned.1.call-done = bf16[4,1024,1536]{2,1,0:T(8,128)(2,1)} async-done(((bf16[4,128,1536]{2,1,0:T(8,128)(2,1)}), bf16[4,1024,1536]{2,1,0:T(8,128)(2,1)}) %all-gather.18.cloned.1.call-update) | async-done | bytes 12582928 | tf_op jit(solution)/shard_map/all_gather | solution.py:149
  555.9 13.3 multiply_convert_fusion.1
  569.2 15.2 fusion.45
  593.9 7.2 fusion.44
  604.3 18.0 %all-to-all-done.3 = bf16[1,4,192,1536]{3,1,0,2:T(4,128)(2,1)} async-done(((bf16[1,4,192,1536]{3,1,0,2:T(4,128)(2,1)}), bf16[1,4,192,1536]{3,1,0,2:T(4,128)(2,1)}, u32[]{:S(2)}, u32[]{:S(2)}) %all-to-all-start.3) | async-done | bytes 2359328 | tf_op jit(solution)/shard_map/all_to_all | solution.py:255
  639.2 6.8 reduce_sum.151
  646.0 8.4 all-to-all-done.1
  664.3 9.6 multiply_reduce_fusion
  684.8 141.3 %while.29 = (s32[]{:T(128)}, f32[256,8,3,64]{0,3,2,1:T(8,128)}, bf16[8,256,1024]{2,1,0:T(8,128)(2,1)}, bf16[8,256,8,64]{1,3,2,0:T(8,128)(2,1)}, s32[256]{0:T(256...) while((s32[]{:T(128)}, f32[256,8,3,64]{0,3,2,1:T(8,128)}, ...), condition=%wide.region_23.24_spmd.clone, body=%wide.region_22.23_spmd.clone.sunk | while | flops 1028194304 | bytes 95961384 | solution.py:289
  828.6 7.9 convolution_convert_fusion.1
  838.3 14.0 convolution_convert_fusion
  860.4 12.3 reduce-scatter.9.cloned.1.call-done
  874.0 7.9 fusion.64
  881.9 93.9 %reduce-scatter.19.cloned.1.call-done = f32[48,16]{1,0:T(8,128)} async-done(((f32[1536,16]{1,0:T(8,128)}), f32[48,16]{1,0:T(8,128)}) %reduce-scatter.19.cloned.1.call-update) | async-done | bytes 3088
  977.2 7.1 fusion.56
  984.3 41.0 %all-reduce.4 = (f32[1536]{0:T(1024)S(1)}, f32[1536]{0:T(1024)S(1)}) all-reduce(f32[1536]{0:T(1024)S(1)} %get-tuple-element.356, f32[1536]{0:T(1024)S(1)} %get-tuple-element.352), channel_id=3, replica_groups=mesh['ctx'=8,'exp'=4] {'ctx','exp'}, use_global_device_ids=true, to_apply=%region_27.28.clone | all-reduce | flops 3072 | bytes 24576
  1029.2 75.6 %reduce-scatter.17.cloned.1.call-done = bf16[4,128,1536]{2,1,0:T(8,128)(2,1)} async-done(((bf16[4,1024,1536]{2,1,0:T(8,128)(2,1)}), bf16[4,128,1536]{2,1,0:T(8,128)(2,1)}) %reduce-scatter.17.cloned.1.call-update) | async-done | bytes 1572880 | tf_op jit(solution)/shard_map/reduce_scatter | solution.py:327
  1108.3 244.3 %reduce-scatter.15.cloned.1.call-done = bf16[4,192,2048]{2,1,0:T(8,128)(2,1)} async-done(((bf16[4,1536,2048]{2,1,0:T(8,128)(2,1)}), bf16[4,192,2048]{2,1,0:T(8,128)(2,1)}) %reduce-scatter.15.cloned.1.call-update) | async-done | bytes 3145744 | tf_op jit(solution)/shard_map/reduce_scatter | solution.py:324
  1358.0 137.6 %reduce-scatter.13.cloned.1.call-done = f32[48,1536]{1,0:T(8,128)} async-done(((f32[1536,1536]{1,0:T(8,128)}), f32[48,1536]{1,0:T(8,128)}) %reduce-scatter.13.cloned.1.call-update) | async-done | bytes 294928 | tf_op jit(solution)/shard_map/reduce_scatter | solution.py:319
  1495.5 176.8 %reduce-scatter.11.cloned.1.call-done = f32[48,2560]{1,0:T(8,128)} async-done(((f32[1536,2560]{1,0:T(8,128)}), f32[48,2560]{1,0:T(8,128)}) %reduce-scatter.11.cloned.1.call-update) | async-done | bytes 491536 | tf_op jit(solution)/shard_map/reduce_scatter | solution.py:318
  (448 shorter events, 405.5 us)
Async XLA Ops:
  7.2 81.2 %all-gather.8.cloned.1.call-start = ((), (), s32[]{:S(2)}) async-start(), calls=%async_computation.10 | async-start | bytes 8110080 | tf_op jit(solution)/shard_map/all_gather | solution.py:142
  9.0 114.8 %all-gather.10.cloned.1.call-start = ((), (), s32[]{:S(2)}) async-start(), calls=%async_computation.11 | async-start | bytes 2359296 | tf_op jit(solution)/shard_map/all_gather | solution.py:170
  51.7 42.4 %copy-start.28 = (f32[1536]{0:T(1024)}, f32[1536]{0:T(1024)S(1)}, u32[]{:S(2)}) copy-start(f32[1536]{0:T(1024)S(1)} %convert_element_type.171) | copy-start | bytes 18436
  53.1 41.0 %copy-start.32 = (f32[256]{0:T(256)}, f32[256]{0:T(256)S(1)}, u32[]{:S(2)}) copy-start(f32[256]{0:T(256)S(1)} %add_rsqrt_fusion.1) | copy-start | bytes 3076
  53.1 43.7 %copy-start.27 = (f32[48,1536]{1,0:T(8,128)S(1)}, f32[48,1536]{1,0:T(8,128)}, u32[]{:S(2)}) copy-start(f32[48,1536]{1,0:T(8,128)} %param.23) | copy-start | bytes 884740
  96.1 58.6 %all-gather.12.cloned.1.call-start = ((), (), s32[]{:S(2)}) async-start(), calls=%async_computation.12 | async-start | bytes 2359296 | tf_op jit(solution)/shard_map/all_gather | solution.py:171
  96.8 203.4 %all-gather.14.cloned.1.call-start = ((), (), s32[]{:S(2)}) async-start(), calls=%async_computation.13 | async-start | bytes 4866048 | tf_op jit(solution)/shard_map/all_gather | solution.py:143
  97.6 355.4 %all-gather.16.cloned.1.call-start = ((), (), s32[]{:S(2)}) async-start(), calls=%async_computation.14 | async-start | bytes 28311552 | tf_op jit(solution)/shard_map/all_gather | solution.py:148
  102.6 453.3 %all-gather.18.cloned.1.call-start = ((), (), s32[]{:S(2)}) async-start(), calls=%async_computation.15 | async-start | bytes 14155776 | tf_op jit(solution)/shard_map/all_gather | solution.py:149
  305.6 105.7 %copy-start.19 = (bf16[256,1536]{1,0:T(8,128)(2,1)}, bf16[256,1536]{1,0:T(8,128)(2,1)S(1)}, u32[]{:S(2)}) copy-start(bf16[256,1536]{1,0:T(8,128)(2,1)S(1)} %multiply_convert_fusion.5) | copy-start | bytes 2359300
  313.9 104.2 %all-to-all-start = ((bf16[4,4,48,1536]{3,2,1,0:T(8,128)(2,1)}), bf16[4,4,48,1536]{3,2,1,0:T(8,128)(2,1)}, u32[]{:S(2)}, u32[]{:S(2)}) async-start(bf16[4,4,48,1536]{3,2,1,0:T(8,128)(2,1)} %bitcast.259), calls=%async_computation | async-start | bytes 4718592 | tf_op jit(solution)/shard_map/all_to_all | solution.py:199
  322.7 5.2 copy-start.36
  411.7 6.4 copy-start.34
  418.1 31.3 %all-to-all-start.2 = ((bf16[4,4,48,1536]{3,2,1,0:T(8,128)(2,1)}), bf16[4,4,48,1536]{3,2,1,0:T(8,128)(2,1)}, u32[]{:S(2)}, u32[]{:S(2)}) async-start(bf16[4,4,48,1536]{3,2,1,0:T(8,128)(2,1)} %bitcast.26), calls=%async_computation.2 | async-start | bytes 4718592 | tf_op jit(solution)/shard_map/all_to_all | solution.py:235
  424.7 28.3 %copy-start.5 = (bf16[1,4,4,48,1536]{4,3,2,1,0:T(8,128)(2,1)}, bf16[1,4,4,48,1536]{4,3,2,1,0:T(8,128)(2,1)S(1)}, u32[]{:S(2)}) copy-start(bf16[1,4,4,48,1536]{4,3,2,1,0:T(8,128)(2,1)S(1)} %copy.134) | copy-start | bytes 7077892
  569.2 24.6 %copy-start.21 = (bf16[4,192,1024]{2,1,0:T(8,128)(2,1)}, bf16[4,192,1024]{2,1,0:T(8,128)(2,1)S(1)}, u32[]{:S(2)}) copy-start(bf16[4,192,1024]{2,1,0:T(8,128)(2,1)S(1)} %get-tuple-element.420) | copy-start | bytes 4718596
  589.3 32.9 %all-to-all-start.3 = ((bf16[1,4,192,1536]{3,1,0,2:T(4,128)(2,1)}), bf16[1,4,192,1536]{3,1,0,2:T(4,128)(2,1)}, u32[]{:S(2)}, u32[]{:S(2)}) async-start(bf16[1,4,192,1536]{3,1,0,2:T(4,128)(2,1)} %copy.139), calls=%async_computation.3 | async-start | bytes 4718592 | tf_op jit(solution)/shard_map/all_to_all | solution.py:255
  622.3 32.1 %all-to-all-start.1 = ((bf16[1,4,192,1536]{3,1,0,2:T(4,128)(2,1)}), bf16[1,4,192,1536]{3,1,0,2:T(4,128)(2,1)}, u32[]{:S(2)}, u32[]{:S(2)}) async-start(bf16[1,4,192,1536]{3,1,0,2:T(4,128)(2,1)} %copy.135), calls=%async_computation.1 | async-start | bytes 4718592 | tf_op jit(solution)/shard_map/all_to_all | solution.py:215
  626.8 245.9 %reduce-scatter.9.cloned.1.call-start = ((), (), s32[]{:S(2)}) async-start(), calls=%async_computation.16 | async-start | bytes 4718592 | tf_op jit(solution)/shard_map/reduce_scatter | solution.py:299
  664.3 9.7 copy-start.35
  664.3 9.7 copy-start.9
  674.0 6.2 slice-start
  826.1 149.7 %reduce-scatter.19.cloned.1.call-start = ((), (), s32[]{:S(2)}) async-start(), calls=%async_computation.21 | async-start | bytes 811008
  828.6 276.2 %reduce-scatter.17.cloned.1.call-start = ((), (), s32[]{:S(2)}) async-start(), calls=%async_computation.20 | async-start | bytes 14155776 | tf_op jit(solution)/shard_map/reduce_scatter | solution.py:327
  836.6 516.0 %reduce-scatter.15.cloned.1.call-start = ((), (), s32[]{:S(2)}) async-start(), calls=%async_computation.19 | async-start | bytes 28311552 | tf_op jit(solution)/shard_map/reduce_scatter | solution.py:324
  852.3 643.2 %reduce-scatter.13.cloned.1.call-start = ((), (), s32[]{:S(2)}) async-start(), calls=%async_computation.18 | async-start | bytes 9732096 | tf_op jit(solution)/shard_map/reduce_scatter | solution.py:319
  858.9 15.1 copy-start.12
  858.9 15.1 copy-start.29
  858.9 15.1 copy-start.33
  858.9 813.5 %reduce-scatter.11.cloned.1.call-start = ((), (), s32[]{:S(2)}) async-start(), calls=%async_computation.17 | async-start | bytes 16220160 | tf_op jit(solution)/shard_map/reduce_scatter | solution.py:318
  873.9 7.9 copy-start.26
  977.2 49.2 %copy-start.15 = (f32[256,1536]{1,0:T(8,128)S(1)}, f32[256,1536]{1,0:T(8,128)}, u32[]{:S(2)}) copy-start(f32[256,1536]{1,0:T(8,128)} %copy-done.13) | copy-start | bytes 4718596
  (61 other events, 163.1 us)
Sparse Core Ops, SparseCore 0:
  11.5 76.8 all-gather.7
  96.2 27.6 all-gather.9
  126.0 28.5 all-gather.11
  158.0 63.4 all-gather.13
  223.5 215.8 all-gather.15
  440.9 115.0 all-gather.17
  826.2 46.4 reduce-scatter.8
  878.4 97.4 reduce-scatter.18
  978.1 126.5 reduce-scatter.16
  1107.0 245.5 reduce-scatter.14
  1359.0 136.4 reduce-scatter.12
  1503.0 169.3 reduce-scatter.10
where the time goes:
time: 1690 us; the launch traced here: 1680 us
  waiting for transfers between devices  951 us (56%)
  matrix products  289 us (17%)
  blocking collectives  165 us (10%)
  local copies, waits for them, and re-layouts  129 us (8%)
  other arithmetic  94.4 us (6%)
  starting transfers between devices  19 us (1%)
    reduce_scatter x1, waiting for transfers between devices, on_device(): lax.psum_scatter(grad_in.astype(jnp.bfloat16), 'ctx', scatter_dimension=1...  244 us
    reduce_scatter x1, waiting for transfers between devices, on_device(): lax.psum_scatter(grad_qkv, ('ctx', 'exp'), scatter_dimension=0, tiled=True)  177 us
    reduce_scatter x1, waiting for transfers between devices, on_device(): lax.psum_scatter(grad_attn_out, ('ctx', 'exp'), scatter_dimension=0, tile...  138 us
    unnamed x13, waiting for transfers between devices  94.8 us
    all_gather x1, waiting for transfers between devices, on_device(): lax.all_gather(expert_out.astype(jnp.bfloat16), 'ctx', axis=1, tiled=True)  88.6 us
    all_gather x1, blocking collectives, on_device(): lax.all_gather(router_weight.astype(jnp.bfloat16), ('ctx', 'exp'), axis=0...  83.1 us
    unnamed x2, blocking collectives  81.9 us
    reduce_scatter x1, waiting for transfers between devices, on_device(): lax.psum_scatter(grad_down.astype(jnp.bfloat16), 'ctx', scatter_dimension...  75.6 us
  transfers between devices with their start and end apart: 16, of which 13 were waited for; matrix products, arithmetic and copies ran while one was open for 17% of the time, Pallas kernels for 0%

commit v1 on v0

v1 whole, which is shorter than its diff:
```python
import functools

import jax
import jax.numpy as jnp
from jax import lax
from jax.experimental import pallas as pl
from jax.experimental.pallas import tpu as pltpu
from jax.sharding import Mesh
from jax.sharding import PartitionSpec as P

D = 1536
HEADS = 24
KV_HEADS = 8
HEAD = 64
GROUP = HEADS // KV_HEADS
FF = 1024
EXPERTS = 16
BLK = 128
CAP = 48
AUX = 128

epsilon = 1e-05
far_negative = -1e30
start_max = -1e29
F32 = jnp.float32
BF16 = jnp.bfloat16


def norm_scale(values):
    return lax.rsqrt(jnp.mean(values * values, axis=-1, keepdims=True) + epsilon)


def dot(a, b, dims=((1,), (0,))):
    return lax.dot_general(a, b, (dims, ((), ())), preferred_element_type=F32)


def lane_half(shape, half):
    lane = lax.broadcasted_iota(jnp.int32, shape, 1)
    return (lane >= HEAD) if half else (lane < HEAD)


def head_tiles(ref, rows, group, scale):
    tiles = []
    for i in range(GROUP):
        head = group * GROUP + i
        tile = ref[rows, (head // 2) * 128 : (head // 2 + 1) * 128].astype(F32)
        if head % 2 != group % 2:
            tile = pltpu.roll(tile, HEAD, 1)
        tile = jnp.where(lane_half(tile.shape, group % 2), tile * scale, 0.0)
        tiles.append(tile.astype(BF16))
    return jnp.concatenate(tiles, axis=0)


def block_visibility(lengths_ref, query_block, key_block, parts):
    lanes = lax.broadcasted_iota(jnp.int32, (1, BLK), 1)
    query_pos = query_block * BLK + lanes
    start = jnp.zeros((1, BLK), jnp.int32)
    bound = jnp.int32(0)
    for s in range(parts - 1):
        bound = bound + lengths_ref[0, s]
        start = jnp.where(query_pos >= bound, bound, start)
    key_pos = key_block * BLK + lax.broadcasted_iota(jnp.int32, (BLK, BLK), 0)
    one = ((key_pos >= start) & (key_pos <= query_pos)).astype(jnp.int32)
    return jnp.concatenate([one] * GROUP, axis=1) > 0


def first_row_start(lengths_ref, query_block, parts):
    start = jnp.int32(0)
    bound = jnp.int32(0)
    for s in range(parts - 1):
        bound = bound + lengths_ref[0, s]
        start = jnp.where(query_block * BLK >= bound, bound, start)
    return start


def attend_kernel(
    parts, lengths_ref, order_ref, mine_ref, q_ref, kv_ref, exact_ref, out_ref, lse_ref, q_s, m_s, acc_s
):
    width = KV_HEADS * HEAD
    for qb in range(q_ref.shape[0] // BLK):
        rows = pl.ds(qb * BLK, BLK)
        for g in range(KV_HEADS):
            q_s[g] = head_tiles(q_ref, rows, g, HEAD**-0.5)
            m_s[g] = jnp.full((8, GROUP * BLK), start_max, F32)
            acc_s[g] = jnp.zeros((BLK, GROUP * BLK), F32)
        query_block = order_ref[0, mine_ref[0] + qb]
        first = first_row_start(lengths_ref, query_block, parts)

        @pl.loop(0, order_ref.shape[1])
        def _(kb):
            key_block = order_ref[0, kb]

            @pl.when((key_block <= query_block) & (key_block * BLK + BLK > first))
            def _():
                seen = block_visibility(lengths_ref, query_block, key_block, parts)
                key_rows = pl.ds(kb * BLK, BLK)
                for g in range(KV_HEADS):
                    lanes = pl.ds((g // 2) * 128, 128)
                    keys = kv_ref[key_rows, lanes]
                    values = kv_ref[key_rows, pl.ds(width + (g // 2) * 128, 128)]
                    values = jnp.where(lane_half(values.shape, g % 2), values, jnp.ones_like(values))
                    scores = dot(keys, q_s[g], ((1,), (1,)))
                    scores = jnp.where(seen, scores, far_negative)
                    old = m_s[g, 0:1, :]
                    new = jnp.maximum(old, jnp.max(scores, axis=0, keepdims=True))
                    weights = jnp.exp(scores - new)
                    acc_s[g] = acc_s[g] * jnp.exp(old - new) + dot(
                        values, weights.astype(BF16), ((0,), (0,))
                    )
                    m_s[g, 0:1, :] = new

        tiles = []
        for g in range(KV_HEADS):
            acc = acc_s[g]
            at = (1 - g % 2) * HEAD
            total = acc[at : at + 1, :]
            lse_ref[qb, g : g + 1, :] = m_s[g, 0:1, :] + jnp.log(total)
            acc = acc / total
            for i in range(GROUP):
                head = g * GROUP + i
                tile = jnp.transpose(acc[:, i * BLK : (i + 1) * BLK])
                if head % 2 != g % 2:
                    tile = pltpu.roll(tile, HEAD, 1)
                tiles.append(tile)
                if head % 2 == 1:
                    both = jnp.where(lane_half(tile.shape, 0), tiles[head - 1], tile)
                    lanes = pl.ds((head // 2) * 128, 128)
                    exact_ref[rows, lanes] = both
                    out_ref[rows, lanes] = both.astype(BF16)


def attend(lengths, order, mine, projected, kv):
    rows = projected.shape[0]
    smem = pl.BlockSpec(memory_space=pltpu.SMEM)
    vmem = pl.BlockSpec(memory_space=pltpu.VMEM)
    wide = GROUP * BLK
    return pl.pallas_call(
        functools.partial(attend_kernel, lengths.shape[1]),
        out_shape=(
            jax.ShapeDtypeStruct((rows, HEADS * HEAD), F32),
            jax.ShapeDtypeStruct((rows, HEADS * HEAD), BF16),
            jax.ShapeDtypeStruct((rows // BLK, KV_HEADS, wide), F32),
        ),
        in_specs=[smem, smem, smem, vmem, vmem],
        out_specs=(vmem, vmem, vmem),
        scratch_shapes=[
            pltpu.VMEM((KV_HEADS, wide, 128), BF16),
            pltpu.VMEM((KV_HEADS, 8, wide), F32),
            pltpu.VMEM((KV_HEADS, BLK, wide), F32),
        ],
        compiler_params=pltpu.CompilerParams(vmem_limit_bytes=48 * 2**20),
        cost_estimate=pl.CostEstimate(flops=10**10, bytes_accessed=10**7, transcendentals=10**7),
        name="attend",
    )(lengths, order, mine, projected, kv)


def attend_back_kernel(
    parts,
    lengths_ref,
    order_ref,
    mine_ref,
    q_ref,
    kv_ref,
    grad_ref,
    lse_ref,
    delta_ref,
    dq_ref,
    dkv_ref,
    q_s,
    g_s,
    dq_s,
    dkv_s,
):
    width = KV_HEADS * HEAD

    @pl.loop(0, order_ref.shape[1])
    def _(kb):
        dkv_s[pl.ds(kb * BLK, BLK), :] = jnp.zeros((BLK, 2 * width), F32)

    for qb in range(q_ref.shape[0] // BLK):
        rows = pl.ds(qb * BLK, BLK)
        for g in range(KV_HEADS):
            q_s[g] = head_tiles(q_ref, rows, g, HEAD**-0.5)
            g_s[g] = head_tiles(grad_ref, rows, g, 1.0)
            dq_s[g] = jnp.zeros((GROUP * BLK, 128), F32)
        query_block = order_ref[0, mine_ref[0] + qb]
        first = first_row_start(lengths_ref, query_block, parts)

        @pl.loop(0, order_ref.shape[1])
        def _(kb):
            key_block = order_ref[0, kb]

            @pl.when((key_block <= query_block) & (key_block * BLK + BLK > first))
            def _():
                seen = block_visibility(lengths_ref, query_block, key_block, parts)
                key_rows = pl.ds(kb * BLK, BLK)
                for pair in range(KV_HEADS // 2):
                    key_lanes = pl.ds(pair * 128, 128)
                    value_lanes = pl.ds(width + pair * 128, 128)
                    keys = kv_ref[key_rows, key_lanes]
                    values = kv_ref[key_rows, value_lanes]
                    grad_keys = dkv_s[key_rows, key_lanes]
                    grad_values = dkv_s[key_rows, value_lanes]
                    for g in (2 * pair, 2 * pair + 1):
                        scores = dot(keys, q_s[g], ((1,), (1,)))
                        scores = jnp.where(seen, scores, far_negative)
                        probs = jnp.exp(scores - lse_ref[qb, g : g + 1, :])
                        grad_probs = dot(values, g_s[g], ((1,), (1,)))
                        grad_scores = (probs * (grad_probs - delta_ref[qb, g : g + 1, :])).astype(BF16)
                        grad_values = grad_values + dot(probs.astype(BF16), g_s[g])
                        grad_keys = grad_keys + dot(grad_scores, q_s[g])
                        dq_s[g] += dot(grad_scores, keys, ((0,), (0,)))
                    dkv_s[key_rows, key_lanes] = grad_keys
                    dkv_s[key_rows, value_lanes] = grad_values

        tiles = []
        for g in range(KV_HEADS):
            for i in range(GROUP):
                head = g * GROUP + i
                tile = dq_s[g, i * BLK : (i + 1) * BLK, :] * HEAD**-0.5
                if head % 2 != g % 2:
                    tile = pltpu.roll(tile, HEAD, 1)
                tiles.append(tile)
                if head % 2 == 1:
                    both = jnp.where(lane_half(tile.shape, 0), tiles[head - 1], tile)
                    dq_ref[rows, (head // 2) * 128 : (head // 2 + 1) * 128] = both.astype(BF16)

    @pl.loop(0, order_ref.shape[1])
    def _(kb):
        key_rows = pl.ds(kb * BLK, BLK)
        dkv_ref[key_rows, :] = dkv_s[key_rows, :].astype(BF16)


def attend_back(lengths, order, mine, projected, kv, grad_attended, lse, delta):
    rows = projected.shape[0]
    smem = pl.BlockSpec(memory_space=pltpu.SMEM)
    vmem = pl.BlockSpec(memory_space=pltpu.VMEM)
    wide = GROUP * BLK
    return pl.pallas_call(
        functools.partial(attend_back_kernel, lengths.shape[1]),
        out_shape=(
            jax.ShapeDtypeStruct((rows, HEADS * HEAD), BF16),
            jax.ShapeDtypeStruct(kv.shape, BF16),
        ),
        in_specs=[smem, smem, smem, vmem, vmem, vmem, vmem, vmem],
        out_specs=(vmem, vmem),
        scratch_shapes=[
            pltpu.VMEM((KV_HEADS, wide, 128), BF16),
            pltpu.VMEM((KV_HEADS, wide, 128), BF16),
            pltpu.VMEM((KV_HEADS, wide, 128), F32),
            pltpu.VMEM(kv.shape, F32),
        ],
        compiler_params=pltpu.CompilerParams(vmem_limit_bytes=56 * 2**20),
        cost_estimate=pl.CostEstimate(flops=3 * 10**10, bytes_accessed=10**7, transcendentals=10**7),
        name="attend_back",
    )(lengths, order, mine, projected, kv, grad_attended, lse, delta)


CTX = ("le", "rep", "core")
ALL = ("le", "rep", "core", "exp")
OWNERS = ("exp", "le")


def on_device(
    tokens,
    cotangent,
    routes,
    lengths,
    block_order,
    gain_attn,
    qkv_weight,
    out_weight,
    gain_moe,
    router_weight,
    expert_in,
    expert_out,
):
    tok_rows = tokens.shape[1]
    head_width = HEADS * HEAD
    exp_local = expert_in.shape[0]
    n_ctx = D // expert_in.shape[1]
    copies = n_ctx // exp_local
    in_rows, out_rows = expert_in.shape[1], expert_out.shape[1]

    aux = jnp.concatenate([gain_attn[:, None], gain_moe[:, None], router_weight], axis=1)
    aux = jnp.pad(aux, ((0, 0), (0, AUX - aux.shape[1]))).astype(BF16)
    w_first = lax.all_gather(
        jnp.concatenate([qkv_weight.astype(BF16), aux], axis=1), ALL, axis=0, tiled=True
    )
    w_qkv = w_first[:, : qkv_weight.shape[1]]
    aux_all = w_first[:, qkv_weight.shape[1] :]
    gain_first = aux_all[:, 0].astype(F32)
    gain_second = aux_all[:, 1].astype(F32)
    w_router = aux_all[:, 2 : 2 + EXPERTS]
    w_attn_out = lax.all_gather(out_weight.astype(BF16), ALL, axis=0, tiled=True)

    def to_owner(weight):
        rows, cols = weight.shape[1:]
        halves = weight.astype(BF16).reshape(exp_local, rows, 2, cols // 2).transpose(0, 2, 1, 3)
        halves = jnp.broadcast_to(
            halves[:, None], (exp_local, copies // 2, 2, rows, cols // 2)
        ).reshape(n_ctx, rows, cols // 2)
        mine = lax.all_to_all(halves, CTX, split_axis=0, concat_axis=0, tiled=True)
        return lax.all_gather(mine.reshape(n_ctx * rows, cols // 2), "core", axis=0)

    w_in = to_owner(expert_in)
    w_down = to_owner(expert_out)

    route_hot = (
        routes[0][:, :, None] == jnp.arange(EXPERTS, dtype=jnp.int32)[None, None, :]
    ).astype(F32)
    flat_hot = route_hot.reshape(tok_rows * 2, EXPERTS).astype(BF16)
    order = jnp.arange(tok_rows * 2, dtype=jnp.int32)
    earlier = (order[:, None] > order[None, :]).astype(BF16)
    ranks = dot(earlier, flat_hot)
    slot_index = jnp.sum(ranks * flat_hot.astype(F32), axis=1).astype(jnp.int32)
    target = (routes[0].reshape(tok_rows * 2) * CAP + slot_index).reshape(tok_rows, 2)
    slots = jnp.arange(EXPERTS * CAP, dtype=jnp.int32)
    picks = [(target[:, k : k + 1] == slots[None, :]) for k in range(2)]
    sends = [(target[:, k][None, :] == slots[:, None]) for k in range(2)]
    send_hot = (sends[0] | sends[1]).astype(BF16)

    def to_experts(rows):
        return lax.all_to_all(
            rows.reshape((EXPERTS, CAP) + rows.shape[1:]),
            OWNERS,
            split_axis=0,
            concat_axis=0,
            tiled=True,
        ).reshape(rows.shape)

    grad_y_rows = to_experts(dot(send_hot, cotangent[0]).astype(BF16)).astype(F32)

    inputs = tokens[0].astype(F32)
    scale_first = norm_scale(inputs)
    norm_first = inputs * scale_first
    first = (norm_first * gain_first).astype(BF16)
    projected = dot(first, w_qkv).astype(BF16)
    kv = lax.all_gather(projected[:, head_width:], CTX, axis=0, tiled=True)
    mine = (lax.axis_index(CTX) * (tok_rows // BLK)).astype(jnp.int32).reshape(1)
    exact, attended, lse = attend(lengths, block_order, mine, projected, kv)
    middle = inputs + dot(attended, w_attn_out)
    scale_second = norm_scale(middle)
    norm_second = middle * scale_second
    second = (norm_second * gain_second).astype(BF16)
    logits = dot(second, w_router)
    chosen = jnp.sum(route_hot * logits[:, None, :], axis=-1)
    gates = jax.nn.softmax(chosen, axis=-1)

    gate_rows = jnp.sum(
        jnp.where(sends[0], gates[:, 0][None, :], 0.0) + jnp.where(sends[1], gates[:, 1][None, :], 0.0),
        axis=1,
        keepdims=True,
    )
    high = lax.reduce_precision(gate_rows, 8, 7)
    rest = gate_rows - high
    mid = lax.reduce_precision(rest, 8, 7)
    low = rest - mid
    gate_parts = jnp.pad(
        jnp.concatenate([high, mid, low], axis=1).astype(BF16), ((0, 0), (0, AUX - 3))
    )
    payload = to_experts(
        jnp.concatenate([dot(send_hot, second).astype(BF16), gate_parts], axis=1)
    )
    received = payload[:, :D]
    gate_got = jnp.sum(payload[:, D : D + 3].astype(F32), axis=1, keepdims=True)

    gate_part = dot(received, w_in[0])
    up_part = dot(received, w_in[1])
    sigmoid_gate = jax.nn.sigmoid(gate_part)
    silu_gate = gate_part * sigmoid_gate
    hidden = (silu_gate * up_part).astype(BF16)
    expert_rows = jnp.concatenate([dot(hidden, w_down[0]), dot(hidden, w_down[1])], axis=1)
    returned = to_experts(expert_rows.astype(BF16))

    grad_rows = (gate_got * grad_y_rows).astype(BF16)
    half_d = D // 2
    grad_hidden = dot(grad_rows[:, :half_d], w_down[0], ((1,), (1,))) + dot(
        grad_rows[:, half_d:], w_down[1], ((1,), (1,))
    )
    grad_gate = (
        grad_hidden * up_part * sigmoid_gate * (1.0 + gate_part * (1.0 - sigmoid_gate))
    ).astype(BF16)
    grad_up = (grad_hidden * silu_gate).astype(BF16)
    grad_back = dot(grad_gate, w_in[0], ((1,), (1,))) + dot(grad_up, w_in[1], ((1,), (1,)))
    grad_returned = to_experts(grad_back.astype(BF16))

    grad_in = jnp.stack(
        [dot(received, grad_gate, ((0,), (0,))), dot(received, grad_up, ((0,), (0,)))]
    ).astype(BF16)
    grad_down = jnp.stack(
        [
            dot(hidden, grad_rows[:, :half_d], ((0,), (0,))),
            dot(hidden, grad_rows[:, half_d:], ((0,), (0,))),
        ]
    ).astype(BF16)

    def to_rows(grad, rows):
        cols = grad.shape[2]
        half = lax.psum_scatter(grad, "core", scatter_dimension=0, tiled=True)
        got = lax.all_to_all(
            half.reshape(n_ctx, rows, cols), CTX, split_axis=0, concat_axis=0, tiled=True
        ).astype(F32)
        got = got.reshape(exp_local, copies // 2, 2, rows, cols).sum(axis=1)
        return got.transpose(0, 2, 1, 3).reshape(exp_local, rows, 2 * cols)

    sum_in = to_rows(grad_in, in_rows)
    sum_down = to_rows(grad_down, out_rows)

    grad_y = cotangent[0].astype(F32)
    pick_hot = [p.astype(BF16) for p in picks]
    picked = [dot(p, returned) for p in pick_hot]
    block_out = (middle + gates[:, 0:1] * picked[0] + gates[:, 1:2] * picked[1]).astype(BF16)
    grad_gates = jnp.stack([jnp.sum(grad_y * p, axis=-1) for p in picked], axis=1)
    grad_chosen = gates * (grad_gates - jnp.sum(gates * grad_gates, axis=-1, keepdims=True))
    grad_logits = jnp.sum(grad_chosen[:, :, None] * route_hot, axis=1).astype(BF16)
    grad_router = dot(second, grad_logits, ((0,), (0,)))
    grad_second = dot(pick_hot[0] + pick_hot[1], grad_returned) + dot(
        grad_logits, w_router, ((1,), (1,))
    )
    grad_gain_second = jnp.sum(grad_second * norm_second, axis=0)
    grad_norm_second = grad_second * gain_second
    grad_middle = grad_y + scale_second * (
        grad_norm_second
        - norm_second * jnp.mean(grad_norm_second * norm_second, axis=-1, keepdims=True)
    )
    grad_branch = grad_middle.astype(BF16)
    grad_attn_out = dot(attended, grad_branch, ((0,), (0,)))
    late = jnp.concatenate([grad_gain_second[:, None], grad_router], axis=1)
    late = jnp.pad(late, ((0, 0), (0, AUX - late.shape[1])))
    sum_second = lax.psum_scatter(
        jnp.concatenate([grad_attn_out, late], axis=1).astype(BF16),
        ALL,
        scatter_dimension=0,
        tiled=True,
    ).astype(F32)

    grad_attended = dot(grad_branch, w_attn_out, ((1,), (1,))).astype(BF16)
    delta = jnp.sum(
        (grad_attended.astype(F32) * exact).reshape(tok_rows, HEADS, HEAD), axis=-1
    )
    delta = (
        delta.reshape(tok_rows // BLK, BLK, KV_HEADS, GROUP)
        .transpose(0, 2, 3, 1)
        .reshape(lse.shape)
    )
    grad_queries, grad_kv = attend_back(
        lengths, block_order, mine, projected, kv, grad_attended, lse, delta
    )
    grad_kv = lax.psum_scatter(grad_kv, CTX, scatter_dimension=0, tiled=True)
    grad_projected = jnp.concatenate([grad_queries, grad_kv], axis=1)
    grad_qkv = dot(first, grad_projected, ((0,), (0,)))
    grad_first = dot(grad_projected, w_qkv, ((1,), (1,)))
    grad_gain_first = jnp.sum(grad_first * norm_first, axis=0)
    grad_norm_first = grad_first * gain_first
    grad_inputs = grad_middle + scale_first * (
        grad_norm_first
        - norm_first * jnp.mean(grad_norm_first * norm_first, axis=-1, keepdims=True)
    )
    last = jnp.pad(grad_gain_first[:, None], ((0, 0), (0, AUX - 1)))
    sum_first = lax.psum_scatter(
        jnp.concatenate([grad_qkv, last], axis=1).astype(BF16),
        ALL,
        scatter_dimension=0,
        tiled=True,
    ).astype(F32)
    cols = qkv_weight.shape[1]
    return (
        block_out[None],
        grad_inputs.astype(BF16)[None],
        sum_first[:, cols],
        sum_first[:, :cols],
        sum_second[:, :D],
        sum_second[:, D],
        sum_second[:, D + 1 : D + 1 + EXPERTS],
        sum_in,
        sum_down,
    )


def solution(mesh):
    n_ctx, n_exp = mesh.shape["ctx"], mesh.shape["exp"]
    exp_local = EXPERTS // n_exp
    copies = n_ctx // exp_local
    inner = Mesh(mesh.devices.reshape(exp_local, copies // 2, 2, n_exp), ALL)
    by_token = P("exp", CTX, None)
    by_row = P(ALL, None)
    by_expert = P("exp", CTX, None)
    return jax.shard_map(
        on_device,
        mesh=inner,
        in_specs=(
            by_token,
            by_token,
            by_token,
            P("exp", None),
            P("exp", None),
            P(ALL),
            by_row,
            by_row,
            P(ALL),
            by_row,
            by_expert,
            by_expert,
        ),
        out_specs=(
            by_token,
            by_token,
            P(ALL),
            by_row,
            by_row,
            P(ALL),
            by_row,
            by_expert,
            by_expert,
        ),
        check_vma=False,
    )
```

time: 1690 us -> 983 us (0.58)
  waiting for transfers between devices: 951 us -> 644 us
  matrix products: 289 us -> 91.4 us
  blocking collectives: 165 us -> 43.7 us
  local copies, waits for them, and re-layouts: 129 us -> 60.5 us
  other arithmetic: 94.4 us -> 40.7 us
  starting transfers between devices: 19 us -> 54.5 us
  Pallas kernels: 0 us -> 24.9 us
    reduce_scatter x5 -> x4, waiting for transfers between devices: 647 us -> 147 us  [the longest x1 109 us: on_device(): lax.psum_scatter(jnp.concatenate([grad_qkv, last], axis=1).astype(BF16),...]
    all_to_all x4 -> x7, waiting for transfers between devices: 51.1 us -> 249 us  [the longest x4 188 us: to_experts(): lax.all_to_all(rows.reshape((EXPERTS, CAP) + rows.shape[1:]), OWNERS, spl...]
    dot_general x70 -> x27, matrix products: 288 us -> 91.4 us  [dot(): return lax.dot_general(a, b, (dims, ((), ())), preferred_element_type=F32)]
    all_gather x1 -> x0, blocking collectives: 83.1 us -> none  [on_device(): lax.all_gather(router_weight.astype(jnp.bfloat16), ('ctx', 'exp'), axis=0...]
    unnamed x2 -> x0, blocking collectives: 81.9 us -> none
    reduce_sum x13 -> x4, other arithmetic: 52.4 us -> 1.45 us  [the longest x1 1.07 us: on_device(): gate_got = jnp.sum(payload[:, D:D + 3].astype(F32), axis=1, keepdims=True)]
    all_to_all x0 -> x1, blocking collectives: none -> 43.7 us  [to_rows(): lax.all_to_all(half.reshape(n_ctx, rows, cols), CTX, split_axis=0, concat...]
    all_to_all x4 -> x7, starting transfers between devices: 18.3 us -> 53.3 us  [the longest x4 34 us: to_experts(): lax.all_to_all(rows.reshape((EXPERTS, CAP) + rows.shape[1:]), OWNERS, spl...]
  transfers between devices with their start and end apart: 16 -> 17, of which waited for: 13 -> 11; matrix products, arithmetic and copies ran while one was open for 17% -> 15% of each run, Pallas kernels for 0% -> 1%
where the time goes in v1:
time: 983 us; the launch traced here: 976 us
  waiting for transfers between devices  644 us (66%)
  matrix products  91.4 us (9%)
  local copies, waits for them, and re-layouts  60.5 us (6%)
  starting transfers between devices  54.5 us (6%)
  blocking collectives  43.7 us (4%)
  other arithmetic  40.7 us (4%)
  Pallas kernels  24.9 us (3%)
  between operations  16.7 us (2%)
    all_to_all x4, waiting for transfers between devices, to_experts(): lax.all_to_all(rows.reshape((EXPERTS, CAP) + rows.shape[1:]), OWNERS, spl...  188 us
    reduce_scatter x1, waiting for transfers between devices, on_device(): lax.psum_scatter(jnp.concatenate([grad_qkv, last], axis=1).astype(BF16),...  109 us
    unnamed x11, waiting for transfers between devices  100 us
    dot_general x27, matrix products, dot(): return lax.dot_general(a, b, (dims, ((), ())), preferred_element_type=F32)  91.4 us
    all_gather x1, waiting for transfers between devices, on_device(): lax.all_gather(jnp.concatenate([qkv_weight.astype(BF16), aux], axis=1), A...  77.7 us
    all_gather x1, waiting for transfers between devices, on_device(): lax.all_gather(out_weight.astype(BF16), ALL, axis=0, tiled=True)  70.2 us
    all_to_all x2, waiting for transfers between devices, to_owner(): mine = lax.all_to_all(halves, CTX, split_axis=0, concat_axis=0, tiled=True)  60.6 us
    all_to_all x1, blocking collectives, to_rows(): lax.all_to_all(half.reshape(n_ctx, rows, cols), CTX, split_axis=0, concat...  43.7 us
  transfers between devices with their start and end apart: 17, of which 11 were waited for; matrix products, arithmetic and copies ran while one was open for 15% of the time, Pallas kernels for 1%

profile of v1, /device:TPU:8, one launch (start us, length us, event | category | flops | bytes accessed | tf_op | source)
XLA Modules:
  0.0 976.4 jit_solution(9464775653949261257)
XLA Ops:
  12.9 77.7 %all-gather.6.cloned.1.call-done = bf16[1536,2688]{1,0:T(8,128)(2,1)} async-done(((bf16[48,2688]{1,0:T(8,128)(2,1)}), bf16[1536,2688]{1,0:T(8,128)(2,1)}) %all-gather.6.cloned.1.call-update) | async-done | bytes 8257552 | tf_op jit(solution)/shard_map/all_gather | solution.py:287
  92.3 5.6 fusion.8.q_ref
  113.6 60.6 %all-to-all-done.2 = bf16[8,128,768]{2,1,0:T(8,128)(2,1)S(1)} async-done(((bf16[8,128,768]{2,1,0:T(8,128)(2,1)}), bf16[8,128,768]{2,1,0:T(8,128)(2,1)S(1)}, u32[]{:S(2)}, u32[]{:S(2)}) %all-to-all-start.2) | async-done | bytes 1572896 | tf_op jit(solution)/shard_map/all_to_all | solution.py:303
  175.3 8.5 all-to-all-start.1
  186.2 10.7 %attend.1 = (f32[256,1536]{1,0:T(8,128)S(1)}, bf16[256,1536]{1,0:T(8,128)(2,1)S(1)}, f32[2,8,384]{2,1,0:T(8,128)S(1)}) custom-call(s32[1,3]{1,0:T(1,128)S(1)} %copy-done.2, s32[1,16]{1,0:T(1,128)S(1)} %copy-done.3, s32[1]{0:T(128)} %bitcast.1.mine_ref, bf16[256,2560]{1,0:T(8,128)(2,1)S(1)} %copy-done.1, bf16[2048,1024]{1,0:T(8,128)(2,1)} %all-gather.8.cloned.1.call-done.kv_ref), custom_call_target="tpu_custom_call" | custom-call | flops 10000000000 | bytes 10000000 | tf_op jit(solution)/shard_map/attend/pallas_call | solution.py:137
  197.5 70.2 %all-gather.10.cloned.1.call-done = bf16[1536,1536]{1,0:T(8,128)(2,1)} async-done(((bf16[48,1536]{1,0:T(8,128)(2,1)}), bf16[1536,1536]{1,0:T(8,128)(2,1)}) %all-gather.10.cloned.1.call-update) | async-done | bytes 4718608 | tf_op jit(solution)/shard_map/all_gather | solution.py:295
  277.4 6.3 all-to-all-start
  287.6 54.1 %all-to-all-done = bf16[16,48,1664]{2,1,0:T(8,128)(2,1)} async-done(((bf16[16,48,1664]{2,1,0:T(8,128)(2,1)}), bf16[16,48,1664]{2,1,0:T(8,128)(2,1)}, u32[]{:S(2)}, u32[]{:S(2)}) %all-to-all-start) | async-done | bytes 2555936 | tf_op jit(solution)/shard_map/all_to_all | solution.py:324
  341.7 10.4 %all-to-all-start.4 = ((bf16[16,48,1536]{2,1,0:T(8,128)(2,1)}), bf16[16,48,1536]{2,1,0:T(8,128)(2,1)}, u32[]{:S(2)}, u32[]{:S(2)}) async-start(bf16[16,48,1536]{2,1,0:T(8,128)(2,1)} %bitcast.127), calls=%async_computation.4 | async-start | bytes 4718592 | tf_op jit(solution)/shard_map/all_to_all | solution.py:324
  353.8 49.7 %all-to-all-done.4 = bf16[16,48,1536]{2,1,0:T(8,128)(2,1)} async-done(((bf16[16,48,1536]{2,1,0:T(8,128)(2,1)}), bf16[16,48,1536]{2,1,0:T(8,128)(2,1)}, u32[]{:S(2)}, u32[]{:S(2)}) %all-to-all-start.4) | async-done | bytes 2359328 | tf_op jit(solution)/shard_map/all_to_all | solution.py:324
  406.9 7.0 fusion.16
  414.0 6.0 fusion.15
  433.8 8.6 all-to-all-start.3
  442.4 5.1 fusion.14
  447.6 5.8 add_convert_fusion
  453.4 39.9 %all-to-all-done.3 = bf16[16,48,1536]{2,1,0:T(8,128)(2,1)} async-done(((bf16[16,48,1536]{2,1,0:T(8,128)(2,1)}), bf16[16,48,1536]{2,1,0:T(8,128)(2,1)}, u32[]{:S(2)}, u32[]{:S(2)}) %all-to-all-start.3) | async-done | bytes 2359328 | tf_op jit(solution)/shard_map/all_to_all | solution.py:324
  493.3 8.8 all-to-all-start.5
  508.5 44.5 %all-to-all-done.5 = bf16[16,48,1536]{2,1,0:T(8,128)(2,1)} async-done(((bf16[16,48,1536]{2,1,0:T(8,128)(2,1)}), bf16[16,48,1536]{2,1,0:T(8,128)(2,1)}, u32[]{:S(2)}, u32[]{:S(2)}) %all-to-all-start.5) | async-done | bytes 2359328 | tf_op jit(solution)/shard_map/all_to_all | solution.py:324
  558.1 5.8 convert_multiply_fusion.5
  566.5 14.3 %attend_back.1 = (bf16[256,1536]{1,0:T(8,128)(2,1)}, bf16[2048,1024]{1,0:T(8,128)(2,1)}) custom-call(s32[1,3]{1,0:T(1,128)} %lengths_ref.3, s32[1,16]{1,0:T(1,128)} %order_ref.3, s32[1]{0:T(128)} %bitcast.1.mine_ref, bf16[256,2560]{1,0:T(8,128)(2,1)} %copy-done, bf16[2048,1024]{1,0:T(8,128)(2,1)} %all-gather.8.cloned.1.call-done.kv_ref, ...), custom_call_target="tpu_custom_call" | custom-call | flops 30000001024 | bytes 10000000 | tf_op jit(solution)/shard_map/attend_back/pallas_call | solution.py:239
  587.9 4.9 fusion.12
  606.0 7.7 copy.76
  615.8 37.2 %reduce-scatter.8.cloned.1.call-done = bf16[256,1024]{1,0:T(8,128)(2,1)} async-done(((bf16[2048,1024]{1,0:T(8,128)(2,1)}), bf16[256,1024]{1,0:T(8,128)(2,1)}) %reduce-scatter.8.cloned.1.call-update) | async-done | bytes 524304 | tf_op jit(solution)/shard_map/reduce_scatter | solution.py:450
  654.9 7.2 fusion.30
  668.8 43.7 %all_to_all.40 = bf16[8,128,768]{2,1,0:T(8,128)(2,1)} all-to-all(bf16[8,128,768]{2,1,0:T(8,128)(2,1)} %bitcast.135), channel_id=1, replica_groups=mesh['le'=4,'rep'=1,'core'=2,'exp'=4] {'le','rep','core'}, dimensions={0} | all-to-all | bytes 3145728 | tf_op jit(solution)/shard_map/all_to_all | solution.py:401
  712.5 6.8 all-to-all-start.6
  719.3 4.7 copy.83
  724.0 5.5 reshape.255
  729.5 99.3 %reduce-scatter.16.cloned.1.call-done = bf16[48,1664]{1,0:T(8,128)(2,1)} async-done(((bf16[1536,1664]{1,0:T(8,128)(2,1)}), bf16[48,1664]{1,0:T(8,128)(2,1)}) %reduce-scatter.16.cloned.1.call-update) | async-done | bytes 159760
  838.5 7.8 copy.82
  846.3 9.3 reshape.253
  855.7 109.4 %reduce-scatter.10.cloned.1.call-done = bf16[48,2688]{1,0:T(8,128)(2,1)} async-done(((bf16[1536,2688]{1,0:T(8,128)(2,1)}), bf16[48,2688]{1,0:T(8,128)(2,1)}) %reduce-scatter.10.cloned.1.call-update) | async-done | bytes 258064 | tf_op jit(solution)/shard_map/reduce_scatter | solution.py:461
  (181 shorter events, 116.8 us)
Async XLA Ops:
  8.0 84.2 %copy-start.10 = (bf16[1,256,1536]{2,1,0:T(8,128)(2,1)S(1)}, bf16[1,256,1536]{2,1,0:T(8,128)(2,1)}, u32[]{:S(2)}) copy-start(bf16[1,256,1536]{2,1,0:T(8,128)(2,1)} %param.12) | copy-start | bytes 2359300
  8.0 82.6 %all-gather.6.cloned.1.call-start = ((), (), s32[]{:S(2)}) async-start(), calls=%async_computation.13 | async-start | bytes 8515584 | tf_op jit(solution)/shard_map/all_gather | solution.py:287
  11.4 173.5 %all-gather.8.cloned.1.call-start = ((), (), s32[]{:S(2)}) async-start(), calls=%async_computation.14 | async-start | bytes 4718592 | tf_op jit(solution)/shard_map/all_gather | solution.py:339
  12.9 85.0 %copy-start.22 = (f32[256]{0:T(256)}, f32[256]{0:T(256)S(1)}, u32[]{:S(2)}) copy-start(f32[256]{0:T(256)S(1)} %add_rsqrt_fusion.1) | copy-start | bytes 3076
  92.2 5.6 copy-start.20
  92.3 7.6 copy-start.19
  99.8 167.9 %all-gather.10.cloned.1.call-start = ((), (), s32[]{:S(2)}) async-start(), calls=%async_computation.15 | async-start | bytes 4866048 | tf_op jit(solution)/shard_map/all_gather | solution.py:295
  104.0 70.2 %all-to-all-start.2 = ((bf16[8,128,768]{2,1,0:T(8,128)(2,1)}), bf16[8,128,768]{2,1,0:T(8,128)(2,1)S(1)}, u32[]{:S(2)}, u32[]{:S(2)}) async-start(bf16[8,128,768]{2,1,0:T(8,128)(2,1)} %bitcast.129), calls=%async_computation.2 | async-start | bytes 3145728 | tf_op jit(solution)/shard_map/all_to_all | solution.py:303
  174.2 9.6 copy-start.24
  174.2 10.7 %copy-start.2 = (s32[1,3]{1,0:T(1,128)S(1)}, s32[1,3]{1,0:T(1,128)}, u32[]{:S(2)}) copy-start(s32[1,3]{1,0:T(1,128)} %lengths_ref.3) | copy-start | bytes 40
  174.2 10.7 %copy-start.3 = (s32[1,16]{1,0:T(1,128)S(1)}, s32[1,16]{1,0:T(1,128)}, u32[]{:S(2)}) copy-start(s32[1,16]{1,0:T(1,128)} %order_ref.3) | copy-start | bytes 196
  175.3 102.1 %all-to-all-start.1 = ((bf16[8,192,1024]{2,1,0:T(8,128)(2,1)}), bf16[8,192,1024]{2,1,0:T(8,128)(2,1)}, u32[]{:S(2)}, u32[]{:S(2)}) async-start(bf16[8,192,1024]{2,1,0:T(8,128)(2,1)} %bitcast.124), calls=%async_computation.1 | async-start | bytes 6291456 | tf_op jit(solution)/shard_map/all_to_all | solution.py:303
  277.4 64.3 %all-to-all-start = ((bf16[16,48,1664]{2,1,0:T(8,128)(2,1)}), bf16[16,48,1664]{2,1,0:T(8,128)(2,1)}, u32[]{:S(2)}, u32[]{:S(2)}) async-start(bf16[16,48,1664]{2,1,0:T(8,128)(2,1)} %bitcast.126), calls=%async_computation | async-start | bytes 5111808 | tf_op jit(solution)/shard_map/all_to_all | solution.py:324
  283.7 123.3 %all-gather.12.cloned.1.call-start = ((), (), s32[]{:S(2)}) async-start(), calls=%async_computation.16 | async-start | bytes 9437184 | tf_op jit(solution)/shard_map/all_gather | solution.py:304
  341.7 61.7 %all-to-all-start.4 = ((bf16[16,48,1536]{2,1,0:T(8,128)(2,1)}), bf16[16,48,1536]{2,1,0:T(8,128)(2,1)}, u32[]{:S(2)}, u32[]{:S(2)}) async-start(bf16[16,48,1536]{2,1,0:T(8,128)(2,1)} %bitcast.127), calls=%async_computation.4 | async-start | bytes 4718592 | tf_op jit(solution)/shard_map/all_to_all | solution.py:324
  352.1 67.8 %all-gather.14.cloned.1.call-start = ((), (), s32[]{:S(2)}) async-start(), calls=%async_computation.17 | async-start | bytes 4718592 | tf_op jit(solution)/shard_map/all_gather | solution.py:304
  406.9 7.0 copy-start.25
  419.9 5.3 copy-start.30
  433.8 59.5 %all-to-all-start.3 = ((bf16[16,48,1536]{2,1,0:T(8,128)(2,1)}), bf16[16,48,1536]{2,1,0:T(8,128)(2,1)}, u32[]{:S(2)}, u32[]{:S(2)}) async-start(bf16[16,48,1536]{2,1,0:T(8,128)(2,1)} %pad_maximum_fusion.4), calls=%async_computation.3 | async-start | bytes 4718592 | tf_op jit(solution)/shard_map/all_to_all | solution.py:324
  442.4 5.1 copy-start.32
  493.3 59.7 %all-to-all-start.5 = ((bf16[16,48,1536]{2,1,0:T(8,128)(2,1)}), bf16[16,48,1536]{2,1,0:T(8,128)(2,1)}, u32[]{:S(2)}, u32[]{:S(2)}) async-start(bf16[16,48,1536]{2,1,0:T(8,128)(2,1)} %bitcast.133), calls=%async_computation.5 | async-start | bytes 4718592 | tf_op jit(solution)/shard_map/all_to_all | solution.py:324
  502.1 150.9 %reduce-scatter.8.cloned.1.call-start = ((), (), s32[]{:S(2)}) async-start(), calls=%async_computation.18 | async-start | bytes 4718592 | tf_op jit(solution)/shard_map/reduce_scatter | solution.py:450
  558.1 5.8 copy-start.5
  580.8 88.0 %reduce-scatter.14.cloned.1.call-start = ((), (), s32[]{:S(2)}) async-start(), calls=%async_computation.21 | async-start | bytes 4718592 | tf_op jit(solution)/shard_map/reduce_scatter | solution.py:400
  587.9 124.7 %reduce-scatter.12.cloned.1.call-start = ((), (), s32[]{:S(2)}) async-start(), calls=%async_computation.20 | async-start | bytes 9437184 | tf_op jit(solution)/shard_map/reduce_scatter | solution.py:400
  600.6 228.2 %reduce-scatter.16.cloned.1.call-start = ((), (), s32[]{:S(2)}) async-start(), calls=%async_computation.22 | async-start | bytes 5271552
  613.7 41.2 %copy-start.11 = (bf16[1,256,1536]{2,1,0:T(8,128)(2,1)S(1)}, bf16[1,256,1536]{2,1,0:T(8,128)(2,1)}, u32[]{:S(2)}) copy-start(bf16[1,256,1536]{2,1,0:T(8,128)(2,1)} %param.12) | copy-start | bytes 2359300
  613.7 41.2 %copy-start.21 = (f32[1536]{0:T(1024)S(1)}, f32[1536]{0:T(1024)}, u32[]{:S(2)}) copy-start(f32[1536]{0:T(1024)} %copy-done.20) | copy-start | bytes 18436
  613.7 41.1 %copy-start.23 = (f32[256]{0:T(256)S(1)}, f32[256]{0:T(256)}, u32[]{:S(2)}) copy-start(f32[256]{0:T(256)} %copy-done.22) | copy-start | bytes 3076
  613.7 351.4 %reduce-scatter.10.cloned.1.call-start = ((), (), s32[]{:S(2)}) async-start(), calls=%async_computation.19 | async-start | bytes 8515584 | tf_op jit(solution)/shard_map/reduce_scatter | solution.py:461
  654.9 7.4 copy-start.15
  712.5 126.0 %all-to-all-start.6 = ((bf16[8,192,1024]{2,1,0:T(8,128)(2,1)}), bf16[8,192,1024]{2,1,0:T(8,128)(2,1)}, u32[]{:S(2)}, u32[]{:S(2)}) async-start(bf16[8,192,1024]{2,1,0:T(8,128)(2,1)} %bitcast.132), calls=%async_computation.9 | async-start | bytes 6291456 | tf_op jit(solution)/shard_map/all_to_all | solution.py:401
  (18 other events, 42.0 us)
Sparse Core Ops, SparseCore 0:
  12.3 78.2 all-gather.5
  99.9 73.7 all-gather.7
  177.2 90.5 all-gather.9
  580.9 71.9 reduce-scatter.7
  655.6 13.1 reduce-scatter.13
  671.6 15.6 reduce-scatter.11
  692.9 135.8 reduce-scatter.15
  835.7 129.3 reduce-scatter.9
Sparse Core Ops, SparseCore 1:
  285.7 17.8 all-gather.11
  354.1 13.2 all-gather.13

commit v2 on v1

--- a/solution.py
+++ b/solution.py
@@ -256,6 +256,460 @@
     )(lengths, order, mine, projected, kv, grad_attended, lse, delta)
 
 
+MESH = pl.DeviceIdType.MESH
+
+
+def place(z, core, exp):
+    return {"le": z, "rep": 0, "core": core, "exp": exp}
+
+
+def x_of(exp):
+    return (exp // 2) * 2 + 1 - exp % 2
+
+
+def y_of(exp):
+    return (1 - exp // 2) * 2 + exp % 2
+
+
+def remote(src, dst, send_sem, recv_sem, device):
+    return pltpu.make_async_remote_copy(
+        src_ref=src,
+        dst_ref=dst,
+        send_sem=send_sem,
+        recv_sem=recv_sem,
+        device_id=device,
+        device_id_type=MESH,
+    )
+
+
+def meet(devices):
+    barrier = pltpu.get_barrier_semaphore()
+    for device in devices:
+        pl.semaphore_signal(barrier, inc=1, device_id=device, device_id_type=MESH)
+    pl.semaphore_wait(barrier, len(devices))
+
+
+def spread_kernel(
+    layers,
+    shard_ref,
+    in_ref,
+    down_ref,
+    all_ref,
+    w_in_ref,
+    w_down_ref,
+    unit_sem,
+    line_sem,
+    x_sem,
+    y_sem,
+    far_sem,
+    core_sem,
+    half_sem,
+    half_send,
+    over_sem,
+    over_send,
+    own_sem,
+):
+    z, core, exp = lax.axis_index("le"), lax.axis_index("core"), lax.axis_index("exp")
+    other = 1 - core
+    column = [((z + s) % layers, p) for s in range(layers) for p in range(2)]
+    x, y = x_of(exp), y_of(exp)
+    meet(
+        [place(zz, (core + p) % 2, exp) for zz, p in column if not (zz is column[0][0] and p == 0)]
+        + [place(z, core, x), place(z, core, y)]
+    )
+    rows = shard_ref.shape[0]
+
+    def number(zz, cc, ee):
+        return (zz * 2 + cc) * 4 + ee
+
+    def unit(zz, cc, ee):
+        return all_ref.at[pl.ds(number(zz, cc, ee) * rows, rows), :]
+
+    def send(src, who, sem, device):
+        return remote(src, unit(*who), sem, unit_sem.at[number(*who)], device)
+
+    def arrive(who):
+        send(unit(*who), who, line_sem.at[0], place(z, other, exp)).wait_recv()
+
+    started = []
+
+    def go(copy, condition=None):
+        if condition is None:
+            copy.start()
+        else:
+            pl.when(condition)(copy.start)
+        started.append((copy, condition))
+
+    me = (z, core, exp)
+    keep = pltpu.make_async_copy(shard_ref, unit(*me), own_sem.at[0])
+    keep.start()
+    go(send(shard_ref, me, line_sem.at[layers], place(z + 1, core, exp)), z < layers - 1)
+    go(send(shard_ref, me, line_sem.at[layers + 1], place(z - 1, core, exp)), z > 0)
+
+    ctx = z * 2 + core
+    arrays = ((in_ref, w_in_ref), (down_ref, w_down_ref))
+
+    def half(a, source, p):
+        src, dst = arrays[a]
+        n, cols = src.shape[1], src.shape[2] // 2
+        return dst.at[pl.ds(source * n, n), pl.ds(pl.multiple_of(p * cols, 128), cols)]
+
+    def mine(a, zz, p):
+        src = arrays[a][0]
+        cols = src.shape[2] // 2
+        return src.at[zz, :, pl.ds(pl.multiple_of(p * cols, 128), cols)]
+
+    for a in range(2):
+        pltpu.make_async_copy(mine(a, z, core), half(a, ctx, core), own_sem.at[1 + a]).start()
+
+    def own_sends(k, src):
+        go(send(src, me, x_sem.at[k], place(z, core, x)))
+        go(send(src, me, y_sem.at[k], place(z, core, y)))
+        go(send(src, me, core_sem.at[k], place(z, other, exp)))
+
+    own_sends(layers, shard_ref)
+    def layer(k):
+        return jnp.where(z < layers // 2, k, layers - 1 - k)
+
+    for k in range(layers):
+        zz = layer(k)
+        who = (zz, core, exp)
+
+        @pl.when(zz != z)
+        def _(zz=zz, who=who, k=k):
+            arrive(who)
+
+        go(send(unit(*who), who, line_sem.at[k], place(z + 1, core, exp)), (zz < z) & (z < layers - 1))
+        go(send(unit(*who), who, line_sem.at[k], place(z - 1, core, exp)), (zz > z) & (z > 0))
+        go(send(unit(*who), who, x_sem.at[k], place(z, core, x)), zz != z)
+        go(send(unit(*who), who, y_sem.at[k], place(z, core, y)), zz != z)
+        go(send(unit(*who), who, core_sem.at[k], place(z, other, exp)), zz != z)
+
+    for s in range(layers):
+        zz = (z + s) % layers
+        for p in range(2):
+            if s == 0 and p == 0:
+                continue
+            pp = (core + p) % 2
+            for a in range(2):
+                go(
+                    remote(
+                        mine(a, zz, pp),
+                        half(a, ctx, pp),
+                        half_send.at[a, s * 2 + p],
+                        half_sem.at[a, ctx],
+                        place(zz, pp, exp),
+                    )
+                )
+    for a in range(2):
+        go(
+            remote(
+                mine(a, z, core),
+                half(a, ctx, core),
+                over_send.at[a, 2 * layers],
+                over_sem.at[a, ctx],
+                place(z, other, exp),
+            )
+        )
+
+    for k in range(layers):
+        zz = layer(k)
+        from_x, from_y = (zz, core, x), (zz, core, y)
+        arrive(from_x)
+        go(send(unit(*from_x), from_x, core_sem.at[layers + 1 + k], place(z, other, exp)))
+        if k % 2 == 0:
+            go(send(unit(*from_x), from_x, far_sem.at[k], place(z, core, y)))
+        arrive(from_y)
+        go(send(unit(*from_y), from_y, core_sem.at[2 * layers + 1 + k], place(z, other, exp)))
+        if k % 2 == 1:
+            go(send(unit(*from_y), from_y, far_sem.at[k], place(z, core, x)))
+    for k in range(layers):
+        far = (layer(k), core, y_of(x))
+        arrive(far)
+        go(send(unit(*far), far, core_sem.at[3 * layers + 1 + k], place(z, other, exp)))
+
+    for s in range(layers):
+        for p in range(2):
+            if s == 0 and p == 0:
+                continue
+            source = ((z + s) % layers) * 2 + (core + p) % 2
+            for a in range(2):
+                copy = remote(
+                    half(a, source, core),
+                    half(a, source, core),
+                    over_send.at[a, s * 2 + p],
+                    over_sem.at[a, source],
+                    place(z, other, exp),
+                )
+                remote(
+                    half(a, source, core),
+                    half(a, source, core),
+                    half_send.at[a, 0],
+                    half_sem.at[a, source],
+                    place(z, other, exp),
+                ).wait_recv()
+                go(copy)
+
+    for ee in range(4):
+        for zz in range(layers):
+            arrive((zz, other, ee))
+    for source in range(2 * layers):
+        for a in range(2):
+            remote(
+                half(a, source, other),
+                half(a, source, other),
+                half_send.at[a, 0],
+                over_sem.at[a, source],
+                place(z, other, exp),
+            ).wait_recv()
+    keep.wait()
+    for a in range(2):
+        pltpu.make_async_copy(mine(a, z, core), half(a, ctx, core), own_sem.at[1 + a]).wait()
+    for copy, condition in started:
+        if condition is None:
+            copy.wait_send()
+        else:
+            pl.when(condition)(copy.wait_send)
+
+
+def spread(shard, expert_in, expert_out):
+    layers = expert_in.shape[0]
+    rows_in, rows_out = expert_in.shape[1], expert_out.shape[1]
+    any_space = pl.BlockSpec(memory_space=pl.ANY)
+    dma = pltpu.SemaphoreType.DMA
+    return pl.pallas_call(
+        functools.partial(spread_kernel, layers),
+        out_shape=(
+            jax.ShapeDtypeStruct((shard.shape[0] * 8 * layers, shard.shape[1]), BF16),
+            jax.ShapeDtypeStruct((rows_in * 2 * layers, expert_in.shape[2]), BF16),
+            jax.ShapeDtypeStruct((rows_out * 2 * layers, expert_out.shape[2]), BF16),
+        ),
+        in_specs=[any_space] * 3,
+        out_specs=(any_space,) * 3,
+        scratch_shapes=[
+            dma((8 * layers,)),
+            dma((layers + 2,)),
+            dma((layers + 1,)),
+            dma((layers + 1,)),
+            dma((layers,)),
+            dma((4 * layers + 1,)),
+            dma((2, 2 * layers)),
+            dma((2, 2 * layers)),
+            dma((2, 2 * layers)),
+            dma((2, 2 * layers + 1)),
+            dma((3,)),
+        ],
+        compiler_params=pltpu.CompilerParams(collective_id=0, has_side_effects=True),
+        name="spread",
+    )(shard, expert_in, expert_out)
+
+
+def collect_kernel(
+    layers,
+    part_ref,
+    in_ref,
+    down_ref,
+    out_ref,
+    got_in_ref,
+    got_down_ref,
+    own,
+    pair,
+    near,
+    line,
+    half_sem,
+    half_send,
+    load_sem,
+    pair_sem,
+    pair_send,
+    near_sem,
+    near_send,
+    line_sem,
+    line_send,
+):
+    z, core, exp = lax.axis_index("le"), lax.axis_index("core"), lax.axis_index("exp")
+    other = 1 - core
+    x, y = x_of(exp), y_of(exp)
+    layer_mates = (x, y, y_of(x))
+    meet(
+        [
+            place((z + s) % layers, (core + p) % 2, exp)
+            for s in range(layers)
+            for p in range(2)
+            if s + p > 0
+        ]
+        + [place(z, core, mate) for mate in layer_mates]
+    )
+    rows = out_ref.shape[0]
+    ctx = z * 2 + core
+    started = []
+
+    def go(copy):
+        copy.start()
+        started.append(copy)
+
+    order = [(z + s) % layers for s in (2, 1, 3, 0)] if layers == 4 else [(z + s) % layers for s in range(layers)]
+    loads = []
+    for k, zz in enumerate(order):
+        go(
+            remote(
+                part_ref.at[pl.ds((zz * 2 + other) * 4 * rows, 4 * rows), :],
+                pair.at[zz],
+                pair_send.at[k],
+                pair_sem.at[zz],
+                place(z, other, exp),
+            )
+        )
+        load = pltpu.make_async_copy(
+            part_ref.at[pl.ds((zz * 2 + core) * 4 * rows, 4 * rows), :], own.at[zz], load_sem.at[k]
+        )
+        load.start()
+        loads.append(load)
+
+    arrays = ((in_ref, got_in_ref), (down_ref, got_down_ref))
+
+    def mine(a, owner):
+        n = arrays[a][1].shape[1]
+        return arrays[a][0].at[pl.ds(owner * n, n), :]
+
+    def half(a, expert, p):
+        cols = arrays[a][0].shape[1]
+        return arrays[a][1].at[expert, :, pl.ds(pl.multiple_of(p * cols, 128), cols)]
+
+    keeps = []
+    for a in range(2):
+        keep = pltpu.make_async_copy(mine(a, ctx), half(a, z, core), load_sem.at[layers + a])
+        keep.start()
+        keeps.append(keep)
+    for s in range(layers):
+        for p in range(2):
+            if s + p == 0:
+                continue
+            zz, pp = (z + s) % layers, (core + p) % 2
+            for a in range(2):
+                go(
+                    remote(
+                        mine(a, zz * 2 + pp),
+                        half(a, z, core),
+                        half_send.at[a, s * 2 + p],
+                        half_sem.at[a, ctx],
+                        place(zz, pp, exp),
+                    )
+                )
+
+    slab = 16
+    for k, zz in enumerate(order):
+        loads[k].wait()
+        remote(pair.at[zz], pair.at[zz], pair_send.at[k], pair_sem.at[zz], place(z, other, exp)).wait_recv()
+
+        @pl.loop(0, 4 * rows // slab)
+        def _(i, zz=zz):
+            at = pl.ds(pl.multiple_of(i * slab, slab), slab)
+            own[zz, at, :] = (own[zz, at, :].astype(F32) + pair[zz, at, :].astype(F32)).astype(BF16)
+
+        for m, mate in enumerate(layer_mates):
+            go(
+                remote(
+                    own.at[zz, pl.ds(pl.multiple_of(mate * rows, slab), rows), :],
+                    near.at[m, zz],
+                    near_send.at[m, k],
+                    near_sem.at[m, zz],
+                    place(z, core, mate),
+                )
+            )
+
+    for k, zz in enumerate(order):
+        for m, mate in enumerate(layer_mates):
+            remote(
+                near.at[m, zz], near.at[m, zz], near_send.at[m, k], near_sem.at[m, zz], place(z, core, mate)
+            ).wait_recv()
+
+        @pl.loop(0, rows // slab)
+        def _(i, zz=zz):
+            at = pl.ds(pl.multiple_of(exp * rows + i * slab, slab), slab)
+            here = pl.ds(pl.multiple_of(i * slab, slab), slab)
+            total = own[zz, at, :].astype(F32)
+            for m in range(3):
+                total = total + near[m, zz, here, :].astype(F32)
+            own[zz, at, :] = total.astype(BF16)
+
+        if k < layers - 1:
+            go(
+                remote(
+                    own.at[zz, pl.ds(pl.multiple_of(exp * rows, slab), rows), :],
+                    line.at[z],
+                    line_send.at[k],
+                    line_sem.at[z],
+                    place(zz, core, exp),
+                )
+            )
+
+    for zz in order[:-1]:
+        remote(line.at[zz], line.at[zz], line_send.at[0], line_sem.at[zz], place(zz, core, exp)).wait_recv()
+
+    @pl.loop(0, rows // slab)
+    def _(i):
+        at = pl.ds(pl.multiple_of(exp * rows + i * slab, slab), slab)
+        here = pl.ds(pl.multiple_of(i * slab, slab), slab)
+        total = own[z, at, :].astype(F32)
+        for zz in order[:-1]:
+            total = total + line[zz, here, :].astype(F32)
+        out_ref[here, :] = total
+
+    for source in range(2 * layers):
+        for a in range(2):
+
+            @pl.when(source != ctx)
+            def _(source=source, a=a):
+                remote(
+                    half(a, source // 2, source % 2),
+                    half(a, source // 2, source % 2),
+                    half_send.at[a, 0],
+                    half_sem.at[a, source],
+                    place(z, other, exp),
+                ).wait_recv()
+
+    for keep in keeps:
+        keep.wait()
+    for copy in started:
+        copy.wait_send()
+
+
+def collect(part, grad_in, grad_down, layers):
+    rows, cols = part.shape[0] // (8 * layers), part.shape[1]
+    n_in, n_down = grad_in.shape[0] // (2 * layers), grad_down.shape[0] // (2 * layers)
+    any_space = pl.BlockSpec(memory_space=pl.ANY)
+    dma = pltpu.SemaphoreType.DMA
+    return pl.pallas_call(
+        functools.partial(collect_kernel, layers),
+        out_shape=(
+            jax.ShapeDtypeStruct((rows, cols), F32),
+            jax.ShapeDtypeStruct((layers, n_in, 2 * grad_in.shape[1]), BF16),
+            jax.ShapeDtypeStruct((layers, n_down, 2 * grad_down.shape[1]), BF16),
+        ),
+        in_specs=[any_space] * 3,
+        out_specs=(pl.BlockSpec(memory_space=pltpu.VMEM), any_space, any_space),
+        scratch_shapes=[
+            pltpu.VMEM((layers, 4 * rows, cols), BF16),
+            pltpu.VMEM((layers, 4 * rows, cols), BF16),
+            pltpu.VMEM((3, layers, rows, cols), BF16),
+            pltpu.VMEM((layers, rows, cols), BF16),
+            dma((2, 2 * layers)),
+            dma((2, 2 * layers)),
+            dma((layers + 2,)),
+            dma((layers,)),
+            dma((layers,)),
+            dma((3, layers)),
+            dma((3, layers)),
+            dma((layers,)),
+            dma((layers,)),
+        ],
+        compiler_params=pltpu.CompilerParams(
+            collective_id=1, has_side_effects=True, vmem_limit_bytes=40 * 2**20
+        ),
+        name="collect",
+    )(part, grad_in, grad_down)
+
+
 CTX = ("le", "rep", "core")
 ALL = ("le", "rep", "core", "exp")
 OWNERS = ("exp", "le")
@@ -280,31 +734,35 @@
     exp_local = expert_in.shape[0]
     n_ctx = D // expert_in.shape[1]
     copies = n_ctx // exp_local
+    n_exp = EXPERTS // exp_local
     in_rows, out_rows = expert_in.shape[1], expert_out.shape[1]
 
+    cols = qkv_weight.shape[1]
     aux = jnp.concatenate([gain_attn[:, None], gain_moe[:, None], router_weight], axis=1)
-    aux = jnp.pad(aux, ((0, 0), (0, AUX - aux.shape[1]))).astype(BF16)
-    w_first = lax.all_gather(
-        jnp.concatenate([qkv_weight.astype(BF16), aux], axis=1), ALL, axis=0, tiled=True
-    )
-    w_qkv = w_first[:, : qkv_weight.shape[1]]
-    aux_all = w_first[:, qkv_weight.shape[1] :]
+    aux = jnp.pad(aux, ((0, 0), (0, AUX - aux.shape[1])))
+    shard = jnp.concatenate([qkv_weight, aux, out_weight], axis=1).astype(BF16)
+    if (copies, exp_local, n_exp) == (2, 4, 4):
+        w_all, w_in, w_down = spread(shard, expert_in.astype(BF16), expert_out.astype(BF16))
+    else:
+        w_all = lax.all_gather(shard, ALL, axis=0, tiled=True)
+
+        def to_owner(weight):
+            rows, width = weight.shape[1:]
+            halves = weight.astype(BF16).reshape(exp_local, rows, 2, width // 2).transpose(0, 2, 1, 3)
+            halves = jnp.broadcast_to(
+                halves[:, None], (exp_local, copies // 2, 2, rows, width // 2)
+            ).reshape(n_ctx, rows, width // 2)
+            mine = lax.all_to_all(halves, CTX, split_axis=0, concat_axis=0, tiled=True)
+            return lax.all_gather(mine.reshape(n_ctx * rows, width // 2), "core", axis=1, tiled=True)
+
+        w_in = to_owner(expert_in)
+        w_down = to_owner(expert_out)
+    w_qkv = w_all[:, :cols]
+    aux_all = w_all[:, cols : cols + AUX]
+    w_attn_out = w_all[:, cols + AUX :]
     gain_first = aux_all[:, 0].astype(F32)
     gain_second = aux_all[:, 1].astype(F32)
     w_router = aux_all[:, 2 : 2 + EXPERTS]
-    w_attn_out = lax.all_gather(out_weight.astype(BF16), ALL, axis=0, tiled=True)
-
-    def to_owner(weight):
-        rows, cols = weight.shape[1:]
-        halves = weight.astype(BF16).reshape(exp_local, rows, 2, cols // 2).transpose(0, 2, 1, 3)
-        halves = jnp.broadcast_to(
-            halves[:, None], (exp_local, copies // 2, 2, rows, cols // 2)
-        ).reshape(n_ctx, rows, cols // 2)
-        mine = lax.all_to_all(halves, CTX, split_axis=0, concat_axis=0, tiled=True)
-        return lax.all_gather(mine.reshape(n_ctx * rows, cols // 2), "core", axis=0)
-
-    w_in = to_owner(expert_in)
-    w_down = to_owner(expert_out)
 
     route_hot = (
         routes[0][:, :, None] == jnp.arange(EXPERTS, dtype=jnp.int32)[None, None, :]
@@ -329,16 +787,17 @@
             tiled=True,
         ).reshape(rows.shape)
 
-    grad_y_rows = to_experts(dot(send_hot, cotangent[0]).astype(BF16)).astype(F32)
-
     inputs = tokens[0].astype(F32)
     scale_first = norm_scale(inputs)
     norm_first = inputs * scale_first
     first = (norm_first * gain_first).astype(BF16)
     projected = dot(first, w_qkv).astype(BF16)
     kv = lax.all_gather(projected[:, head_width:], CTX, axis=0, tiled=True)
+    kv, grad_y_send = lax.optimization_barrier((kv, dot(send_hot, cotangent[0]).astype(BF16)))
+    grad_y_rows = to_experts(grad_y_send)
     mine = (lax.axis_index(CTX) * (tok_rows // BLK)).astype(jnp.int32).reshape(1)
     exact, attended, lse = attend(lengths, block_order, mine, projected, kv)
+    attended, grad_y_rows = lax.optimization_barrier((attended, grad_y_rows))
     middle = inputs + dot(attended, w_attn_out)
     scale_second = norm_scale(middle)
     norm_second = middle * scale_second
@@ -352,38 +811,45 @@
         axis=1,
         keepdims=True,
     )
-    high = lax.reduce_precision(gate_rows, 8, 7)
-    rest = gate_rows - high
-    mid = lax.reduce_precision(rest, 8, 7)
-    low = rest - mid
-    gate_parts = jnp.pad(
-        jnp.concatenate([high, mid, low], axis=1).astype(BF16), ((0, 0), (0, AUX - 3))
-    )
+
+    def in_parts(column):
+        high = lax.reduce_precision(column, 8, 7)
+        rest = column - high
+        mid = lax.reduce_precision(rest, 8, 7)
+        parts = jnp.concatenate([high, mid, rest - mid], axis=1).astype(BF16)
+        return jnp.pad(parts, ((0, 0), (0, AUX - 3)))
+
+    gate_parts = in_parts(gate_rows)
     payload = to_experts(
         jnp.concatenate([dot(send_hot, second).astype(BF16), gate_parts], axis=1)
     )
     received = payload[:, :D]
     gate_got = jnp.sum(payload[:, D : D + 3].astype(F32), axis=1, keepdims=True)
 
-    gate_part = dot(received, w_in[0])
-    up_part = dot(received, w_in[1])
+    gate_up = dot(received, w_in)
+    gate_part = gate_up[:, :FF]
+    up_part = gate_up[:, FF:]
     sigmoid_gate = jax.nn.sigmoid(gate_part)
     silu_gate = gate_part * sigmoid_gate
     hidden = (silu_gate * up_part).astype(BF16)
-    expert_rows = jnp.concatenate([dot(hidden, w_down[0]), dot(hidden, w_down[1])], axis=1)
-    returned = to_experts(expert_rows.astype(BF16))
+    expert_rows = dot(hidden, w_down)
+    expert_rows = expert_rows.astype(BF16)
+    grad_y_rows = grad_y_rows.astype(F32)
+    returned = to_experts(expert_rows)
 
     grad_rows = (gate_got * grad_y_rows).astype(BF16)
+    gate_grad_parts = in_parts(
+        jnp.sum(grad_y_rows * expert_rows.astype(F32), axis=1, keepdims=True)
+    )
     half_d = D // 2
-    grad_hidden = dot(grad_rows[:, :half_d], w_down[0], ((1,), (1,))) + dot(
-        grad_rows[:, half_d:], w_down[1], ((1,), (1,))
-    )
+    grad_hidden = dot(grad_rows, w_down, ((1,), (1,)))
     grad_gate = (
         grad_hidden * up_part * sigmoid_gate * (1.0 + gate_part * (1.0 - sigmoid_gate))
     ).astype(BF16)
     grad_up = (grad_hidden * silu_gate).astype(BF16)
-    grad_back = dot(grad_gate, w_in[0], ((1,), (1,))) + dot(grad_up, w_in[1], ((1,), (1,)))
-    grad_returned = to_experts(grad_back.astype(BF16))
+    grad_gate_up = jnp.concatenate([grad_gate, grad_up], axis=1)
+    grad_back = dot(grad_gate_up, w_in, ((1,), (1,)))
+    grad_returned = to_experts(jnp.concatenate([grad_back.astype(BF16), gate_grad_parts], axis=1))
 
     grad_in = jnp.stack(
         [dot(received, grad_gate, ((0,), (0,))), dot(received, grad_up, ((0,), (0,)))]
@@ -395,27 +861,19 @@
         ]
     ).astype(BF16)
 
-    def to_rows(grad, rows):
-        cols = grad.shape[2]
-        half = lax.psum_scatter(grad, "core", scatter_dimension=0, tiled=True)
-        got = lax.all_to_all(
-            half.reshape(n_ctx, rows, cols), CTX, split_axis=0, concat_axis=0, tiled=True
-        ).astype(F32)
-        got = got.reshape(exp_local, copies // 2, 2, rows, cols).sum(axis=1)
-        return got.transpose(0, 2, 1, 3).reshape(exp_local, rows, 2 * cols)
-
-    sum_in = to_rows(grad_in, in_rows)
-    sum_down = to_rows(grad_down, out_rows)
+    grad_in = lax.psum_scatter(grad_in, "core", scatter_dimension=0, tiled=True)[0]
+    grad_down = lax.psum_scatter(grad_down, "core", scatter_dimension=0, tiled=True)[0]
+    grad_returned, grad_in, grad_down = lax.optimization_barrier((grad_returned, grad_in, grad_down))
 
     grad_y = cotangent[0].astype(F32)
     pick_hot = [p.astype(BF16) for p in picks]
-    picked = [dot(p, returned) for p in pick_hot]
-    block_out = (middle + gates[:, 0:1] * picked[0] + gates[:, 1:2] * picked[1]).astype(BF16)
-    grad_gates = jnp.stack([jnp.sum(grad_y * p, axis=-1) for p in picked], axis=1)
+    grad_gates = jnp.concatenate(
+        [jnp.sum(dot(p, grad_returned[:, D:]), axis=1, keepdims=True) for p in pick_hot], axis=1
+    )
     grad_chosen = gates * (grad_gates - jnp.sum(gates * grad_gates, axis=-1, keepdims=True))
     grad_logits = jnp.sum(grad_chosen[:, :, None] * route_hot, axis=1).astype(BF16)
     grad_router = dot(second, grad_logits, ((0,), (0,)))
-    grad_second = dot(pick_hot[0] + pick_hot[1], grad_returned) + dot(
+    grad_second = dot(pick_hot[0] + pick_hot[1], grad_returned[:, :D]) + dot(
         grad_logits, w_router, ((1,), (1,))
     )
     grad_gain_second = jnp.sum(grad_second * norm_second, axis=0)
@@ -428,13 +886,6 @@
     grad_attn_out = dot(attended, grad_branch, ((0,), (0,)))
     late = jnp.concatenate([grad_gain_second[:, None], grad_router], axis=1)
     late = jnp.pad(late, ((0, 0), (0, AUX - late.shape[1])))
-    sum_second = lax.psum_scatter(
-        jnp.concatenate([grad_attn_out, late], axis=1).astype(BF16),
-        ALL,
-        scatter_dimension=0,
-        tiled=True,
-    ).astype(F32)
-
     grad_attended = dot(grad_branch, w_attn_out, ((1,), (1,))).astype(BF16)
     delta = jnp.sum(
         (grad_attended.astype(F32) * exact).reshape(tok_rows, HEADS, HEAD), axis=-1
@@ -447,6 +898,9 @@
     grad_queries, grad_kv = attend_back(
         lengths, block_order, mine, projected, kv, grad_attended, lse, delta
     )
+    grad_queries, grad_kv, returned = lax.optimization_barrier((grad_queries, grad_kv, returned))
+    picked = [dot(p, returned) for p in pick_hot]
+    block_out = (middle + gates[:, 0:1] * picked[0] + gates[:, 1:2] * picked[1]).astype(BF16)
     grad_kv = lax.psum_scatter(grad_kv, CTX, scatter_dimension=0, tiled=True)
     grad_projected = jnp.concatenate([grad_queries, grad_kv], axis=1)
     grad_qkv = dot(first, grad_projected, ((0,), (0,)))
@@ -458,23 +912,35 @@
         - norm_first * jnp.mean(grad_norm_first * norm_first, axis=-1, keepdims=True)
     )
     last = jnp.pad(grad_gain_first[:, None], ((0, 0), (0, AUX - 1)))
-    sum_first = lax.psum_scatter(
-        jnp.concatenate([grad_qkv, last], axis=1).astype(BF16),
-        ALL,
-        scatter_dimension=0,
-        tiled=True,
-    ).astype(F32)
-    cols = qkv_weight.shape[1]
+    part = jnp.concatenate(
+        [grad_qkv.astype(BF16), last.astype(BF16), grad_attn_out.astype(BF16), late.astype(BF16)], axis=1
+    )
+    if (copies, exp_local, n_exp) == (2, 4, 4):
+        total, sum_in, sum_down = collect(part, grad_in, grad_down, exp_local)
+    else:
+        total = lax.psum_scatter(part, ALL, scatter_dimension=0, tiled=True).astype(F32)
+
+        def to_rows(half, rows):
+            width = half.shape[1]
+            got = lax.all_to_all(
+                half.reshape(n_ctx, rows, width), CTX, split_axis=0, concat_axis=0, tiled=True
+            ).astype(F32)
+            got = got.reshape(exp_local, copies // 2, 2, rows, width).sum(axis=1)
+            return got.transpose(0, 2, 1, 3).reshape(exp_local, rows, 2 * width)
+
+        sum_in = to_rows(grad_in, in_rows)
+        sum_down = to_rows(grad_down, out_rows)
+    sum_second = total[:, cols + AUX :]
     return (
         block_out[None],
         grad_inputs.astype(BF16)[None],
-        sum_first[:, cols],
-        sum_first[:, :cols],
+        total[:, cols],
+        total[:, :cols],
         sum_second[:, :D],
         sum_second[:, D],
         sum_second[:, D + 1 : D + 1 + EXPERTS],
-        sum_in,
-        sum_down,
+        sum_in.astype(F32),
+        sum_down.astype(F32),
     )
 
 

time: 983 us -> 770 us (0.78)
  waiting for transfers between devices: 644 us -> 147 us
  Pallas kernels: 24.9 us -> 316 us
  blocking collectives: 43.7 us -> 129 us
  local copies, waits for them, and re-layouts: 60.5 us -> 17.2 us
  starting transfers between devices: 54.5 us -> 14.5 us
    pallas_call x0 -> x2, Pallas kernels: none -> 278 us  [the longest x1 145 us: collect(): pl.pallas_call(functools.partial(collect_kernel, layers), out_shape=(jax....]
    all_gather x4 -> x0, waiting for transfers between devices: 148 us -> none  [the longest x1 77.7 us: on_device(): lax.all_gather(jnp.concatenate([qkv_weight.astype(BF16), aux], axis=1), A...]
    all_to_all x4 -> x2, waiting for transfers between devices: 188 us -> 45.8 us  [to_experts(): lax.all_to_all(rows.reshape((EXPERTS, CAP) + rows.shape[1:]), OWNERS, spl...]
    reduce_scatter x3 -> x2, waiting for transfers between devices: 110 us -> 0.04 us  [the longest x1 0.02 us: on_device(): lax.psum_scatter(grad_down, 'core', scatter_dimension=0, tiled=True)[0]]
    unnamed x11 -> x4, waiting for transfers between devices: 100 us -> 0.07 us
    all_to_all x1 -> x2, blocking collectives: 43.7 us -> 129 us  [to_experts(): lax.all_to_all(rows.reshape((EXPERTS, CAP) + rows.shape[1:]), OWNERS, spl...]
    all_gather x1, waiting for transfers between devices: 0.02 us -> 61.2 us  [on_device(): kv = lax.all_gather(projected[:, head_width:], CTX, axis=0, tiled=True)]
    all_to_all x3 -> x0, waiting for transfers between devices: 60.6 us -> none  [the longest x2 60.6 us: to_owner(): mine = lax.all_to_all(halves, CTX, split_axis=0, concat_axis=0, tiled=True)]
  transfers between devices with their start and end apart: 17 -> 6, of which waited for: 11 -> 4; matrix products, arithmetic and copies ran while one was open for 15% -> 8% of each run, Pallas kernels for 1% -> 5%
where the time goes in v2:
time: 770 us; the launch traced here: 767 us
  Pallas kernels  316 us (41%)
  waiting for transfers between devices  147 us (19%)
  blocking collectives  129 us (17%)
  matrix products  88 us (11%)
  other arithmetic  39.9 us (5%)
  local copies, waits for them, and re-layouts  17.2 us (2%)
  between operations  14.6 us (2%)
  starting transfers between devices  14.5 us (2%)
    pallas_call x1, Pallas kernels, collect(): pl.pallas_call(functools.partial(collect_kernel, layers), out_shape=(jax....  145 us
    pallas_call x1, Pallas kernels, spread(): pl.pallas_call(functools.partial(spread_kernel, layers), out_shape=(jax.S...  133 us
    all_to_all x2, blocking collectives, to_experts(): lax.all_to_all(rows.reshape((EXPERTS, CAP) + rows.shape[1:]), OWNERS, spl...  129 us
    dot_general x25, matrix products, dot(): return lax.dot_general(a, b, (dims, ((), ())), preferred_element_type=F32)  88 us
    all_gather x1, waiting for transfers between devices, on_device(): kv = lax.all_gather(projected[:, head_width:], CTX, axis=0, tiled=True)  61.2 us
    all_to_all x2, waiting for transfers between devices, to_experts(): lax.all_to_all(rows.reshape((EXPERTS, CAP) + rows.shape[1:]), OWNERS, spl...  45.8 us
    reduce_scatter x1, waiting for transfers between devices, on_device(): grad_kv = lax.psum_scatter(grad_kv, CTX, scatter_dimension=0, tiled=True)  40.3 us
    pallas_call x1, Pallas kernels, attend_back(): pl.pallas_call(functools.partial(attend_back_kernel, lengths.shape[1]), o...  20.8 us
  transfers between devices with their start and end apart: 6, of which 4 were waited for; matrix products, arithmetic and copies ran while one was open for 8% of the time, Pallas kernels for 5%

profile of v2, /device:TPU:8, one launch (start us, length us, event | category | flops | bytes accessed | tf_op | source)
XLA Modules:
  0.0 766.7 jit_solution(11642697573638768679)
XLA Ops:
  13.0 3.2 convert_element_type.151.down_ref
  16.2 4.9 convert_element_type.150.in_ref
  22.0 132.8 %spread.1 = (bf16[1536,4224]{1,0:T(8,128)(2,1)}, bf16[1536,2048]{1,0:T(8,128)(2,1)}, bf16[1024,1536]{1,0:T(8,128)(2,1)}) custom-call(bf16[48,4224]{1,0:T(8,128)(2,1)} %pad_maximum_fusion.2.shard_ref, bf16[4,192,2048]{2,1,0:T(8,128)(2,1)} %convert_element_type.150.in_ref, bf16[4,128,1536]{2,1,0:T(8,128)(2,1)} %convert_element_type.151.down_ref), custom_call_target="tpu_custom_call" | custom-call | tf_op jit(solution)/shard_map/spread/pallas_call | solution.py:480
  156.4 5.5 fusion.18.q_ref
  167.0 61.2 %all-gather.2.cloned.1.call-done.kv_ref = bf16[2048,1024]{1,0:T(8,128)(2,1)} async-done(((bf16[256,1024]{1,0:T(8,128)(2,1)}), bf16[2048,1024]{1,0:T(8,128)(2,1)}) %all-gather.2.cloned.1.call-update) | async-done | bytes 4194320 | tf_op jit(solution)/shard_map/all_gather | solution.py:795
  228.3 6.5 all-to-all-start
  236.4 17.0 %attend.1 = (f32[256,1536]{1,0:T(8,128)S(1)}, bf16[256,1536]{1,0:T(8,128)(2,1)S(1)}, f32[2,8,384]{2,1,0:T(8,128)S(1)}) custom-call(s32[1,3]{1,0:T(1,128)S(1)} %copy-done.6, s32[1,16]{1,0:T(1,128)S(1)} %copy-done.7, s32[1]{0:T(128)} %bitcast.1.mine_ref, bf16[256,2560]{1,0:T(8,128)(2,1)S(1)} %copy-done.5, bf16[2048,1024]{1,0:T(8,128)(2,1)} %all-gather.2.cloned.1.call-done.kv_ref), custom_call_target="tpu_custom_call" | custom-call | flops 10000000000 | bytes 10000000 | tf_op jit(solution)/shard_map/attend/pallas_call | solution.py:137
  254.0 32.7 %all-to-all-done = bf16[16,48,1536]{2,1,0:T(8,128)(2,1)} async-done(((bf16[16,48,1536]{2,1,0:T(8,128)(2,1)}), bf16[16,48,1536]{2,1,0:T(8,128)(2,1)}, u32[]{:S(2)}, u32[]{:S(2)}) %all-to-all-start) | async-done | bytes 2359328 | tf_op jit(solution)/shard_map/all_to_all | solution.py:782
  286.7 3.8 multiply_reduce_fusion.2
  297.2 66.9 %all_to_all.20 = bf16[16,48,1664]{2,1,0:T(8,128)(2,1)S(1)} all-to-all(bf16[16,48,1664]{2,1,0:T(8,128)(2,1)S(1)} %bitcast.79), channel_id=1, replica_groups=mesh['le'=4,'rep'=1,'core'=2,'exp'=4] {'exp','le'}, dimensions={0} | all-to-all | bytes 5111808 | tf_op jit(solution)/shard_map/all_to_all | solution.py:782
  364.2 7.9 %fusion.47 = f32[768,2048]{1,0:T(8,128)S(1)} fusion(bf16[1536,2048]{1,0:T(8,128)(2,1)} %get-tuple-element.37, bf16[768,1664]{1,0:T(8,128)(2,1)S(1)} %bitcast.83), kind=kOutput, calls=%fused_computation.67 | convolution fusion | flops 4831838208 | bytes 14942208 | tf_op jit(solution)/shard_map/dot_general | solution.py:34
  374.7 5.4 multiply_convert_fusion.2
  385.5 4.9 fusion.21
  390.4 2.9 fusion.22
  393.4 3.2 pad_maximum_fusion
  396.6 7.1 fusion.13
  403.9 9.0 %convolution_convert_fusion.5 = bf16[768,1536]{1,0:T(8,128)(2,1)S(1)} fusion(bf16[1536,2048]{1,0:T(8,128)(2,1)} %get-tuple-element.37, bf16[768,1024]{1,0:T(8,128)(2,1)} %get-tuple-element.116, bf16[768,1024]{1,0:T(8,128)(2,1)} %get-tuple-element.115), kind=kOutput, calls=%fused_computation.31 | convolution fusion | flops 4839309312 | bytes 11796480 | tf_op jit(solution)/shard_map/dot_general | solution.py:34
  413.1 62.6 %all_to_all.21 = bf16[16,48,1664]{2,1,0:T(8,128)(2,1)} all-to-all(bf16[16,48,1664]{2,1,0:T(8,128)(2,1)S(1)} %bitcast.80), channel_id=1, replica_groups=mesh['le'=4,'rep'=1,'core'=2,'exp'=4] {'exp','le'}, dimensions={0} | all-to-all | bytes 5111808 | tf_op jit(solution)/shard_map/all_to_all | solution.py:782
  475.7 7.0 all-to-all-start.3
  485.7 2.6 fusion.43
  490.9 5.8 convert_multiply_fusion.4
  499.4 20.8 %attend_back.1 = (bf16[256,1536]{1,0:T(8,128)(2,1)}, bf16[2048,1024]{1,0:T(8,128)(2,1)}) custom-call(s32[1,3]{1,0:T(1,128)} %lengths_ref.3, s32[1,16]{1,0:T(1,128)} %order_ref.3, s32[1]{0:T(128)} %bitcast.1.mine_ref, bf16[256,2560]{1,0:T(8,128)(2,1)} %copy-done.4, bf16[2048,1024]{1,0:T(8,128)(2,1)} %all-gather.2.cloned.1.call-done.kv_ref, ...), custom_call_target="tpu_custom_call" | custom-call | flops 30000001024 | bytes 10000000 | tf_op jit(solution)/shard_map/attend_back/pallas_call | solution.py:239
  520.2 13.1 %all-to-all-done.3 = bf16[16,48,1536]{2,1,0:T(8,128)(2,1)} async-done(((bf16[16,48,1536]{2,1,0:T(8,128)(2,1)}), bf16[16,48,1536]{2,1,0:T(8,128)(2,1)}, u32[]{:S(2)}, u32[]{:S(2)}) %all-to-all-start.3) | async-done | bytes 2359328 | tf_op jit(solution)/shard_map/all_to_all | solution.py:782
  536.0 2.5 fusion.28
  538.5 3.5 fusion.38
  542.0 3.6 convolution_convert_fusion.1
  545.6 40.3 %reduce-scatter.8.cloned.1.call-done = bf16[256,1024]{1,0:T(8,128)(2,1)} async-done(((bf16[2048,1024]{1,0:T(8,128)(2,1)}), bf16[256,1024]{1,0:T(8,128)(2,1)}) %reduce-scatter.8.cloned.1.call-update) | async-done | bytes 524304 | tf_op jit(solution)/shard_map/reduce_scatter | solution.py:904
  587.2 6.8 fusion.55
  594.0 2.3 convolution_convert_fusion
  596.7 6.1 fusion.5.part_ref
  602.7 145.0 %collect.1 = (f32[48,4352]{1,0:T(8,128)S(1)}, bf16[4,192,2048]{2,1,0:T(8,128)(2,1)S(1)}, bf16[4,128,1536]{2,1,0:T(8,128)(2,1)S(1)}) custom-call(bf16[1536,4352]{1,0:T(8,128)(2,1)} %fusion.5.part_ref, bf16[1536,1024]{1,0:T(8,128)(2,1)S(1)} %bitcast.75, bf16[1024,768]{1,0:T(8,128)(2,1)S(1)} %bitcast.76), custom_call_target="tpu_custom_call" | custom-call | tf_op jit(solution)/shard_map/collect/pallas_call | solution.py:682
  751.8 3.5 convert_element_type.186
  (144 shorter events, 51.4 us)
Async XLA Ops:
  7.2 221.1 %all-gather.2.cloned.1.call-start = ((), (), s32[]{:S(2)}) async-start(), calls=%async_computation.7 | async-start | bytes 4718592 | tf_op jit(solution)/shard_map/all_gather | solution.py:795
  22.0 134.4 %copy-start.15 = (bf16[1,256,1536]{2,1,0:T(8,128)(2,1)S(1)}, bf16[1,256,1536]{2,1,0:T(8,128)(2,1)}, u32[]{:S(2)}) copy-start(bf16[1,256,1536]{2,1,0:T(8,128)(2,1)} %param.12) | copy-start | bytes 2359300
  156.4 7.5 copy-start.24
  161.9 2.9 copy-start.19
  228.3 6.8 copy-start.6
  228.3 6.8 copy-start.7
  228.3 58.4 %all-to-all-start = ((bf16[16,48,1536]{2,1,0:T(8,128)(2,1)}), bf16[16,48,1536]{2,1,0:T(8,128)(2,1)}, u32[]{:S(2)}, u32[]{:S(2)}) async-start(bf16[16,48,1536]{2,1,0:T(8,128)(2,1)} %bitcast.7), calls=%async_computation | async-start | bytes 4718592 | tf_op jit(solution)/shard_map/all_to_all | solution.py:782
  234.7 248.3 %reduce-scatter.6.cloned.1.call-start = ((), (), s32[]{:S(2)}) async-start(), calls=%async_computation.9 | async-start | bytes 4718592 | tf_op jit(solution)/shard_map/reduce_scatter | solution.py:865
  290.5 4.2 copy-start.9
  364.1 8.1 %copy-start.21 = (bf16[16,48,1664]{2,1,0:T(8,128)(2,1)}, bf16[16,48,1664]{2,1,0:T(8,128)(2,1)S(1)}, u32[]{:S(2)}) copy-start(bf16[16,48,1664]{2,1,0:T(8,128)(2,1)S(1)} %all_to_all.20) | copy-start | bytes 7667716
  372.1 2.6 copy-start.25
  380.1 1.5 copy-start.26
  385.0 98.1 %reduce-scatter.4.cloned.1.call-start = ((), (), s32[]{:S(2)}) async-start(), calls=%async_computation.8 | async-start | bytes 9437184 | tf_op jit(solution)/shard_map/reduce_scatter | solution.py:864
  385.5 4.9 copy-start.22
  385.5 4.9 copy-start.27
  475.7 57.6 %all-to-all-start.3 = ((bf16[16,48,1536]{2,1,0:T(8,128)(2,1)}), bf16[16,48,1536]{2,1,0:T(8,128)(2,1)}, u32[]{:S(2)}, u32[]{:S(2)}) async-start(bf16[16,48,1536]{2,1,0:T(8,128)(2,1)} %bitcast.89), calls=%async_computation.5 | async-start | bytes 4718592 | tf_op jit(solution)/shard_map/all_to_all | solution.py:782
  482.8 103.1 %reduce-scatter.8.cloned.1.call-start = ((), (), s32[]{:S(2)}) async-start(), calls=%async_computation.10 | async-start | bytes 4718592 | tf_op jit(solution)/shard_map/reduce_scatter | solution.py:904
  485.7 2.7 copy-start.10
  488.5 2.0 copy-start.20
  490.9 5.8 copy-start.12
  533.4 2.6 copy-start.11
  538.5 3.5 copy-start.13
  542.0 43.9 %copy-start.18 = (bf16[256,2560]{1,0:T(8,128)(2,1)S(1)}, bf16[256,2560]{1,0:T(8,128)(2,1)}, u32[]{:S(2)}) copy-start(bf16[256,2560]{1,0:T(8,128)(2,1)} %constant_dynamic-update-slice_fusion.1) | copy-start | bytes 3932164
  542.0 45.1 %copy-start.16 = (bf16[1,256,1536]{2,1,0:T(8,128)(2,1)S(1)}, bf16[1,256,1536]{2,1,0:T(8,128)(2,1)}, u32[]{:S(2)}) copy-start(bf16[1,256,1536]{2,1,0:T(8,128)(2,1)} %param.12) | copy-start | bytes 2359300
  585.9 10.7 %slice-start = ((s8[4718592]{0:T(1024)(128)(4,1)}), s8[4194304]{0:T(1024)(128)(4,1)S(1)}, s32[]{:S(2)}) async-start(s8[4718592]{0:T(1024)(128)(4,1)} %bitcast.77), calls=%async_computation.11 | async-start | bytes 8388608
  587.1 9.5 %slice-start.1 = ((s8[4718592]{0:T(1024)(128)(4,1)}), s8[524288]{0:T(1024)(128)(4,1)S(1)}, s32[]{:S(2)}) async-start(s8[4718592]{0:T(1024)(128)(4,1)} %bitcast.77), calls=%async_computation.12 | async-start | bytes 1048576
  596.6 6.1 copy-start
  596.6 6.1 copy-start.1
  751.8 3.6 copy-start.3
  755.3 2.1 copy-start.14
  755.3 2.3 copy-start.17
  755.3 3.2 copy-start.23
  (4 other events, 4.2 us)
Sparse Core Ops, SparseCore 0:
  164.0 64.2 all-gather.1
  385.1 10.6 reduce-scatter.5
  398.8 15.6 reduce-scatter.3
  533.5 52.3 reduce-scatter.7

commit v3 on v2

--- a/solution.py
+++ b/solution.py
@@ -289,14 +289,23 @@
     pl.semaphore_wait(barrier, len(devices))
 
 
-def spread_kernel(
+def front_kernel(
     layers,
     shard_ref,
     in_ref,
     down_ref,
-    all_ref,
+    tokens_ref,
+    w_all_ref,
     w_in_ref,
     w_down_ref,
+    first_ref,
+    projected_ref,
+    kv_ref,
+    weights,
+    in_wide,
+    down_wide,
+    in_half,
+    down_half,
     unit_sem,
     line_sem,
     x_sem,
@@ -307,23 +316,41 @@
     half_send,
     over_sem,
     over_send,
+    kv_sem,
+    kv_send,
     own_sem,
+    wide_sem,
 ):
     z, core, exp = lax.axis_index("le"), lax.axis_index("core"), lax.axis_index("exp")
     other = 1 - core
-    column = [((z + s) % layers, p) for s in range(layers) for p in range(2)]
     x, y = x_of(exp), y_of(exp)
+    ctx = z * 2 + core
+    rows = shard_ref.shape[0]
+    order = [(z + s) % layers for s in ((2, 1, 3, 0) if layers == 4 else range(layers))]
+    wides = ((in_ref, in_wide), (down_ref, down_wide))
+    halves = ((in_half, w_in_ref), (down_half, w_down_ref))
+
+    loads = []
+    for k, zz in enumerate(order):
+        for a in range(2):
+            load = pltpu.make_async_copy(wides[a][0].at[zz], wides[a][1].at[zz], wide_sem.at[a, k])
+            load.start()
+            loads.append(load)
     meet(
-        [place(zz, (core + p) % 2, exp) for zz, p in column if not (zz is column[0][0] and p == 0)]
+        [
+            place((z + s) % layers, (core + p) % 2, exp)
+            for s in range(layers)
+            for p in range(2)
+            if s + p > 0
+        ]
         + [place(z, core, x), place(z, core, y)]
     )
-    rows = shard_ref.shape[0]
 
     def number(zz, cc, ee):
         return (zz * 2 + cc) * 4 + ee
 
     def unit(zz, cc, ee):
-        return all_ref.at[pl.ds(number(zz, cc, ee) * rows, rows), :]
+        return weights.at[pl.ds(pl.multiple_of(number(zz, cc, ee) * rows, 16), rows), :]
 
     def send(src, who, sem, device):
         return remote(src, unit(*who), sem, unit_sem.at[number(*who)], device)
@@ -345,29 +372,31 @@
     keep.start()
     go(send(shard_ref, me, line_sem.at[layers], place(z + 1, core, exp)), z < layers - 1)
     go(send(shard_ref, me, line_sem.at[layers + 1], place(z - 1, core, exp)), z > 0)
-
-    ctx = z * 2 + core
-    arrays = ((in_ref, w_in_ref), (down_ref, w_down_ref))
+    go(send(shard_ref, me, x_sem.at[layers], place(z, core, x)))
+    go(send(shard_ref, me, y_sem.at[layers], place(z, core, y)))
+    go(send(shard_ref, me, core_sem.at[layers], place(z, other, exp)))
+
+    slab = 16
+    for k, zz in enumerate(order):
+        for a in range(2):
+            loads[2 * k + a].wait()
+            src, dst = wides[a][1], halves[a][0]
+
+            @pl.loop(0, src.shape[1] // slab)
+            def _(i, zz=zz, src=src, dst=dst):
+                at = pl.ds(pl.multiple_of(i * slab, slab), slab)
+                dst[zz, at, :] = src[zz, at, :].astype(BF16)
 
     def half(a, source, p):
-        src, dst = arrays[a]
+        src, dst = halves[a]
         n, cols = src.shape[1], src.shape[2] // 2
         return dst.at[pl.ds(source * n, n), pl.ds(pl.multiple_of(p * cols, 128), cols)]
 
     def mine(a, zz, p):
-        src = arrays[a][0]
+        src = halves[a][0]
         cols = src.shape[2] // 2
         return src.at[zz, :, pl.ds(pl.multiple_of(p * cols, 128), cols)]
 
-    for a in range(2):
-        pltpu.make_async_copy(mine(a, z, core), half(a, ctx, core), own_sem.at[1 + a]).start()
-
-    def own_sends(k, src):
-        go(send(src, me, x_sem.at[k], place(z, core, x)))
-        go(send(src, me, y_sem.at[k], place(z, core, y)))
-        go(send(src, me, core_sem.at[k], place(z, other, exp)))
-
-    own_sends(layers, shard_ref)
     def layer(k):
         return jnp.where(z < layers // 2, k, layers - 1 - k)
 
@@ -376,7 +405,7 @@
         who = (zz, core, exp)
 
         @pl.when(zz != z)
-        def _(zz=zz, who=who, k=k):
+        def _(who=who):
             arrive(who)
 
         go(send(unit(*who), who, line_sem.at[k], place(z + 1, core, exp)), (zz < z) & (z < layers - 1))
@@ -385,13 +414,15 @@
         go(send(unit(*who), who, y_sem.at[k], place(z, core, y)), zz != z)
         go(send(unit(*who), who, core_sem.at[k], place(z, other, exp)), zz != z)
 
-    for s in range(layers):
-        zz = (z + s) % layers
-        for p in range(2):
-            if s == 0 and p == 0:
-                continue
-            pp = (core + p) % 2
-            for a in range(2):
+    for a in range(2):
+        pltpu.make_async_copy(mine(a, z, core), half(a, ctx, core), own_sem.at[1 + a]).start()
+
+    def hand_out(a):
+        for s, zz in enumerate(order):
+            for p in range(2):
+                if s == layers - 1 and p == 0:
+                    continue
+                pp = (core + p) % 2
                 go(
                     remote(
                         mine(a, zz, pp),
@@ -401,7 +432,6 @@
                         place(zz, pp, exp),
                     )
                 )
-    for a in range(2):
         go(
             remote(
                 mine(a, z, core),
@@ -411,6 +441,8 @@
                 place(z, other, exp),
             )
         )
+
+    hand_out(0)
 
     for k in range(layers):
         zz = layer(k)
@@ -427,20 +459,69 @@
         far = (layer(k), core, y_of(x))
         arrive(far)
         go(send(unit(*far), far, core_sem.at[3 * layers + 1 + k], place(z, other, exp)))
-
-    for s in range(layers):
+    for ee in range(4):
+        for zz in range(layers):
+            arrive((zz, other, ee))
+    keep.wait()
+    save = pltpu.make_async_copy(weights, w_all_ref, own_sem.at[3])
+    save.start()
+
+    depth, count = tokens_ref.shape[1], tokens_ref.shape[0]
+    qkv_cols, head_cols = projected_ref.shape[1], HEADS * HEAD
+    inputs = tokens_ref[...].astype(F32)
+    gain = jnp.concatenate(
+        [
+            jnp.transpose(weights[i * 128 : (i + 1) * 128, qkv_cols : qkv_cols + AUX].astype(F32))[0:1, :]
+            for i in range(depth // 128)
+        ],
+        axis=1,
+    )
+    first_ref[...] = (inputs * norm_scale(inputs) * gain).astype(BF16)
+    tile = 512
+
+    @pl.loop(0, (qkv_cols - head_cols) // tile)
+    def _(i):
+        at = pl.ds(pl.multiple_of(head_cols + i * tile, tile), tile)
+        projected_ref[:, at] = dot(first_ref[...], weights[:, at]).astype(BF16)
+
+    def block(source):
+        return kv_ref.at[pl.ds(pl.multiple_of(source * count, 16), count), :]
+
+    def share(src, source, sem, device):
+        return remote(src, block(source), sem, kv_sem.at[source], device)
+
+    own = projected_ref.at[:, pl.ds(head_cols, qkv_cols - head_cols)]
+    keep_kv = pltpu.make_async_copy(own, block(ctx), own_sem.at[0])
+    keep_kv.start()
+    go(share(own, ctx, kv_send.at[2 * layers], place(z + 1, core, exp)), z < layers - 1)
+    go(share(own, ctx, kv_send.at[2 * layers + 1], place(z - 1, core, exp)), z > 0)
+    go(share(own, ctx, kv_send.at[2 * layers + 2], place(z, other, exp)))
+
+    @pl.loop(0, head_cols // tile)
+    def _(i):
+        at = pl.ds(pl.multiple_of(i * tile, tile), tile)
+        projected_ref[:, at] = dot(first_ref[...], weights[:, at]).astype(BF16)
+
+    for k in range(layers):
+        zz = layer(k)
+        source = zz * 2 + core
+
+        @pl.when(zz != z)
+        def _(source=source):
+            share(block(source), source, kv_send.at[0], place(z, other, exp)).wait_recv()
+
+        go(share(block(source), source, kv_send.at[k], place(z + 1, core, exp)), (zz < z) & (z < layers - 1))
+        go(share(block(source), source, kv_send.at[k], place(z - 1, core, exp)), (zz > z) & (z > 0))
+        go(share(block(source), source, kv_send.at[layers + k], place(z, other, exp)), zz != z)
+        if k == layers // 2:
+            hand_out(1)
+
+    for s, zz in enumerate(order[::-1]):
         for p in range(2):
             if s == 0 and p == 0:
                 continue
-            source = ((z + s) % layers) * 2 + (core + p) % 2
+            source = zz * 2 + (core + p) % 2
             for a in range(2):
-                copy = remote(
-                    half(a, source, core),
-                    half(a, source, core),
-                    over_send.at[a, s * 2 + p],
-                    over_sem.at[a, source],
-                    place(z, other, exp),
-                )
                 remote(
                     half(a, source, core),
                     half(a, source, core),
@@ -448,11 +529,19 @@
                     half_sem.at[a, source],
                     place(z, other, exp),
                 ).wait_recv()
-                go(copy)
-
-    for ee in range(4):
-        for zz in range(layers):
-            arrive((zz, other, ee))
+                go(
+                    remote(
+                        half(a, source, core),
+                        half(a, source, core),
+                        over_send.at[a, s * 2 + p],
+                        over_sem.at[a, source],
+                        place(z, other, exp),
+                    )
+                )
+
+    for zz in range(layers):
+        source = zz * 2 + other
+        share(block(source), source, kv_send.at[0], place(z, other, exp)).wait_recv()
     for source in range(2 * layers):
         for a in range(2):
             remote(
@@ -462,7 +551,8 @@
                 over_sem.at[a, source],
                 place(z, other, exp),
             ).wait_recv()
-    keep.wait()
+    keep_kv.wait()
+    save.wait()
     for a in range(2):
         pltpu.make_async_copy(mine(a, z, core), half(a, ctx, core), own_sem.at[1 + a]).wait()
     for copy, condition in started:
@@ -472,21 +562,32 @@
             pl.when(condition)(copy.wait_send)
 
 
-def spread(shard, expert_in, expert_out):
+def front(shard, expert_in, expert_out, tokens, qkv_cols):
     layers = expert_in.shape[0]
     rows_in, rows_out = expert_in.shape[1], expert_out.shape[1]
+    depth, cols = shard.shape[0] * 8 * layers, shard.shape[1]
+    count = tokens.shape[0]
     any_space = pl.BlockSpec(memory_space=pl.ANY)
+    vmem = pl.BlockSpec(memory_space=pltpu.VMEM)
     dma = pltpu.SemaphoreType.DMA
     return pl.pallas_call(
-        functools.partial(spread_kernel, layers),
+        functools.partial(front_kernel, layers),
         out_shape=(
-            jax.ShapeDtypeStruct((shard.shape[0] * 8 * layers, shard.shape[1]), BF16),
+            jax.ShapeDtypeStruct((depth, cols), BF16),
             jax.ShapeDtypeStruct((rows_in * 2 * layers, expert_in.shape[2]), BF16),
             jax.ShapeDtypeStruct((rows_out * 2 * layers, expert_out.shape[2]), BF16),
+            jax.ShapeDtypeStruct((count, depth), BF16),
+            jax.ShapeDtypeStruct((count, qkv_cols), BF16),
+            jax.ShapeDtypeStruct((count * 2 * layers, qkv_cols - HEADS * HEAD), BF16),
         ),
-        in_specs=[any_space] * 3,
-        out_specs=(any_space,) * 3,
+        in_specs=[any_space] * 3 + [vmem],
+        out_specs=(any_space,) * 3 + (vmem, vmem, any_space),
         scratch_shapes=[
+            pltpu.VMEM((depth, cols), BF16),
+            pltpu.VMEM(expert_in.shape, F32),
+            pltpu.VMEM(expert_out.shape, F32),
+            pltpu.VMEM(expert_in.shape, BF16),
+            pltpu.VMEM(expert_out.shape, BF16),
             dma((8 * layers,)),
             dma((layers + 2,)),
             dma((layers + 1,)),
@@ -497,11 +598,276 @@
             dma((2, 2 * layers)),
             dma((2, 2 * layers)),
             dma((2, 2 * layers + 1)),
-            dma((3,)),
+            dma((2 * layers,)),
+            dma((2 * layers + 3,)),
+            dma((4,)),
+            dma((2, layers)),
         ],
-        compiler_params=pltpu.CompilerParams(collective_id=0, has_side_effects=True),
-        name="spread",
-    )(shard, expert_in, expert_out)
+        compiler_params=pltpu.CompilerParams(
+            collective_id=0, has_side_effects=True, vmem_limit_bytes=48 * 2**20
+        ),
+        name="front",
+    )(shard, expert_in, expert_out, tokens)
+
+
+def experts_kernel(
+    layers,
+    rows_ref,
+    gates_ref,
+    grads_ref,
+    w_in_ref,
+    w_down_ref,
+    out_ref,
+    back_ref,
+    back_gates_ref,
+    d_in_ref,
+    d_down_ref,
+    w_in,
+    w_down,
+    got,
+    got_gates,
+    x_s,
+    grad_s,
+    hidden_s,
+    inner_s,
+    back_s,
+    back_gates_s,
+    other_in,
+    other_down,
+    pair_in,
+    pair_down,
+    row_sem,
+    row_send,
+    gate_sem,
+    gate_send,
+    back_sem,
+    back_send,
+    back_gate_sem,
+    back_gate_send,
+    pair_sem,
+    pair_send,
+    load_sem,
+):
+    z, core, exp = lax.axis_index("le"), lax.axis_index("core"), lax.axis_index("exp")
+    other = 1 - core
+    columns = rows_ref.shape[0] // layers
+    me = exp * layers + z
+    cap, depth = rows_ref.shape[1], rows_ref.shape[2]
+    chunk = columns * cap
+    loads = [
+        pltpu.make_async_copy(w_in_ref, w_in, load_sem.at[0]),
+        pltpu.make_async_copy(w_down_ref, w_down, load_sem.at[1]),
+    ]
+    for load in loads:
+        load.start()
+    order = [(z + s) % layers for s in ((2, 1, 3, 0) if layers == 4 else range(layers))]
+    peers = [
+        (zz, (exp + t) % columns)
+        for s, zz in enumerate(order)
+        for t in range(columns)
+        if not (s == layers - 1 and t == 0)
+    ]
+    meet([place(zz, core, ee) for zz, ee in peers] + [place(z, other, exp)])
+
+    started = []
+
+    def go(copy):
+        copy.start()
+        started.append(copy)
+
+    keeps = [
+        pltpu.make_async_copy(rows_ref.at[me], got.at[me], load_sem.at[2]),
+        pltpu.make_async_copy(gates_ref.at[me], got_gates.at[me], load_sem.at[3]),
+    ]
+    for keep in keeps:
+        keep.start()
+    for k, (zz, ee) in enumerate(peers):
+        there = ee * layers + zz
+        go(remote(gates_ref.at[there], got_gates.at[me], gate_send.at[k], gate_sem.at[me], place(zz, core, ee)))
+        go(remote(rows_ref.at[there], got.at[me], row_send.at[k], row_sem.at[me], place(zz, core, ee)))
+    for load in loads + keeps:
+        load.wait()
+
+    eye = lax.broadcasted_iota(jnp.int32, (cap, 128), 0) == lax.broadcasted_iota(jnp.int32, (cap, 128), 1)
+    tile = 256
+
+    def tiles(i):
+        return pl.ds(pl.multiple_of(i * tile, tile), tile)
+
+    for k, zz in enumerate(order[::-1]):
+        rows = pl.ds(k * chunk, chunk)
+        for ee in range(columns):
+            source = ee * layers + zz
+
+            @pl.when(source != me)
+            def _(source=source):
+                here = place(z, other, exp)
+                remote(got.at[source], got.at[source], row_send.at[0], row_sem.at[source], here).wait_recv()
+                remote(
+                    got_gates.at[source], got_gates.at[source], gate_send.at[0], gate_sem.at[source], here
+                ).wait_recv()
+
+            at = pl.ds(k * chunk + ee * cap, cap)
+            x_s[at, :] = got[source]
+            gate = jnp.sum(jnp.where(eye, got_gates[source, 0:1, :], 0.0), axis=1, keepdims=True)
+            grad_s[at, :] = (gate * grads_ref[source].astype(F32)).astype(BF16)
+
+        @pl.loop(0, FF // tile)
+        def _(i, rows=rows):
+            up_at = pl.ds(pl.multiple_of(FF + i * tile, tile), tile)
+            gate = dot(x_s[rows, :], w_in[:, tiles(i)])
+            up = dot(x_s[rows, :], w_in[:, up_at])
+            grad_hidden = dot(grad_s[rows, :], w_down[tiles(i), :], ((1,), (1,)))
+            sigmoid = jax.nn.sigmoid(gate)
+            silu = gate * sigmoid
+            hidden_s[rows, tiles(i)] = (silu * up).astype(BF16)
+            inner_s[rows, tiles(i)] = (grad_hidden * up * sigmoid * (1.0 + gate * (1.0 - sigmoid))).astype(BF16)
+            inner_s[rows, up_at] = (grad_hidden * silu).astype(BF16)
+
+        @pl.loop(0, depth // tile)
+        def _(i, rows=rows, zz=zz):
+            back = dot(inner_s[rows, :], w_in[tiles(i), :], ((1,), (1,))).astype(BF16)
+            for ee in range(columns):
+                back_s[ee * layers + zz, :, tiles(i)] = back[ee * cap : (ee + 1) * cap]
+
+        @pl.loop(0, depth // tile, init_carry=jnp.zeros((chunk, 128), F32))
+        def gate_grads(i, sums, rows=rows, zz=zz):
+            result = dot(hidden_s[rows, :], w_down[:, tiles(i)]).astype(BF16)
+            parts = []
+            for ee in range(columns):
+                part = result[ee * cap : (ee + 1) * cap]
+                out_ref[ee * layers + zz, :, tiles(i)] = part
+                parts.append(part.astype(F32) * grads_ref[ee * layers + zz, :, tiles(i)].astype(F32))
+            product = jnp.concatenate(parts, axis=0)
+            return sums + product[:, :128] + product[:, 128:]
+
+        gate_grads = jnp.sum(gate_grads, axis=1, keepdims=True)
+        for ee in range(columns):
+            there = ee * layers + zz
+            column = gate_grads[ee * cap : (ee + 1) * cap]
+            line = jnp.sum(jnp.where(eye, column, 0.0), axis=0, keepdims=True)
+            back_gates_s[there] = jnp.broadcast_to(line, (8, 128))
+            row_copy = remote(
+                back_s.at[there],
+                back_ref.at[me],
+                back_send.at[there],
+                back_sem.at[me],
+                place(zz, core, ee),
+            )
+            gate_copy = remote(
+                back_gates_s.at[there],
+                back_gates_ref.at[me],
+                back_gate_send.at[there],
+                back_gate_sem.at[me],
+                place(zz, core, ee),
+            )
+
+            @pl.when(there != me)
+            def _(row_copy=row_copy, gate_copy=gate_copy):
+                row_copy.start()
+                gate_copy.start()
+
+    own = [
+        pltpu.make_async_copy(back_s.at[me], back_ref.at[me], load_sem.at[2]),
+        pltpu.make_async_copy(back_gates_s.at[me], back_gates_ref.at[me], load_sem.at[3]),
+    ]
+    for copy in own:
+        copy.start()
+
+    half_in, half_down = d_in_ref.shape[1], d_down_ref.shape[1]
+
+    def in_part(i, p):
+        cols = pl.ds(pl.multiple_of(p * half_in, 128), half_in)
+        return dot(x_s[:, tiles(i)], inner_s[:, cols], ((0,), (0,)))
+
+    def down_part(i, p):
+        cols = pl.ds(pl.multiple_of(p * half_down, 128), half_down)
+        return dot(hidden_s[:, tiles(i)], grad_s[:, cols], ((0,), (0,)))
+
+    @pl.loop(0, depth // tile)
+    def _(i):
+        other_in[tiles(i), :] = in_part(i, other).astype(BF16)
+
+    go(remote(other_in, pair_in, pair_send.at[0], pair_sem.at[0], place(z, other, exp)))
+
+    @pl.loop(0, FF // tile)
+    def _(i):
+        other_down[tiles(i), :] = down_part(i, other).astype(BF16)
+
+    go(remote(other_down, pair_down, pair_send.at[1], pair_sem.at[1], place(z, other, exp)))
+    remote(other_in, pair_in, pair_send.at[0], pair_sem.at[0], place(z, other, exp)).wait_recv()
+
+    @pl.loop(0, depth // tile)
+    def _(i):
+        d_in_ref[tiles(i), :] = (in_part(i, core) + pair_in[tiles(i), :].astype(F32)).astype(BF16)
+
+    remote(other_down, pair_down, pair_send.at[1], pair_sem.at[1], place(z, other, exp)).wait_recv()
+
+    @pl.loop(0, FF // tile)
+    def _(i):
+        d_down_ref[tiles(i), :] = (down_part(i, core) + pair_down[tiles(i), :].astype(F32)).astype(BF16)
+
+    for copy in own:
+        copy.wait()
+    for k, (zz, ee) in enumerate(peers):
+        there = ee * layers + zz
+        row_copy = remote(
+            back_s.at[there], back_ref.at[there], back_send.at[there], back_sem.at[there], place(zz, core, ee)
+        )
+        gate_copy = remote(
+            back_gates_s.at[there],
+            back_gates_ref.at[there],
+            back_gate_send.at[there],
+            back_gate_sem.at[there],
+            place(zz, core, ee),
+        )
+        row_copy.wait()
+        gate_copy.wait()
+    for copy in started:
+        copy.wait_send()
+
+
+def experts(rows, gates, grads, w_in, w_down, layers):
+    count, cap, depth = rows.shape
+    any_space = pl.BlockSpec(memory_space=pl.ANY)
+    vmem = pl.BlockSpec(memory_space=pltpu.VMEM)
+    dma = pltpu.SemaphoreType.DMA
+    half_in = jax.ShapeDtypeStruct((depth, FF), BF16)
+    half_down = jax.ShapeDtypeStruct((FF, depth // 2), BF16)
+    return pl.pallas_call(
+        functools.partial(experts_kernel, layers),
+        out_shape=(
+            jax.ShapeDtypeStruct(rows.shape, BF16),
+            jax.ShapeDtypeStruct(rows.shape, BF16),
+            jax.ShapeDtypeStruct(gates.shape, F32),
+            half_in,
+            half_down,
+        ),
+        in_specs=[any_space, any_space, vmem, any_space, any_space],
+        out_specs=(vmem, any_space, any_space, vmem, vmem),
+        scratch_shapes=[
+            pltpu.VMEM(w_in.shape, BF16),
+            pltpu.VMEM(w_down.shape, BF16),
+            pltpu.VMEM(rows.shape, BF16),
+            pltpu.VMEM(gates.shape, F32),
+            pltpu.VMEM((count * cap, depth), BF16),
+            pltpu.VMEM((count * cap, depth), BF16),
+            pltpu.VMEM((count * cap, FF), BF16),
+            pltpu.VMEM((count * cap, 2 * FF), BF16),
+            pltpu.VMEM(rows.shape, BF16),
+            pltpu.VMEM(gates.shape, F32),
+            pltpu.VMEM(half_in.shape, BF16),
+            pltpu.VMEM(half_down.shape, BF16),
+            pltpu.VMEM(half_in.shape, BF16),
+            pltpu.VMEM(half_down.shape, BF16),
+        ]
+        + [dma((count,))] * 8
+        + [dma((2,)), dma((2,)), dma((4,))],
+        compiler_params=pltpu.CompilerParams(
+            collective_id=2, has_side_effects=True, vmem_limit_bytes=60 * 2**20
+        ),
+        name="experts",
+    )(rows, gates, grads, w_in, w_down)
 
 
 def collect_kernel(
@@ -741,8 +1107,9 @@
     aux = jnp.concatenate([gain_attn[:, None], gain_moe[:, None], router_weight], axis=1)
     aux = jnp.pad(aux, ((0, 0), (0, AUX - aux.shape[1])))
     shard = jnp.concatenate([qkv_weight, aux, out_weight], axis=1).astype(BF16)
-    if (copies, exp_local, n_exp) == (2, 4, 4):
-        w_all, w_in, w_down = spread(shard, expert_in.astype(BF16), expert_out.astype(BF16))
+    special = (copies, exp_local, n_exp) == (2, 4, 4)
+    if special:
+        w_all, w_in, w_down, first, projected, kv = front(shard, expert_in, expert_out, tokens[0], cols)
     else:
         w_all = lax.all_gather(shard, ALL, axis=0, tiled=True)
 
@@ -790,9 +1157,10 @@
     inputs = tokens[0].astype(F32)
     scale_first = norm_scale(inputs)
     norm_first = inputs * scale_first
-    first = (norm_first * gain_first).astype(BF16)
-    projected = dot(first, w_qkv).astype(BF16)
-    kv = lax.all_gather(projected[:, head_width:], CTX, axis=0, tiled=True)
+    if not special:
+        first = (norm_first * gain_first).astype(BF16)
+        projected = dot(first, w_qkv).astype(BF16)
+        kv = lax.all_gather(projected[:, head_width:], CTX, axis=0, tiled=True)
     kv, grad_y_send = lax.optimization_barrier((kv, dot(send_hot, cotangent[0]).astype(BF16)))
     grad_y_rows = to_experts(grad_y_send)
     mine = (lax.axis_index(CTX) * (tok_rows // BLK)).astype(jnp.int32).reshape(1)
@@ -811,69 +1179,86 @@
         axis=1,
         keepdims=True,
     )
-
-    def in_parts(column):
-        high = lax.reduce_precision(column, 8, 7)
-        rest = column - high
-        mid = lax.reduce_precision(rest, 8, 7)
-        parts = jnp.concatenate([high, mid, rest - mid], axis=1).astype(BF16)
-        return jnp.pad(parts, ((0, 0), (0, AUX - 3)))
-
-    gate_parts = in_parts(gate_rows)
-    payload = to_experts(
-        jnp.concatenate([dot(send_hot, second).astype(BF16), gate_parts], axis=1)
-    )
-    received = payload[:, :D]
-    gate_got = jnp.sum(payload[:, D : D + 3].astype(F32), axis=1, keepdims=True)
-
-    gate_up = dot(received, w_in)
-    gate_part = gate_up[:, :FF]
-    up_part = gate_up[:, FF:]
-    sigmoid_gate = jax.nn.sigmoid(gate_part)
-    silu_gate = gate_part * sigmoid_gate
-    hidden = (silu_gate * up_part).astype(BF16)
-    expert_rows = dot(hidden, w_down)
-    expert_rows = expert_rows.astype(BF16)
-    grad_y_rows = grad_y_rows.astype(F32)
-    returned = to_experts(expert_rows)
-
-    grad_rows = (gate_got * grad_y_rows).astype(BF16)
-    gate_grad_parts = in_parts(
-        jnp.sum(grad_y_rows * expert_rows.astype(F32), axis=1, keepdims=True)
-    )
-    half_d = D // 2
-    grad_hidden = dot(grad_rows, w_down, ((1,), (1,)))
-    grad_gate = (
-        grad_hidden * up_part * sigmoid_gate * (1.0 + gate_part * (1.0 - sigmoid_gate))
-    ).astype(BF16)
-    grad_up = (grad_hidden * silu_gate).astype(BF16)
-    grad_gate_up = jnp.concatenate([grad_gate, grad_up], axis=1)
-    grad_back = dot(grad_gate_up, w_in, ((1,), (1,)))
-    grad_returned = to_experts(jnp.concatenate([grad_back.astype(BF16), gate_grad_parts], axis=1))
-
-    grad_in = jnp.stack(
-        [dot(received, grad_gate, ((0,), (0,))), dot(received, grad_up, ((0,), (0,)))]
-    ).astype(BF16)
-    grad_down = jnp.stack(
-        [
-            dot(hidden, grad_rows[:, :half_d], ((0,), (0,))),
-            dot(hidden, grad_rows[:, half_d:], ((0,), (0,))),
-        ]
-    ).astype(BF16)
-
-    grad_in = lax.psum_scatter(grad_in, "core", scatter_dimension=0, tiled=True)[0]
-    grad_down = lax.psum_scatter(grad_down, "core", scatter_dimension=0, tiled=True)[0]
-    grad_returned, grad_in, grad_down = lax.optimization_barrier((grad_returned, grad_in, grad_down))
+    if special:
+        slot_gates = jnp.broadcast_to(
+            jnp.pad(gate_rows.reshape(EXPERTS, 1, CAP), ((0, 0), (0, 0), (0, 128 - CAP))), (EXPERTS, 8, 128)
+        )
+        expert_rows, grad_returned, gate_grads, grad_in, grad_down = experts(
+            dot(send_hot, second).astype(BF16).reshape(EXPERTS, CAP, D),
+            slot_gates,
+            grad_y_rows.reshape(EXPERTS, CAP, D),
+            w_in,
+            w_down,
+            exp_local,
+        )
+        returned = to_experts(expert_rows.reshape(EXPERTS * CAP, D))
+        grad_returned = grad_returned.reshape(EXPERTS * CAP, D)
+        gate_grads = gate_grads[:, 0, :CAP].reshape(1, EXPERTS * CAP)
+    else:
+        def in_parts(column):
+            high = lax.reduce_precision(column, 8, 7)
+            rest = column - high
+            mid = lax.reduce_precision(rest, 8, 7)
+            parts = jnp.concatenate([high, mid, rest - mid], axis=1).astype(BF16)
+            return jnp.pad(parts, ((0, 0), (0, AUX - 3)))
+
+        gate_parts = in_parts(gate_rows)
+        payload = to_experts(
+            jnp.concatenate([dot(send_hot, second).astype(BF16), gate_parts], axis=1)
+        )
+        received = payload[:, :D]
+        gate_got = jnp.sum(payload[:, D : D + 3].astype(F32), axis=1, keepdims=True)
+
+        gate_up = dot(received, w_in)
+        gate_part = gate_up[:, :FF]
+        up_part = gate_up[:, FF:]
+        sigmoid_gate = jax.nn.sigmoid(gate_part)
+        silu_gate = gate_part * sigmoid_gate
+        hidden = (silu_gate * up_part).astype(BF16)
+        expert_rows = dot(hidden, w_down)
+        expert_rows = expert_rows.astype(BF16)
+        grad_y_rows = grad_y_rows.astype(F32)
+        returned = to_experts(expert_rows)
+
+        grad_rows = (gate_got * grad_y_rows).astype(BF16)
+        gate_grad_parts = in_parts(
+            jnp.sum(grad_y_rows * expert_rows.astype(F32), axis=1, keepdims=True)
+        )
+        half_d = D // 2
+        grad_hidden = dot(grad_rows, w_down, ((1,), (1,)))
+        grad_gate = (
+            grad_hidden * up_part * sigmoid_gate * (1.0 + gate_part * (1.0 - sigmoid_gate))
+        ).astype(BF16)
+        grad_up = (grad_hidden * silu_gate).astype(BF16)
+        grad_gate_up = jnp.concatenate([grad_gate, grad_up], axis=1)
+        grad_back = dot(grad_gate_up, w_in, ((1,), (1,)))
+        grad_returned = to_experts(jnp.concatenate([grad_back.astype(BF16), gate_grad_parts], axis=1))
+
+        grad_in = jnp.stack(
+            [dot(received, grad_gate, ((0,), (0,))), dot(received, grad_up, ((0,), (0,)))]
+        ).astype(BF16)
+        grad_down = jnp.stack(
+            [
+                dot(hidden, grad_rows[:, :half_d], ((0,), (0,))),
+                dot(hidden, grad_rows[:, half_d:], ((0,), (0,))),
+            ]
+        ).astype(BF16)
+
+        grad_in = lax.psum_scatter(grad_in, "core", scatter_dimension=0, tiled=True)[0]
+        grad_down = lax.psum_scatter(grad_down, "core", scatter_dimension=0, tiled=True)[0]
+        grad_returned, grad_in, grad_down = lax.optimization_barrier((grad_returned, grad_in, grad_down))
+        gate_grads = jnp.sum(grad_returned[:, D:].astype(F32), axis=1).reshape(1, EXPERTS * CAP)
+        grad_returned = grad_returned[:, :D]
 
     grad_y = cotangent[0].astype(F32)
     pick_hot = [p.astype(BF16) for p in picks]
     grad_gates = jnp.concatenate(
-        [jnp.sum(dot(p, grad_returned[:, D:]), axis=1, keepdims=True) for p in pick_hot], axis=1
+        [jnp.sum(jnp.where(p, gate_grads, 0.0), axis=1, keepdims=True) for p in picks], axis=1
     )
     grad_chosen = gates * (grad_gates - jnp.sum(gates * grad_gates, axis=-1, keepdims=True))
     grad_logits = jnp.sum(grad_chosen[:, :, None] * route_hot, axis=1).astype(BF16)
     grad_router = dot(second, grad_logits, ((0,), (0,)))
-    grad_second = dot(pick_hot[0] + pick_hot[1], grad_returned[:, :D]) + dot(
+    grad_second = dot(pick_hot[0] + pick_hot[1], grad_returned) + dot(
         grad_logits, w_router, ((1,), (1,))
     )
     grad_gain_second = jnp.sum(grad_second * norm_second, axis=0)
@@ -915,7 +1300,7 @@
     part = jnp.concatenate(
         [grad_qkv.astype(BF16), last.astype(BF16), grad_attn_out.astype(BF16), late.astype(BF16)], axis=1
     )
-    if (copies, exp_local, n_exp) == (2, 4, 4):
+    if special:
         total, sum_in, sum_down = collect(part, grad_in, grad_down, exp_local)
     else:
         total = lax.psum_scatter(part, ALL, scatter_dimension=0, tiled=True).astype(F32)

time: 770 us -> 688 us (0.89)
  Pallas kernels: 316 us -> 482 us
  blocking collectives: 129 us -> 0 us
  waiting for transfers between devices: 147 us -> 64.9 us
  matrix products: 88 us -> 44.2 us
  starting transfers between devices: 14.5 us -> 39.1 us
  other arithmetic: 39.9 us -> 19.7 us
    pallas_call x1 -> x2, Pallas kernels: 133 us -> 282 us  [the longest x1 164 us: front(): pl.pallas_call(functools.partial(front_kernel, layers), out_shape=(jax.Sh...]
    all_to_all x2 -> x0, blocking collectives: 129 us -> none  [to_experts(): lax.all_to_all(rows.reshape((EXPERTS, CAP) + rows.shape[1:]), OWNERS, spl...]
    all_gather x1 -> x0, waiting for transfers between devices: 61.2 us -> none  [on_device(): kv = lax.all_gather(projected[:, head_width:], CTX, axis=0, tiled=True)]
    dot_general x25 -> x14, matrix products: 88 us -> 44.2 us  [dot(): return lax.dot_general(a, b, (dims, ((), ())), preferred_element_type=F32)]
    all_to_all x2, starting transfers between devices: 13.5 us -> 39.1 us  [to_experts(): lax.all_to_all(rows.reshape((EXPERTS, CAP) + rows.shape[1:]), OWNERS, spl...]
    all_to_all x2, waiting for transfers between devices: 45.8 us -> 32.4 us  [to_experts(): lax.all_to_all(rows.reshape((EXPERTS, CAP) + rows.shape[1:]), OWNERS, spl...]
    convert_element_type x4 -> x1, other arithmetic: 12 us -> 2.17 us  [on_device(): gain_first = aux_all[:, 0].astype(F32)]
    pallas_call x1, Pallas kernels: 20.8 us -> 29.5 us  [attend_back(): pl.pallas_call(functools.partial(attend_back_kernel, lengths.shape[1]), o...]
  transfers between devices with their start and end apart: 6 -> 3, of which waited for: 4 -> 3; matrix products, arithmetic and copies ran while one was open for 8% -> 4% of each run, Pallas kernels for 5% -> 8%
where the time goes in v3:
time: 688 us; the launch traced here: 683 us
  Pallas kernels  482 us (70%)
  waiting for transfers between devices  64.9 us (9%)
  matrix products  44.2 us (6%)
  starting transfers between devices  39.1 us (6%)
  other arithmetic  19.7 us (3%)
  local copies, waits for them, and re-layouts  17.9 us (3%)
  between operations  15 us (2%)
    pallas_call x1, Pallas kernels, front(): pl.pallas_call(functools.partial(front_kernel, layers), out_shape=(jax.Sh...  164 us
    pallas_call x1, Pallas kernels, collect(): pl.pallas_call(functools.partial(collect_kernel, layers), out_shape=(jax....  145 us
    pallas_call x1, Pallas kernels, experts(): pl.pallas_call(functools.partial(experts_kernel, layers), out_shape=(jax....  118 us
    dot_general x14, matrix products, dot(): return lax.dot_general(a, b, (dims, ((), ())), preferred_element_type=F32)  44.2 us
    all_to_all x2, starting transfers between devices, to_experts(): lax.all_to_all(rows.reshape((EXPERTS, CAP) + rows.shape[1:]), OWNERS, spl...  39.1 us
    all_to_all x2, waiting for transfers between devices, to_experts(): lax.all_to_all(rows.reshape((EXPERTS, CAP) + rows.shape[1:]), OWNERS, spl...  32.4 us
    reduce_scatter x1, waiting for transfers between devices, on_device(): grad_kv = lax.psum_scatter(grad_kv, CTX, scatter_dimension=0, tiled=True)  32.4 us
    pallas_call x1, Pallas kernels, attend_back(): pl.pallas_call(functools.partial(attend_back_kernel, lengths.shape[1]), o...  29.5 us
  transfers between devices with their start and end apart: 3, of which 3 were waited for; matrix products, arithmetic and copies ran while one was open for 4% of the time, Pallas kernels for 8%

profile of v3, /device:TPU:8, one launch (start us, length us, event | category | flops | bytes accessed | tf_op | source)
XLA Modules:
  0.0 682.6 jit_solution(7632069085306315081)
XLA Ops:
  9.4 2.2 convolution_convert_fusion.3
  11.7 163.6 %front.1 = (bf16[1536,4224]{1,0:T(8,128)(2,1)}, bf16[1536,2048]{1,0:T(8,128)(2,1)}, bf16[1024,1536]{1,0:T(8,128)(2,1)}, bf16[256,1536]{1,0:T(8,128)(2,1)S(1)}, b...) custom-call(bf16[48,4224]{1,0:T(8,128)(2,1)S(1)} %pad_maximum_fusion.shard_ref, f32[4,192,2048]{2,1,0:T(8,128)} %in_ref.1, ...), custom_call_target="tpu_custom_call" | custom-call | tf_op jit(solution)/shard_map/front/pallas_call | solution.py:573
  177.3 14.9 %all-to-all-start = ((bf16[16,48,1536]{2,1,0:T(8,128)(2,1)}), bf16[16,48,1536]{2,1,0:T(8,128)(2,1)}, u32[]{:S(2)}, u32[]{:S(2)}) async-start(bf16[16,48,1536]{2,1,0:T(8,128)(2,1)} %bitcast.6), calls=%async_computation | async-start | bytes 4718592 | tf_op jit(solution)/shard_map/all_to_all | solution.py:1149
  192.3 2.2 convert_reduce_fusion
  194.5 1.3 copy-done.6
  195.8 25.4 %attend.1 = (f32[256,1536]{1,0:T(8,128)S(1)}, bf16[256,1536]{1,0:T(8,128)(2,1)S(1)}, f32[2,8,384]{2,1,0:T(8,128)S(1)}) custom-call(s32[1,3]{1,0:T(1,128)S(1)} %copy-done.7, s32[1,16]{1,0:T(1,128)S(1)} %copy-done.8, s32[1]{0:T(128)} %bitcast.1.mine_ref, bf16[256,2560]{1,0:T(8,128)(2,1)S(1)} %copy-done.6, bf16[2048,1024]{1,0:T(8,128)(2,1)} %get-tuple-element.37.kv_ref), custom_call_target="tpu_custom_call" | custom-call | flops 10000000000 | bytes 10000000 | tf_op jit(solution)/shard_map/attend/pallas_call | solution.py:137
  221.8 22.2 %all-to-all-done = bf16[16,48,1536]{2,1,0:T(8,128)(2,1)} async-done(((bf16[16,48,1536]{2,1,0:T(8,128)(2,1)}), bf16[16,48,1536]{2,1,0:T(8,128)(2,1)}, u32[]{:S(2)}, u32[]{:S(2)}) %all-to-all-start) | async-done | bytes 2359328 | tf_op jit(solution)/shard_map/all_to_all | solution.py:1149
  244.0 3.8 multiply_reduce_fusion.2
  248.1 1.8 fusion.55
  249.8 2.2 convolution_convert_fusion.2
  253.1 118.5 %experts.1 = (bf16[16,48,1536]{2,1,0:T(8,128)(2,1)}, bf16[16,48,1536]{2,1,0:T(8,128)(2,1)}, f32[16,8,128]{2,1,0:T(8,128)}, bf16[1536,1024]{1,0:T(8,128)(2,1)}, bf16[1024,768]{1,0:T(8,128)(2,1)}) custom-call(bf16[16,48,1536]{2,1,0:T(8,128)(2,1)} %bitcast.56, f32[16,8,128]{2,1,0:T(8,128)} %broadcast_in_dim.95.gates_ref, ...), custom_call_target="tpu_custom_call" | custom-call | tf_op jit(solution)/shard_map/experts/pallas_call | solution.py:837
  373.0 3.7 fusion.41
  376.6 24.2 %all-to-all-start.1 = ((bf16[16,48,1536]{2,1,0:T(8,128)(2,1)}), bf16[16,48,1536]{2,1,0:T(8,128)(2,1)}, u32[]{:S(2)}, u32[]{:S(2)}) async-start(bf16[16,48,1536]{2,1,0:T(8,128)(2,1)} %get-tuple-element.51), calls=%async_computation.1 | async-start | bytes 4718592 | tf_op jit(solution)/shard_map/all_to_all | solution.py:1149
  400.9 3.0 multiply_reduce_fusion
  404.4 5.8 convert_multiply_fusion.2
  410.2 1.9 copy.88
  412.9 29.5 %attend_back.1 = (bf16[256,1536]{1,0:T(8,128)(2,1)}, bf16[2048,1024]{1,0:T(8,128)(2,1)}) custom-call(s32[1,3]{1,0:T(1,128)} %lengths_ref.3, s32[1,16]{1,0:T(1,128)} %order_ref.3, s32[1]{0:T(128)} %bitcast.1.mine_ref, bf16[256,2560]{1,0:T(8,128)(2,1)} %copy-done.5, bf16[2048,1024]{1,0:T(8,128)(2,1)} %get-tuple-element.37.kv_ref, ...), custom_call_target="tpu_custom_call" | custom-call | flops 30000001024 | bytes 10000000 | tf_op jit(solution)/shard_map/attend_back/pallas_call | solution.py:239
  442.3 10.2 %all-to-all-done.1 = bf16[16,48,1536]{2,1,0:T(8,128)(2,1)} async-done(((bf16[16,48,1536]{2,1,0:T(8,128)(2,1)}), bf16[16,48,1536]{2,1,0:T(8,128)(2,1)}, u32[]{:S(2)}, u32[]{:S(2)}) %all-to-all-start.1) | async-done | bytes 2359328 | tf_op jit(solution)/shard_map/all_to_all | solution.py:1149
  453.4 1.3 convolution_convert_fusion.4
  455.4 1.1 copy.92
  456.5 3.6 convolution_convert_fusion.1
  461.9 2.5 fusion.13
  464.4 3.4 fusion.21
  467.9 32.4 %reduce-scatter.2.cloned.1.call-done = bf16[256,1024]{1,0:T(8,128)(2,1)} async-done(((bf16[2048,1024]{1,0:T(8,128)(2,1)}), bf16[256,1024]{1,0:T(8,128)(2,1)}) %reduce-scatter.2.cloned.1.call-update) | async-done | bytes 524304 | tf_op jit(solution)/shard_map/reduce_scatter | solution.py:1289
  500.3 1.9 constant_dynamic-update-slice_fusion
  502.2 3.7 convolution_convert_fusion
  505.9 6.8 %fusion.30 = (bf16[1536]{0:T(1024)(128)(2,1)S(1)}, f32[256]{0:T(256)S(1)}, f32[256,1536]{1,0:T(8,128)}) fusion(f32[256]{0:T(256)S(1)} %copy-done.24, bf16[1,256,1536]{2,1,0:T(8,128)(2,1)S(1)} %copy-done, f32[1536]{0:T(1024)S(1)} %copy-done.22, bf16[256,2560]{1,0:T(8,128)(2,1)S(1)} %copy-done.16, bf16[1536,4224]{1,0:T(8,128)(2,1)} %get-tuple-element.41), kind=kOutput, calls=%fused_computation.39 | convolution fusion | flops 2016016640 | bytes 11545600 | tf_op jit(solution)/shard_map/dot_general | solution.py:34
  513.1 6.1 fusion.5.part_ref
  519.1 144.9 %collect.1 = (f32[48,4352]{1,0:T(8,128)S(1)}, bf16[4,192,2048]{2,1,0:T(8,128)(2,1)S(1)}, bf16[4,128,1536]{2,1,0:T(8,128)(2,1)S(1)}) custom-call(bf16[1536,4352]{1,0:T(8,128)(2,1)} %fusion.5.part_ref, bf16[1536,1024]{1,0:T(8,128)(2,1)S(1)} %copy-done.1, bf16[1024,768]{1,0:T(8,128)(2,1)S(1)} %copy-done.2), custom_call_target="tpu_custom_call" | custom-call | tf_op jit(solution)/shard_map/collect/pallas_call | solution.py:1048
  666.3 3.6 convert_element_type.125
  669.9 2.1 convert_element_type.126
  672.6 2.7 fusion.33
  (112 shorter events, 15.2 us)
Async XLA Ops:
  7.2 1.8 copy-start.20
  7.2 1.8 copy-start.21
  7.2 1.9 copy-start.23
  7.2 2.0 copy-start.25
  7.2 2.1 copy-start.26
  7.2 2.2 copy-start.17
  9.4 2.3 copy-start
  175.3 0.9 copy-start.3
  176.2 1.1 copy-start.5
  177.3 17.1 %copy-start.7 = (s32[1,3]{1,0:T(1,128)S(1)}, s32[1,3]{1,0:T(1,128)}, u32[]{:S(2)}) copy-start(s32[1,3]{1,0:T(1,128)} %lengths_ref.3) | copy-start | bytes 40
  177.3 17.1 %copy-start.8 = (s32[1,16]{1,0:T(1,128)S(1)}, s32[1,16]{1,0:T(1,128)}, u32[]{:S(2)}) copy-start(s32[1,16]{1,0:T(1,128)} %order_ref.3) | copy-start | bytes 196
  177.3 66.7 %all-to-all-start = ((bf16[16,48,1536]{2,1,0:T(8,128)(2,1)}), bf16[16,48,1536]{2,1,0:T(8,128)(2,1)}, u32[]{:S(2)}, u32[]{:S(2)}) async-start(bf16[16,48,1536]{2,1,0:T(8,128)(2,1)} %bitcast.6), calls=%async_computation | async-start | bytes 4718592 | tf_op jit(solution)/shard_map/all_to_all | solution.py:1149
  194.4 1.3 copy-start.6
  221.2 0.6 copy-start.9
  247.8 2.0 copy-start.10
  248.1 4.0 copy-start.15
  376.6 75.9 %all-to-all-start.1 = ((bf16[16,48,1536]{2,1,0:T(8,128)(2,1)}), bf16[16,48,1536]{2,1,0:T(8,128)(2,1)}, u32[]{:S(2)}, u32[]{:S(2)}) async-start(bf16[16,48,1536]{2,1,0:T(8,128)(2,1)} %get-tuple-element.51), calls=%async_computation.1 | async-start | bytes 4718592 | tf_op jit(solution)/shard_map/all_to_all | solution.py:1149
  400.9 99.5 %reduce-scatter.2.cloned.1.call-start = ((), (), s32[]{:S(2)}) async-start(), calls=%async_computation.3 | async-start | bytes 4718592 | tf_op jit(solution)/shard_map/reduce_scatter | solution.py:1289
  400.9 3.1 copy-start.11
  400.9 3.1 copy-start.18
  404.4 5.8 copy-start.13
  452.6 4.0 copy-start.14
  456.5 3.6 copy-start.19
  460.2 1.7 copy-start.12
  467.9 34.3 %copy-start.4 = (bf16[256,1536]{1,0:T(8,128)(2,1)S(1)}, bf16[256,1536]{1,0:T(8,128)(2,1)}, u32[]{:S(2)}) copy-start(bf16[256,1536]{1,0:T(8,128)(2,1)} %copy-done.3) | copy-start | bytes 2359300
  502.2 3.7 copy-start.16
  502.2 3.7 copy-start.22
  502.2 3.7 copy-start.24
  505.9 7.2 %slice-start = ((s8[4718592]{0:T(1024)(128)(4,1)}), s8[4194304]{0:T(1024)(128)(4,1)S(1)}, s32[]{:S(2)}) async-start(s8[4718592]{0:T(1024)(128)(4,1)} %bitcast.54), calls=%async_computation.4 | async-start | bytes 8388608
  505.9 7.1 %slice-start.1 = ((s8[4718592]{0:T(1024)(128)(4,1)}), s8[524288]{0:T(1024)(128)(4,1)S(1)}, s32[]{:S(2)}) async-start(s8[4718592]{0:T(1024)(128)(4,1)} %bitcast.54), calls=%async_computation.5 | async-start | bytes 1048576
  513.0 6.1 copy-start.1
  513.1 6.1 copy-start.2
Sparse Core Ops, SparseCore 0:
  452.7 47.5 reduce-scatter.1

commit v4 on v3

--- a/solution.py
+++ b/solution.py
@@ -163,11 +163,12 @@
     kv_ref,
     grad_ref,
     lse_ref,
-    delta_ref,
+    exact_ref,
     dq_ref,
     dkv_ref,
     q_s,
     g_s,
+    delta_s,
     dq_s,
     dkv_s,
 ):
@@ -183,6 +184,15 @@
             q_s[g] = head_tiles(q_ref, rows, g, HEAD**-0.5)
             g_s[g] = head_tiles(grad_ref, rows, g, 1.0)
             dq_s[g] = jnp.zeros((GROUP * BLK, 128), F32)
+            for i in range(GROUP):
+                head = g * GROUP + i
+                exact = exact_ref[rows, (head // 2) * 128 : (head // 2 + 1) * 128]
+                if head % 2 != g % 2:
+                    exact = pltpu.roll(exact, HEAD, 1)
+                product = exact * g_s[g, i * BLK : (i + 1) * BLK, :].astype(F32)
+                delta_s[g : g + 1, i * BLK : (i + 1) * BLK] = jnp.sum(
+                    jnp.transpose(product), axis=0, keepdims=True
+                )
         query_block = order_ref[0, mine_ref[0] + qb]
         first = first_row_start(lengths_ref, query_block, parts)
 
@@ -206,7 +216,7 @@
                         scores = jnp.where(seen, scores, far_negative)
                         probs = jnp.exp(scores - lse_ref[qb, g : g + 1, :])
                         grad_probs = dot(values, g_s[g], ((1,), (1,)))
-                        grad_scores = (probs * (grad_probs - delta_ref[qb, g : g + 1, :])).astype(BF16)
+                        grad_scores = (probs * (grad_probs - delta_s[g : g + 1, :])).astype(BF16)
                         grad_values = grad_values + dot(probs.astype(BF16), g_s[g])
                         grad_keys = grad_keys + dot(grad_scores, q_s[g])
                         dq_s[g] += dot(grad_scores, keys, ((0,), (0,)))
@@ -231,7 +241,7 @@
         dkv_ref[key_rows, :] = dkv_s[key_rows, :].astype(BF16)
 
 
-def attend_back(lengths, order, mine, projected, kv, grad_attended, lse, delta):
+def attend_back(lengths, order, mine, projected, kv, grad_attended, lse, exact):
     rows = projected.shape[0]
     smem = pl.BlockSpec(memory_space=pltpu.SMEM)
     vmem = pl.BlockSpec(memory_space=pltpu.VMEM)
@@ -247,13 +257,14 @@
         scratch_shapes=[
             pltpu.VMEM((KV_HEADS, wide, 128), BF16),
             pltpu.VMEM((KV_HEADS, wide, 128), BF16),
+            pltpu.VMEM((KV_HEADS, wide), F32),
             pltpu.VMEM((KV_HEADS, wide, 128), F32),
             pltpu.VMEM(kv.shape, F32),
         ],
         compiler_params=pltpu.CompilerParams(vmem_limit_bytes=56 * 2**20),
-        cost_estimate=pl.CostEstimate(flops=3 * 10**10, bytes_accessed=10**7, transcendentals=10**7),
+        cost_estimate=pl.CostEstimate(flops=10**9, bytes_accessed=10**6, transcendentals=10**5),
         name="attend_back",
-    )(lengths, order, mine, projected, kv, grad_attended, lse, delta)
+    )(lengths, order, mine, projected, kv, grad_attended, lse, exact)
 
 
 MESH = pl.DeviceIdType.MESH
@@ -870,21 +881,123 @@
     )(rows, gates, grads, w_in, w_down)
 
 
-def collect_kernel(
+def add_rows(total, part, rows):
+    slab = 16
+
+    @pl.loop(0, rows // slab)
+    def _(i):
+        at = pl.ds(pl.multiple_of(i * slab, slab), slab)
+        total[at, :] = (total[at, :].astype(F32) + part[at, :].astype(F32)).astype(BF16)
+
+
+class Chain:
+    def __init__(self, layers, z, above, below, own, rows, up, down, sems, sends):
+        self.layers, self.z, self.above, self.below = layers, z, above, below
+        self.own, self.rows, self.up, self.down = own, rows, up, down
+        self.sems, self.sends = sems, sends
+
+    def rise(self, d):
+        return remote(self.own(d), self.up.at[d], self.sends.at[0, d], self.sems.at[0, d], self.above)
+
+    def fall(self, d):
+        return remote(self.own(d), self.down.at[d], self.sends.at[1, d], self.sems.at[1, d], self.below)
+
+    def ends(self):
+        for step in range(self.layers - 1):
+            pl.when(self.z == 0)(self.rise(self.layers - 1 - step).start)
+            pl.when(self.z == self.layers - 1)(self.fall(step).start)
+
+    def middle(self):
+        z, last = self.z, self.layers - 1
+
+        def pass_on(copy, d, buffer):
+            copy.wait_recv()
+            add_rows(self.own(d), buffer.at[d], self.rows)
+            copy.start()
+
+        def both(first_half):
+            for step in range(last):
+                high, low = last - step, step
+
+                def upward(high=high):
+                    pl.when((z > 0) & (z < high))(lambda: pass_on(self.rise(high), high, self.up))
+
+                def downward(low=low):
+                    pl.when((z < last) & (z > low))(lambda: pass_on(self.fall(low), low, self.down))
+
+                for turn in (upward, downward) if first_half else (downward, upward):
+                    turn()
+
+        pl.when(z <= last // 2)(lambda: both(True))
+        pl.when(z > last // 2)(lambda: both(False))
+
+    def finish(self):
+        z, last = self.z, self.layers - 1
+
+        @pl.when(z > 0)
+        def _():
+            self.rise(z).wait_recv()
+            add_rows(self.own(z), self.up.at[z], self.rows)
+
+        @pl.when(z < last)
+        def _():
+            self.fall(z).wait_recv()
+            add_rows(self.own(z), self.down.at[z], self.rows)
+
+    def wait_sends(self):
+        for d in range(self.layers):
+            pl.when(self.z < d)(self.rise(d).wait_send)
+            pl.when(self.z > d)(self.fall(d).wait_send)
+
+
+def finish_kernel(
     layers,
-    part_ref,
+    grad_kv_ref,
+    grad_q_ref,
+    first_ref,
+    tokens_ref,
+    gain_ref,
+    middle_ref,
+    w_all_ref,
+    attended_ref,
+    second_ref,
+    logits_ref,
+    gain_moe_ref,
     in_ref,
     down_ref,
-    out_ref,
+    d_tokens_ref,
+    d_qkv_ref,
+    d_late_ref,
+    d_aux_ref,
     got_in_ref,
     got_down_ref,
-    own,
-    pair,
-    near,
-    line,
+    weights,
+    projected,
+    grad_first,
+    kv_own,
+    kv_pair,
+    kv_up,
+    kv_down,
+    late_both,
+    late_pair,
+    late_near,
+    late_up,
+    late_down,
+    q_both,
+    q_pair,
+    q_near,
+    q_up,
+    q_down,
+    k_both,
+    k_pair,
+    k_near,
+    k_up,
+    k_down,
+    load_sem,
+    kv_sem,
+    kv_send,
     half_sem,
     half_send,
-    load_sem,
     pair_sem,
     pair_send,
     near_sem,
@@ -894,8 +1007,36 @@
 ):
     z, core, exp = lax.axis_index("le"), lax.axis_index("core"), lax.axis_index("exp")
     other = 1 - core
+    partner = place(z, other, exp)
+    above, below = place(z + 1, core, exp), place(z - 1, core, exp)
     x, y = x_of(exp), y_of(exp)
-    layer_mates = (x, y, y_of(x))
+    mates = (x, y, y_of(x))
+    ctx = z * 2 + core
+    rows = d_qkv_ref.shape[0]
+    count = tokens_ref.shape[0]
+    head_cols = HEADS * HEAD
+    qkv_cols = d_qkv_ref.shape[1]
+    kv_cols = qkv_cols - head_cols
+
+    loads = []
+
+    def load(src, dst):
+        copy = pltpu.make_async_copy(src, dst, load_sem.at[len(loads)])
+        copy.start()
+        loads.append(copy)
+        return copy
+
+    kv_loads = [
+        load(grad_kv_ref.at[pl.ds(pl.multiple_of((d * 2 + core) * count, 16), count), :], kv_own.at[d])
+        for d in range(layers)
+    ]
+    depth = w_all_ref.shape[0]
+
+    def weights_part(i):
+        part = w_all_ref.at[pl.ds(i * depth // 2, depth // 2), pl.ds(0, qkv_cols)]
+        return pltpu.make_async_copy(part, weights, load_sem.at[2 * layers + 2])
+
+    weights_part(0).start()
     meet(
         [
             place((z + s) % layers, (core + p) % 2, exp)
@@ -903,33 +1044,95 @@
             for p in range(2)
             if s + p > 0
         ]
-        + [place(z, core, mate) for mate in layer_mates]
+        + [place(z, core, mate) for mate in mates]
     )
-    rows = out_ref.shape[0]
-    ctx = z * 2 + core
     started = []
 
     def go(copy):
         copy.start()
         started.append(copy)
 
-    order = [(z + s) % layers for s in (2, 1, 3, 0)] if layers == 4 else [(z + s) % layers for s in range(layers)]
-    loads = []
-    for k, zz in enumerate(order):
+    for d in range(layers):
         go(
             remote(
-                part_ref.at[pl.ds((zz * 2 + other) * 4 * rows, 4 * rows), :],
-                pair.at[zz],
-                pair_send.at[k],
-                pair_sem.at[zz],
-                place(z, other, exp),
+                grad_kv_ref.at[pl.ds(pl.multiple_of((d * 2 + other) * count, 16), count), :],
+                kv_pair.at[d],
+                kv_send.at[2, d],
+                kv_sem.at[2, d],
+                partner,
             )
         )
-        load = pltpu.make_async_copy(
-            part_ref.at[pl.ds((zz * 2 + core) * 4 * rows, 4 * rows), :], own.at[zz], load_sem.at[k]
+    for d in range(layers):
+        kv_loads[d].wait()
+        remote(kv_pair.at[d], kv_pair.at[d], kv_send.at[2, d], kv_sem.at[2, d], partner).wait_recv()
+        add_rows(kv_own.at[d], kv_pair.at[d], count)
+    kv_line = Chain(
+        layers, z, above, below, lambda d: kv_own.at[d], count, kv_up, kv_down, kv_sem, kv_send
+    )
+    kv_line.ends()
+
+    def near_copy(i, near, own, d, m, target):
+        return remote(
+            own.at[d, pl.ds(pl.multiple_of(target * rows, 16), rows), :],
+            near.at[m, d],
+            near_send.at[i, m, d],
+            near_sem.at[i, m, d],
+            place(z, core, mates[m]),
         )
-        load.start()
-        loads.append(load)
+
+    def pair_sums(i, own, pair, near):
+        for d in range(layers):
+            remote(pair.at[d], pair.at[d], pair_send.at[i, d], pair_sem.at[i, d], partner).wait_recv()
+            add_rows(own.at[d], pair.at[d], 4 * rows)
+            for m in range(3):
+                go(near_copy(i, near, own, d, m, mates[m]))
+
+    def near_sums(i, own, near):
+        for d in range(layers):
+            for m in range(3):
+                near_copy(i, near, own, d, m, exp).wait_recv()
+            mine = own.at[d, pl.ds(pl.multiple_of(exp * rows, 16), rows), :]
+
+            @pl.loop(0, rows // 16)
+            def _(r, mine=mine, d=d):
+                at = pl.ds(pl.multiple_of(r * 16, 16), 16)
+                total = mine[at, :].astype(F32)
+                for m in range(3):
+                    total = total + near[m, d, at, :].astype(F32)
+                mine[at, :] = total.astype(BF16)
+
+    def line_of(i, own, up, down):
+        return Chain(
+            layers,
+            z,
+            above,
+            below,
+            lambda d: own.at[d, pl.ds(pl.multiple_of(exp * rows, 16), rows), :],
+            rows,
+            up,
+            down,
+            line_sem.at[i],
+            line_send.at[i],
+        )
+
+    def outer_product(both, cols, left, right, gains=None):
+        for d in range(layers):
+            block = left[:, d * 8 * rows : (d + 1) * 8 * rows]
+            part = dot(block, right, ((0,), (0,)))
+            if gains is not None:
+                turned = [
+                    jnp.transpose(jnp.broadcast_to(gains[:, at : at + 128], (128, 128)))
+                    for at in range(d * 8 * rows, (d + 1) * 8 * rows, 128)
+                ]
+                lane = lax.broadcasted_iota(jnp.int32, part.shape, 1)
+                part = jnp.where(lane == 0, jnp.concatenate(turned, axis=0), part)
+            part = part.astype(BF16)
+            both[0, d, :, cols] = part[: 4 * rows]
+            both[1, d, :, cols] = part[4 * rows :]
+
+    def pair_up(i, both, pair):
+        for d in range(layers):
+            go(remote(both.at[other, d], pair.at[d], pair_send.at[i, d], pair_sem.at[i, d], partner))
 
     arrays = ((in_ref, got_in_ref), (down_ref, got_down_ref))
 
@@ -941,13 +1144,11 @@
         cols = arrays[a][0].shape[1]
         return arrays[a][1].at[expert, :, pl.ds(pl.multiple_of(p * cols, 128), cols)]
 
-    keeps = []
     for a in range(2):
-        keep = pltpu.make_async_copy(mine(a, ctx), half(a, z, core), load_sem.at[layers + a])
-        keep.start()
-        keeps.append(keep)
-    for s in range(layers):
-        for p in range(2):
+        load(mine(a, ctx), half(a, z, core))
+
+    def hand_back(p):
+        for s in (2, 1, 3, 0) if layers == 4 else range(layers):
             if s + p == 0:
                 continue
             zz, pp = (z + s) % layers, (core + p) % 2
@@ -962,64 +1163,82 @@
                     )
                 )
 
-    slab = 16
-    for k, zz in enumerate(order):
-        loads[k].wait()
-        remote(pair.at[zz], pair.at[zz], pair_send.at[k], pair_sem.at[zz], place(z, other, exp)).wait_recv()
-
-        @pl.loop(0, 4 * rows // slab)
-        def _(i, zz=zz):
-            at = pl.ds(pl.multiple_of(i * slab, slab), slab)
-            own[zz, at, :] = (own[zz, at, :].astype(F32) + pair[zz, at, :].astype(F32)).astype(BF16)
-
-        for m, mate in enumerate(layer_mates):
-            go(
-                remote(
-                    own.at[zz, pl.ds(pl.multiple_of(mate * rows, slab), rows), :],
-                    near.at[m, zz],
-                    near_send.at[m, k],
-                    near_sem.at[m, zz],
-                    place(z, core, mate),
-                )
-            )
-
-    for k, zz in enumerate(order):
-        for m, mate in enumerate(layer_mates):
-            remote(
-                near.at[m, zz], near.at[m, zz], near_send.at[m, k], near_sem.at[m, zz], place(z, core, mate)
-            ).wait_recv()
-
-        @pl.loop(0, rows // slab)
-        def _(i, zz=zz):
-            at = pl.ds(pl.multiple_of(exp * rows + i * slab, slab), slab)
-            here = pl.ds(pl.multiple_of(i * slab, slab), slab)
-            total = own[zz, at, :].astype(F32)
-            for m in range(3):
-                total = total + near[m, zz, here, :].astype(F32)
-            own[zz, at, :] = total.astype(BF16)
-
-        if k < layers - 1:
-            go(
-                remote(
-                    own.at[zz, pl.ds(pl.multiple_of(exp * rows, slab), rows), :],
-                    line.at[z],
-                    line_send.at[k],
-                    line_sem.at[z],
-                    place(zz, core, exp),
-                )
-            )
-
-    for zz in order[:-1]:
-        remote(line.at[zz], line.at[zz], line_send.at[0], line_sem.at[zz], place(zz, core, exp)).wait_recv()
-
-    @pl.loop(0, rows // slab)
-    def _(i):
-        at = pl.ds(pl.multiple_of(exp * rows + i * slab, slab), slab)
-        here = pl.ds(pl.multiple_of(i * slab, slab), slab)
-        total = own[z, at, :].astype(F32)
-        for zz in order[:-1]:
-            total = total + line[zz, here, :].astype(F32)
-        out_ref[here, :] = total
+    outer_product(q_both, slice(0, head_cols), first_ref, grad_q_ref[...])
+    pair_up(1, q_both, q_pair)
+    width = middle_ref.shape[1]
+    outer_product(late_both, slice(0, width), attended_ref, middle_ref[...].astype(BF16))
+    outer_product(late_both, slice(width, width + AUX), second_ref, logits_ref[...], gain_moe_ref[...])
+    pair_up(0, late_both, late_pair)
+    late_own = late_both.at[core]
+    q_own = q_both.at[core]
+    pair_sums(1, q_own, q_pair, q_near)
+    pair_sums(0, late_own, late_pair, late_near)
+    kv_line.middle()
+    kv_line.finish()
+
+    hand_back(0)
+
+    projected[:, :head_cols] = grad_q_ref[...]
+    projected[:, head_cols:] = kv_own[z]
+    outer_product(k_both, slice(0, kv_cols), first_ref, projected[:, head_cols:])
+    tile = 256
+    for i in range(2):
+        weights_part(i).wait()
+
+        @pl.loop(0, depth // 2 // tile)
+        def _(j, i=i):
+            at = pl.ds(pl.multiple_of(j * tile, tile), tile)
+            to = pl.ds(pl.multiple_of(i * depth // 2 + j * tile, tile), tile)
+            grad_first[:, to] = dot(projected[...], weights[at, :], ((1,), (1,)))
+
+        if i == 0:
+            weights_part(1).start()
+
+    inputs = tokens_ref[...].astype(F32)
+    scale = norm_scale(inputs)
+    norm = inputs * scale
+    grad = grad_first[...]
+    grad_gain = jnp.sum(grad * norm, axis=0, keepdims=True)
+    for d in range(layers):
+        block = jnp.concatenate(
+            [
+                jnp.transpose(jnp.broadcast_to(grad_gain[:, at : at + 128], (128, 128)))
+                for at in range(d * 8 * rows, (d + 1) * 8 * rows, 128)
+            ],
+            axis=0,
+        ).astype(BF16)
+        k_both[0, d, :, kv_cols:] = block[: 4 * rows]
+        k_both[1, d, :, kv_cols:] = block[4 * rows :]
+    pair_up(2, k_both, k_pair)
+    grad = grad * gain_ref[...]
+    d_tokens_ref[...] = (
+        middle_ref[...] + scale * (grad - norm * jnp.mean(grad * norm, axis=-1, keepdims=True))
+    ).astype(BF16)
+    k_own = k_both.at[core]
+    pair_sums(2, k_own, k_pair, k_near)
+
+    late_line = line_of(0, late_own, late_up, late_down)
+    q_line = line_of(1, q_own, q_up, q_down)
+    k_line = line_of(2, k_own, k_up, k_down)
+    near_sums(1, q_own, q_near)
+    q_line.ends()
+    near_sums(0, late_own, late_near)
+    late_line.ends()
+    q_line.middle()
+    near_sums(2, k_own, k_near)
+    k_line.ends()
+    late_line.middle()
+    k_line.middle()
+    mine_rows = pl.ds(pl.multiple_of(exp * rows, 16), rows)
+    q_line.finish()
+    d_qkv_ref[:, :head_cols] = q_both[core, z, mine_rows, :].astype(F32)
+    late_line.finish()
+    d_late_ref[...] = late_both[core, z, mine_rows, :].astype(F32)
+    k_line.finish()
+    hand_back(1)
+    last = k_both[core, z, mine_rows, :].astype(F32)
+    d_qkv_ref[:, head_cols:] = last[:, :kv_cols]
+    d_aux_ref[...] = last[:, kv_cols:]
 
     for source in range(2 * layers):
         for a in range(2):
@@ -1031,49 +1250,103 @@
                     half(a, source // 2, source % 2),
                     half_send.at[a, 0],
                     half_sem.at[a, source],
-                    place(z, other, exp),
+                    partner,
                 ).wait_recv()
 
-    for keep in keeps:
-        keep.wait()
+    for copy in loads[-2:]:
+        copy.wait()
+    for line in (kv_line, late_line, q_line, k_line):
+        line.wait_sends()
     for copy in started:
         copy.wait_send()
 
 
-def collect(part, grad_in, grad_down, layers):
-    rows, cols = part.shape[0] // (8 * layers), part.shape[1]
+def finish(
+    grad_kv,
+    grad_q,
+    first,
+    tokens,
+    gain,
+    middle,
+    w_all,
+    attended,
+    second,
+    grad_logits,
+    gain_moe,
+    grad_in,
+    grad_down,
+    layers,
+):
+    depth, count = first.shape[1], first.shape[0]
+    rows = depth // (8 * layers)
+    qkv_cols = grad_q.shape[1] + grad_kv.shape[1]
     n_in, n_down = grad_in.shape[0] // (2 * layers), grad_down.shape[0] // (2 * layers)
     any_space = pl.BlockSpec(memory_space=pl.ANY)
+    vmem = pl.BlockSpec(memory_space=pltpu.VMEM)
     dma = pltpu.SemaphoreType.DMA
+
+    def sums(cols):
+        return [
+            pltpu.VMEM((2, layers, 4 * rows, cols), BF16),
+            pltpu.VMEM((layers, 4 * rows, cols), BF16),
+            pltpu.VMEM((3, layers, rows, cols), BF16),
+            pltpu.VMEM((layers, rows, cols), BF16),
+            pltpu.VMEM((layers, rows, cols), BF16),
+        ]
+
     return pl.pallas_call(
-        functools.partial(collect_kernel, layers),
+        functools.partial(finish_kernel, layers),
         out_shape=(
-            jax.ShapeDtypeStruct((rows, cols), F32),
+            jax.ShapeDtypeStruct((count, depth), BF16),
+            jax.ShapeDtypeStruct((rows, qkv_cols), F32),
+            jax.ShapeDtypeStruct((rows, depth + AUX), F32),
+            jax.ShapeDtypeStruct((rows, AUX), F32),
             jax.ShapeDtypeStruct((layers, n_in, 2 * grad_in.shape[1]), BF16),
             jax.ShapeDtypeStruct((layers, n_down, 2 * grad_down.shape[1]), BF16),
         ),
-        in_specs=[any_space] * 3,
-        out_specs=(pl.BlockSpec(memory_space=pltpu.VMEM), any_space, any_space),
+        in_specs=[any_space] + [vmem] * 5 + [any_space] + [vmem] * 4 + [any_space] * 2,
+        out_specs=(vmem,) * 4 + (any_space,) * 2,
         scratch_shapes=[
-            pltpu.VMEM((layers, 4 * rows, cols), BF16),
-            pltpu.VMEM((layers, 4 * rows, cols), BF16),
-            pltpu.VMEM((3, layers, rows, cols), BF16),
-            pltpu.VMEM((layers, rows, cols), BF16),
+            pltpu.VMEM((depth // 2, qkv_cols), BF16),
+            pltpu.VMEM((count, qkv_cols), BF16),
+            pltpu.VMEM((count, depth), F32),
+        ]
+        + [pltpu.VMEM((layers, count, grad_kv.shape[1]), BF16)] * 4
+        + sums(depth + AUX)
+        + sums(grad_q.shape[1])
+        + sums(grad_kv.shape[1] + AUX)
+        + [
+            dma((2 * layers + 3,)),
+            dma((3, layers)),
+            dma((3, layers)),
             dma((2, 2 * layers)),
             dma((2, 2 * layers)),
-            dma((layers + 2,)),
-            dma((layers,)),
-            dma((layers,)),
             dma((3, layers)),
             dma((3, layers)),
-            dma((layers,)),
-            dma((layers,)),
+            dma((3, 3, layers)),
+            dma((3, 3, layers)),
+            dma((3, 2, layers)),
+            dma((3, 2, layers)),
         ],
         compiler_params=pltpu.CompilerParams(
-            collective_id=1, has_side_effects=True, vmem_limit_bytes=40 * 2**20
+            collective_id=1, has_side_effects=True, vmem_limit_bytes=60 * 2**20
         ),
-        name="collect",
-    )(part, grad_in, grad_down)
+        name="finish",
+    )(
+        grad_kv,
+        grad_q,
+        first,
+        tokens,
+        gain,
+        middle,
+        w_all,
+        attended,
+        second,
+        grad_logits,
+        gain_moe,
+        grad_in,
+        grad_down,
+    )
 
 
 CTX = ("le", "rep", "core")
@@ -1165,7 +1438,6 @@
     grad_y_rows = to_experts(grad_y_send)
     mine = (lax.axis_index(CTX) * (tok_rows // BLK)).astype(jnp.int32).reshape(1)
     exact, attended, lse = attend(lengths, block_order, mine, projected, kv)
-    attended, grad_y_rows = lax.optimization_barrier((attended, grad_y_rows))
     middle = inputs + dot(attended, w_attn_out)
     scale_second = norm_scale(middle)
     norm_second = middle * scale_second
@@ -1257,7 +1529,6 @@
     )
     grad_chosen = gates * (grad_gates - jnp.sum(gates * grad_gates, axis=-1, keepdims=True))
     grad_logits = jnp.sum(grad_chosen[:, :, None] * route_hot, axis=1).astype(BF16)
-    grad_router = dot(second, grad_logits, ((0,), (0,)))
     grad_second = dot(pick_hot[0] + pick_hot[1], grad_returned) + dot(
         grad_logits, w_router, ((1,), (1,))
     )
@@ -1268,42 +1539,51 @@
         - norm_second * jnp.mean(grad_norm_second * norm_second, axis=-1, keepdims=True)
     )
     grad_branch = grad_middle.astype(BF16)
-    grad_attn_out = dot(attended, grad_branch, ((0,), (0,)))
-    late = jnp.concatenate([grad_gain_second[:, None], grad_router], axis=1)
-    late = jnp.pad(late, ((0, 0), (0, AUX - late.shape[1])))
     grad_attended = dot(grad_branch, w_attn_out, ((1,), (1,))).astype(BF16)
-    delta = jnp.sum(
-        (grad_attended.astype(F32) * exact).reshape(tok_rows, HEADS, HEAD), axis=-1
-    )
-    delta = (
-        delta.reshape(tok_rows // BLK, BLK, KV_HEADS, GROUP)
-        .transpose(0, 2, 3, 1)
-        .reshape(lse.shape)
-    )
     grad_queries, grad_kv = attend_back(
-        lengths, block_order, mine, projected, kv, grad_attended, lse, delta
+        lengths, block_order, mine, projected, kv, grad_attended, lse, exact
     )
     grad_queries, grad_kv, returned = lax.optimization_barrier((grad_queries, grad_kv, returned))
     picked = [dot(p, returned) for p in pick_hot]
     block_out = (middle + gates[:, 0:1] * picked[0] + gates[:, 1:2] * picked[1]).astype(BF16)
-    grad_kv = lax.psum_scatter(grad_kv, CTX, scatter_dimension=0, tiled=True)
-    grad_projected = jnp.concatenate([grad_queries, grad_kv], axis=1)
-    grad_qkv = dot(first, grad_projected, ((0,), (0,)))
-    grad_first = dot(grad_projected, w_qkv, ((1,), (1,)))
-    grad_gain_first = jnp.sum(grad_first * norm_first, axis=0)
-    grad_norm_first = grad_first * gain_first
-    grad_inputs = grad_middle + scale_first * (
-        grad_norm_first
-        - norm_first * jnp.mean(grad_norm_first * norm_first, axis=-1, keepdims=True)
-    )
-    last = jnp.pad(grad_gain_first[:, None], ((0, 0), (0, AUX - 1)))
-    part = jnp.concatenate(
-        [grad_qkv.astype(BF16), last.astype(BF16), grad_attn_out.astype(BF16), late.astype(BF16)], axis=1
-    )
     if special:
-        total, sum_in, sum_down = collect(part, grad_in, grad_down, exp_local)
+        grad_inputs, sum_qkv, sum_late, sum_aux, sum_in, sum_down = finish(
+            grad_kv,
+            grad_queries,
+            first,
+            tokens[0],
+            gain_first[None, :],
+            grad_middle,
+            w_all,
+            attended,
+            second,
+            jnp.pad(grad_logits, ((0, 0), (1, AUX - 1 - EXPERTS))),
+            grad_gain_second[None, :],
+            grad_in,
+            grad_down,
+            exp_local,
+        )
     else:
+        grad_router = dot(second, grad_logits, ((0,), (0,)))
+        grad_attn_out = dot(attended, grad_branch, ((0,), (0,)))
+        late = jnp.concatenate([grad_gain_second[:, None], grad_router], axis=1)
+        late = jnp.pad(late, ((0, 0), (0, AUX - late.shape[1])))
+        late = jnp.concatenate([grad_attn_out.astype(BF16), late.astype(BF16)], axis=1)
+        grad_kv = lax.psum_scatter(grad_kv, CTX, scatter_dimension=0, tiled=True)
+        grad_projected = jnp.concatenate([grad_queries, grad_kv], axis=1)
+        grad_qkv = dot(first, grad_projected, ((0,), (0,)))
+        grad_first = dot(grad_projected, w_qkv, ((1,), (1,)))
+        grad_gain_first = jnp.sum(grad_first * norm_first, axis=0)
+        grad_norm_first = grad_first * gain_first
+        grad_inputs = grad_middle + scale_first * (
+            grad_norm_first
+            - norm_first * jnp.mean(grad_norm_first * norm_first, axis=-1, keepdims=True)
+        )
+        grad_inputs = grad_inputs.astype(BF16)
+        last = jnp.pad(grad_gain_first[:, None], ((0, 0), (0, AUX - 1)))
+        part = jnp.concatenate([grad_qkv.astype(BF16), last.astype(BF16), late], axis=1)
         total = lax.psum_scatter(part, ALL, scatter_dimension=0, tiled=True).astype(F32)
+        sum_qkv, sum_aux, sum_late = total[:, :cols], total[:, cols : cols + AUX], total[:, cols + AUX :]
 
         def to_rows(half, rows):
             width = half.shape[1]
@@ -1315,15 +1595,14 @@
 
         sum_in = to_rows(grad_in, in_rows)
         sum_down = to_rows(grad_down, out_rows)
-    sum_second = total[:, cols + AUX :]
     return (
         block_out[None],
-        grad_inputs.astype(BF16)[None],
-        total[:, cols],
-        total[:, :cols],
-        sum_second[:, :D],
-        sum_second[:, D],
-        sum_second[:, D + 1 : D + 1 + EXPERTS],
+        grad_inputs[None],
+        sum_aux[:, 0],
+        sum_qkv,
+        sum_late[:, :D],
+        sum_late[:, D],
+        sum_late[:, D + 1 : D + 1 + EXPERTS],
         sum_in.astype(F32),
         sum_down.astype(F32),
     )

time: 688 us -> 643 us (0.935)
  waiting for transfers between devices: 64.9 us -> 35.4 us
  Pallas kernels: 482 us -> 504 us
  matrix products: 44.2 us -> 26.8 us
  between operations: 15 us -> 1.48 us
  other arithmetic: 19.7 us -> 10.9 us
    pallas_call x1, Pallas kernels: 145 us -> 179 us  [finish(): pl.pallas_call(functools.partial(finish_kernel, layers), out_shape=(jax.S...]
    reduce_scatter x1 -> x0, waiting for transfers between devices: 32.4 us -> none  [on_device(): grad_kv = lax.psum_scatter(grad_kv, CTX, scatter_dimension=0, tiled=True)]
    dot_general x14 -> x10, matrix products: 44.2 us -> 26.8 us  [dot(): return lax.dot_general(a, b, (dims, ((), ())), preferred_element_type=F32)]
  transfers between devices with their start and end apart: 3 -> 2, of which waited for: 3 -> 2; matrix products, arithmetic and copies ran while one was open for 4% -> 4% of each run, Pallas kernels for 8% -> 7%
where the time goes in v4:
time: 643 us; the launch traced here: 632 us
  Pallas kernels  504 us (78%)
  starting transfers between devices  39.2 us (6%)
  waiting for transfers between devices  35.4 us (6%)
  matrix products  26.8 us (4%)
  local copies, waits for them, and re-layouts  14.2 us (2%)
  other arithmetic  10.9 us (2%)
    pallas_call x1, Pallas kernels, finish(): pl.pallas_call(functools.partial(finish_kernel, layers), out_shape=(jax.S...  179 us
    pallas_call x1, Pallas kernels, front(): pl.pallas_call(functools.partial(front_kernel, layers), out_shape=(jax.Sh...  163 us
    pallas_call x1, Pallas kernels, experts(): pl.pallas_call(functools.partial(experts_kernel, layers), out_shape=(jax....  118 us
    all_to_all x2, starting transfers between devices, to_experts(): lax.all_to_all(rows.reshape((EXPERTS, CAP) + rows.shape[1:]), OWNERS, spl...  39.2 us
    all_to_all x2, waiting for transfers between devices, to_experts(): lax.all_to_all(rows.reshape((EXPERTS, CAP) + rows.shape[1:]), OWNERS, spl...  35.4 us
    dot_general x10, matrix products, dot(): return lax.dot_general(a, b, (dims, ((), ())), preferred_element_type=F32)  26.8 us
    pallas_call x1, Pallas kernels, attend_back(): pl.pallas_call(functools.partial(attend_back_kernel, lengths.shape[1]), o...  24.3 us
    pallas_call x1, Pallas kernels, attend(): pl.pallas_call(functools.partial(attend_kernel, lengths.shape[1]), out_sh...  19.1 us
  transfers between devices with their start and end apart: 2, of which 2 were waited for; matrix products, arithmetic and copies ran while one was open for 4% of the time, Pallas kernels for 7%

profile of v4, /device:TPU:8, one launch (start us, length us, event | category | flops | bytes accessed | tf_op | source)
XLA Modules:
  0.0 632.0 jit_solution(13935520692985463480)
XLA Ops:
  0.7 0.7 convert_bitcast_fusion.1
  3.1 0.8 copy.54
  5.2 2.2 convolution_convert_fusion.1
  7.4 163.5 %front.1 = (bf16[1536,4224]{1,0:T(8,128)(2,1)}, bf16[1536,2048]{1,0:T(8,128)(2,1)}, bf16[1024,1536]{1,0:T(8,128)(2,1)}, bf16[256,1536]{1,0:T(8,128)(2,1)S(1)}, b...) custom-call(bf16[48,4224]{1,0:T(8,128)(2,1)S(1)} %pad_maximum_fusion.shard_ref, f32[4,192,2048]{2,1,0:T(8,128)} %in_ref.1, ...), custom_call_target="tpu_custom_call" | custom-call | tf_op jit(solution)/shard_map/front/pallas_call | solution.py:584
  170.9 0.9 copy-done.3
  171.8 15.0 %all-to-all-start = ((bf16[16,48,1536]{2,1,0:T(8,128)(2,1)}), bf16[16,48,1536]{2,1,0:T(8,128)(2,1)}, u32[]{:S(2)}, u32[]{:S(2)}) async-start(bf16[16,48,1536]{2,1,0:T(8,128)(2,1)} %bitcast.36), calls=%async_computation | async-start | bytes 4718592 | tf_op jit(solution)/shard_map/all_to_all | solution.py:1422
  186.9 1.6 convert_reduce_fusion
  188.5 19.1 %attend.1 = (f32[256,1536]{1,0:T(8,128)S(1)}, bf16[256,1536]{1,0:T(8,128)(2,1)S(1)}, f32[2,8,384]{2,1,0:T(8,128)S(1)}) custom-call(s32[1,3]{1,0:T(1,128)S(1)} %copy-done.6, s32[1,16]{1,0:T(1,128)S(1)} %copy-done.7, s32[1]{0:T(128)} %bitcast.1.mine_ref, bf16[256,2560]{1,0:T(8,128)(2,1)S(1)} %get-tuple-element.36.q_ref, ...), custom_call_target="tpu_custom_call" | custom-call | flops 10000000000 | bytes 10000000 | tf_op jit(solution)/shard_map/attend/pallas_call | solution.py:137
  207.6 4.7 multiply_reduce_fusion.2
  212.5 1.8 fusion.35
  214.8 2.2 convolution_convert_fusion
  217.0 21.6 %all-to-all-done.grads_ref = bf16[16,48,1536]{2,1,0:T(8,128)(2,1)} async-done(((bf16[16,48,1536]{2,1,0:T(8,128)(2,1)}), bf16[16,48,1536]{2,1,0:T(8,128)(2,1)}, u32[]{:S(2)}, u32[]{:S(2)}) %all-to-all-start) | async-done | bytes 2359328 | tf_op jit(solution)/shard_map/all_to_all | solution.py:1422
  239.3 118.5 %experts.1 = (bf16[16,48,1536]{2,1,0:T(8,128)(2,1)}, bf16[16,48,1536]{2,1,0:T(8,128)(2,1)}, f32[16,8,128]{2,1,0:T(8,128)}, bf16[1536,1024]{1,0:T(8,128)(2,1)}, bf16[1024,768]{1,0:T(8,128)(2,1)}) custom-call(bf16[16,48,1536]{2,1,0:T(8,128)(2,1)} %bitcast.35, f32[16,8,128]{2,1,0:T(8,128)} %broadcast_in_dim.88.gates_ref, ...), custom_call_target="tpu_custom_call" | custom-call | tf_op jit(solution)/shard_map/experts/pallas_call | solution.py:848
  357.7 24.2 %all-to-all-start.1 = ((bf16[16,48,1536]{2,1,0:T(8,128)(2,1)}), bf16[16,48,1536]{2,1,0:T(8,128)(2,1)}, u32[]{:S(2)}, u32[]{:S(2)}) async-start(bf16[16,48,1536]{2,1,0:T(8,128)(2,1)} %get-tuple-element.50), calls=%async_computation.1 | async-start | bytes 4718592 | tf_op jit(solution)/shard_map/all_to_all | solution.py:1422
  382.6 0.9 slice_reduce_fusion.4
  384.0 0.7 pad.15.logits_ref
  384.7 2.6 fusion.23
  387.4 1.9 multiply_reduce_fusion
  390.3 5.2 fusion.10.grad_ref
  395.6 24.3 %attend_back.1 = (bf16[256,1536]{1,0:T(8,128)(2,1)}, bf16[2048,1024]{1,0:T(8,128)(2,1)}) custom-call(s32[1,3]{1,0:T(1,128)} %lengths_ref.3, s32[1,16]{1,0:T(1,128)} %order_ref.3, s32[1]{0:T(128)} %bitcast.1.mine_ref, bf16[256,2560]{1,0:T(8,128)(2,1)} %copy-done.2, bf16[2048,1024]{1,0:T(8,128)(2,1)} %get-tuple-element.38.kv_ref, ...), custom_call_target="tpu_custom_call" | custom-call | flops 1000000000 | bytes 1000000 | tf_op jit(solution)/shard_map/attend_back/pallas_call | solution.py:249
  419.8 13.8 %all-to-all-done.1 = bf16[16,48,1536]{2,1,0:T(8,128)(2,1)} async-done(((bf16[16,48,1536]{2,1,0:T(8,128)(2,1)}), bf16[16,48,1536]{2,1,0:T(8,128)(2,1)}, u32[]{:S(2)}, u32[]{:S(2)}) %all-to-all-start.1) | async-done | bytes 2359328 | tf_op jit(solution)/shard_map/all_to_all | solution.py:1422
  433.6 178.6 %finish.1 = (bf16[256,1536]{1,0:T(8,128)(2,1)}, f32[48,2560]{1,0:T(8,128)}, f32[48,1664]{1,0:T(8,128)}, f32[48,128]{1,0:T(8,128)}, bf16[4,192,2048]{2,1,0:T(8,128)(2,1)}, /*index=5*/bf16[4,128,1536]{2,1,0:T(8,128)(2,1)}) custom-call(bf16[2048,1024]{1,0:T(8,128)(2,1)} %get-tuple-element.52.grad_kv_ref, bf16[256,1536]{1,0:T(8,128)(2,1)} %get-tuple-element.53.grad_q_ref, ...), custom_call_target="tpu_custom_call" | custom-call | tf_op jit(solution)/shard_map/finish/pallas_call | solution.py:1297
  612.2 0.8 slice.59
  613.0 1.7 slice.57
  614.7 2.5 fusion.5
  617.3 3.5 fusion.13
  620.8 1.4 slice_reduce_fusion.2
  622.9 2.1 convert_element_type.109
  624.9 1.0 copy-done.14
  625.9 3.6 convert_element_type.108
  629.4 0.9 copy.61
  630.8 0.8 copy.62
  (78 shorter events, 7.7 us)
Async XLA Ops:
  0.6 4.0 copy-start.19
  0.7 4.1 copy-start.17
  4.0 1.1 copy-start.12
  5.2 2.2 copy-start
  170.8 0.9 copy-start.3
  171.7 16.7 %copy-start.2 = (bf16[256,2560]{1,0:T(8,128)(2,1)}, bf16[256,2560]{1,0:T(8,128)(2,1)S(1)}, u32[]{:S(2)}) copy-start(bf16[256,2560]{1,0:T(8,128)(2,1)S(1)} %get-tuple-element.36.q_ref) | copy-start | bytes 3932164
  171.8 16.7 %copy-start.6 = (s32[1,3]{1,0:T(1,128)S(1)}, s32[1,3]{1,0:T(1,128)}, u32[]{:S(2)}) copy-start(s32[1,3]{1,0:T(1,128)} %lengths_ref.3) | copy-start | bytes 40
  171.8 16.7 %copy-start.7 = (s32[1,16]{1,0:T(1,128)S(1)}, s32[1,16]{1,0:T(1,128)}, u32[]{:S(2)}) copy-start(s32[1,16]{1,0:T(1,128)} %order_ref.3) | copy-start | bytes 196
  171.8 66.9 %all-to-all-start = ((bf16[16,48,1536]{2,1,0:T(8,128)(2,1)}), bf16[16,48,1536]{2,1,0:T(8,128)(2,1)}, u32[]{:S(2)}, u32[]{:S(2)}) async-start(bf16[16,48,1536]{2,1,0:T(8,128)(2,1)} %bitcast.36), calls=%async_computation | async-start | bytes 4718592 | tf_op jit(solution)/shard_map/all_to_all | solution.py:1422
  207.6 4.7 copy-start.1
  207.6 4.7 copy-start.4
  207.6 4.7 copy-start.5
  212.3 2.0 copy-start.8
  212.5 4.5 copy-start.10
  357.7 75.9 %all-to-all-start.1 = ((bf16[16,48,1536]{2,1,0:T(8,128)(2,1)}), bf16[16,48,1536]{2,1,0:T(8,128)(2,1)}, u32[]{:S(2)}, u32[]{:S(2)}) async-start(bf16[16,48,1536]{2,1,0:T(8,128)(2,1)} %get-tuple-element.50), calls=%async_computation.1 | async-start | bytes 4718592 | tf_op jit(solution)/shard_map/all_to_all | solution.py:1422
  384.7 2.6 copy-start.9
  387.4 2.5 copy-start.13
  390.3 5.2 copy-start.11
  617.3 3.6 copy-start.20
  617.3 5.6 copy-start.15
  622.9 3.0 copy-start.14
  625.9 3.6 copy-start.16
  629.4 1.3 copy-start.18

commit v5 on v4

--- a/solution.py
+++ b/solution.py
@@ -291,6 +291,11 @@
         device_id=device,
         device_id_type=MESH,
     )
+
+
+def between(z, layers, offset):
+    low = layers // 2 - 1
+    return ((z == low) & (offset == 1)) | ((z == low + 1) & (offset == layers - 1))
 
 
 def meet(devices):
@@ -337,7 +342,8 @@
     x, y = x_of(exp), y_of(exp)
     ctx = z * 2 + core
     rows = shard_ref.shape[0]
-    order = [(z + s) % layers for s in ((2, 1, 3, 0) if layers == 4 else range(layers))]
+    offsets = (2, 1, 3, 0)
+    order = [(z + s) % layers for s in offsets]
     wides = ((in_ref, in_wide), (down_ref, down_wide))
     halves = ((in_half, w_in_ref), (down_half, w_down_ref))
 
@@ -411,6 +417,36 @@
     def layer(k):
         return jnp.where(z < layers // 2, k, layers - 1 - k)
 
+    def hand_out(a, early):
+        for s, zz in enumerate(order):
+            across = between(z, layers, offsets[s])
+            for p in range(2):
+                if offsets[s] + p == 0:
+                    continue
+                pp = (core + p) % 2
+                copy = remote(
+                    mine(a, zz, pp),
+                    half(a, ctx, pp),
+                    half_send.at[a, s * 2 + p],
+                    half_sem.at[a, ctx],
+                    place(zz, pp, exp),
+                )
+                if early:
+                    pl.when(across)(copy.start)
+                else:
+                    pl.when(~across)(copy.start)
+                    started.append((copy, None))
+        if not early:
+            go(
+                remote(
+                    mine(a, z, core),
+                    half(a, ctx, core),
+                    over_send.at[a, 2 * layers],
+                    over_sem.at[a, ctx],
+                    place(z, other, exp),
+                )
+            )
+
     for k in range(layers):
         zz = layer(k)
         who = (zz, core, exp)
@@ -424,36 +460,13 @@
         go(send(unit(*who), who, x_sem.at[k], place(z, core, x)), zz != z)
         go(send(unit(*who), who, y_sem.at[k], place(z, core, y)), zz != z)
         go(send(unit(*who), who, core_sem.at[k], place(z, other, exp)), zz != z)
+        if k == 0:
+            hand_out(0, True)
 
     for a in range(2):
         pltpu.make_async_copy(mine(a, z, core), half(a, ctx, core), own_sem.at[1 + a]).start()
 
-    def hand_out(a):
-        for s, zz in enumerate(order):
-            for p in range(2):
-                if s == layers - 1 and p == 0:
-                    continue
-                pp = (core + p) % 2
-                go(
-                    remote(
-                        mine(a, zz, pp),
-                        half(a, ctx, pp),
-                        half_send.at[a, s * 2 + p],
-                        half_sem.at[a, ctx],
-                        place(zz, pp, exp),
-                    )
-                )
-        go(
-            remote(
-                mine(a, z, core),
-                half(a, ctx, core),
-                over_send.at[a, 2 * layers],
-                over_sem.at[a, ctx],
-                place(z, other, exp),
-            )
-        )
-
-    hand_out(0)
+    hand_out(0, False)
 
     for k in range(layers):
         zz = layer(k)
@@ -525,7 +538,8 @@
         go(share(block(source), source, kv_send.at[k], place(z - 1, core, exp)), (zz > z) & (z > 0))
         go(share(block(source), source, kv_send.at[layers + k], place(z, other, exp)), zz != z)
         if k == layers // 2:
-            hand_out(1)
+            hand_out(1, True)
+            hand_out(1, False)
 
     for s, zz in enumerate(order[::-1]):
         for p in range(2):
@@ -671,10 +685,16 @@
     ]
     for load in loads:
         load.start()
-    order = [(z + s) % layers for s in ((2, 1, 3, 0) if layers == 4 else range(layers))]
+    first_half = z < layers // 2
+    by_distance = [
+        z,
+        z + 1 - 2 * (z % 2),
+        jnp.where(first_half, 2, 1),
+        jnp.where(first_half, 3, 0),
+    ]
     peers = [
         (zz, (exp + t) % columns)
-        for s, zz in enumerate(order)
+        for s, zz in enumerate(by_distance[::-1])
         for t in range(columns)
         if not (s == layers - 1 and t == 0)
     ]
@@ -705,7 +725,7 @@
     def tiles(i):
         return pl.ds(pl.multiple_of(i * tile, tile), tile)
 
-    for k, zz in enumerate(order[::-1]):
+    for k, zz in enumerate(by_distance):
         rows = pl.ds(k * chunk, chunk)
         for ee in range(columns):
             source = ee * layers + zz
@@ -895,35 +915,61 @@
         self.layers, self.z, self.above, self.below = layers, z, above, below
         self.own, self.rows, self.up, self.down = own, rows, up, down
         self.sems, self.sends = sems, sends
-
-    def rise(self, d):
-        return remote(self.own(d), self.up.at[d], self.sends.at[0, d], self.sems.at[0, d], self.above)
-
-    def fall(self, d):
-        return remote(self.own(d), self.down.at[d], self.sends.at[1, d], self.sems.at[1, d], self.below)
+        self.parts = sems.shape[2]
+        self.width = up.shape[2] // self.parts
+
+    def columns(self, ref, h):
+        return ref.at[:, pl.ds(h * self.width, self.width)]
+
+    def rise(self, d, h):
+        return remote(
+            self.columns(self.own(d), h),
+            self.columns(self.up.at[d], h),
+            self.sends.at[0, d, h],
+            self.sems.at[0, d, h],
+            self.above,
+        )
+
+    def fall(self, d, h):
+        return remote(
+            self.columns(self.own(d), h),
+            self.columns(self.down.at[d], h),
+            self.sends.at[1, d, h],
+            self.sems.at[1, d, h],
+            self.below,
+        )
+
+    def end(self, step):
+        for h in range(self.parts):
+            pl.when(self.z == 0)(self.rise(self.layers - 1 - step, h).start)
+            pl.when(self.z == self.layers - 1)(self.fall(step, h).start)
 
     def ends(self):
         for step in range(self.layers - 1):
-            pl.when(self.z == 0)(self.rise(self.layers - 1 - step).start)
-            pl.when(self.z == self.layers - 1)(self.fall(step).start)
+            self.end(step)
+
+    def add(self, d, h, buffer):
+        add_rows(self.columns(self.own(d), h), self.columns(buffer.at[d], h), self.rows)
 
     def middle(self):
         z, last = self.z, self.layers - 1
 
-        def pass_on(copy, d, buffer):
-            copy.wait_recv()
-            add_rows(self.own(d), buffer.at[d], self.rows)
-            copy.start()
+        def pass_on(make, d, buffer):
+            for h in range(self.parts):
+                copy = make(d, h)
+                copy.wait_recv()
+                self.add(d, h, buffer)
+                copy.start()
 
         def both(first_half):
             for step in range(last):
                 high, low = last - step, step
 
                 def upward(high=high):
-                    pl.when((z > 0) & (z < high))(lambda: pass_on(self.rise(high), high, self.up))
+                    pl.when((z > 0) & (z < high))(lambda: pass_on(self.rise, high, self.up))
 
                 def downward(low=low):
-                    pl.when((z < last) & (z > low))(lambda: pass_on(self.fall(low), low, self.down))
+                    pl.when((z < last) & (z > low))(lambda: pass_on(self.fall, low, self.down))
 
                 for turn in (upward, downward) if first_half else (downward, upward):
                     turn()
@@ -934,20 +980,19 @@
     def finish(self):
         z, last = self.z, self.layers - 1
 
-        @pl.when(z > 0)
-        def _():
-            self.rise(z).wait_recv()
-            add_rows(self.own(z), self.up.at[z], self.rows)
-
-        @pl.when(z < last)
-        def _():
-            self.fall(z).wait_recv()
-            add_rows(self.own(z), self.down.at[z], self.rows)
+        def take(make, buffer):
+            for h in range(self.parts):
+                make(z, h).wait_recv()
+                self.add(z, h, buffer)
+
+        pl.when(z > 0)(lambda: take(self.rise, self.up))
+        pl.when(z < last)(lambda: take(self.fall, self.down))
 
     def wait_sends(self):
         for d in range(self.layers):
-            pl.when(self.z < d)(self.rise(d).wait_send)
-            pl.when(self.z > d)(self.fall(d).wait_send)
+            for h in range(self.parts):
+                pl.when(self.z < d)(self.rise(d, h).wait_send)
+                pl.when(self.z > d)(self.fall(d, h).wait_send)
 
 
 def finish_kernel(
@@ -963,11 +1008,16 @@
     second_ref,
     logits_ref,
     gain_moe_ref,
+    base_ref,
+    returned_ref,
+    picks_ref,
+    gates_ref,
     in_ref,
     down_ref,
+    block_ref,
     d_tokens_ref,
     d_qkv_ref,
-    d_late_ref,
+    d_out_ref,
     d_aux_ref,
     got_in_ref,
     got_down_ref,
@@ -994,6 +1044,8 @@
     k_up,
     k_down,
     load_sem,
+    kv_pair_sem,
+    kv_pair_send,
     kv_sem,
     kv_send,
     half_sem,
@@ -1052,24 +1104,62 @@
         copy.start()
         started.append(copy)
 
+    arrays = ((in_ref, got_in_ref), (down_ref, got_down_ref))
+
+    def mine(a, owner):
+        n = arrays[a][1].shape[1]
+        return arrays[a][0].at[pl.ds(owner * n, n), :]
+
+    def half(a, expert, p):
+        cols = arrays[a][0].shape[1]
+        return arrays[a][1].at[expert, :, pl.ds(pl.multiple_of(p * cols, 128), cols)]
+
+    for a in range(2):
+        load(mine(a, ctx), half(a, z, core))
+
+    def hand_back(a, early):
+        for s in (2, 1, 3, 0):
+            across = between(z, layers, s)
+            for p in range(2):
+                if s + p == 0:
+                    continue
+                zz, pp = (z + s) % layers, (core + p) % 2
+                copy = remote(
+                    mine(a, zz * 2 + pp),
+                    half(a, z, core),
+                    half_send.at[a, s * 2 + p],
+                    half_sem.at[a, ctx],
+                    place(zz, pp, exp),
+                )
+                if early:
+                    pl.when(across)(copy.start)
+                else:
+                    pl.when(~across)(copy.start)
+                    started.append(copy)
+
+    hand_back(0, True)
+
     for d in range(layers):
         go(
             remote(
                 grad_kv_ref.at[pl.ds(pl.multiple_of((d * 2 + other) * count, 16), count), :],
                 kv_pair.at[d],
-                kv_send.at[2, d],
-                kv_sem.at[2, d],
+                kv_pair_send.at[d],
+                kv_pair_sem.at[d],
                 partner,
             )
         )
-    for d in range(layers):
-        kv_loads[d].wait()
-        remote(kv_pair.at[d], kv_pair.at[d], kv_send.at[2, d], kv_sem.at[2, d], partner).wait_recv()
-        add_rows(kv_own.at[d], kv_pair.at[d], count)
     kv_line = Chain(
         layers, z, above, below, lambda d: kv_own.at[d], count, kv_up, kv_down, kv_sem, kv_send
     )
-    kv_line.ends()
+    for copy in kv_loads:
+        copy.wait()
+    for k in range(layers):
+        d = jnp.where(z < layers // 2, layers - 1 - k, k)
+        remote(kv_pair.at[d], kv_pair.at[d], kv_pair_send.at[d], kv_pair_sem.at[d], partner).wait_recv()
+        add_rows(kv_own.at[d], kv_pair.at[d], count)
+        if k < layers - 1:
+            kv_line.end(k)
 
     def near_copy(i, near, own, d, m, target):
         return remote(
@@ -1134,35 +1224,6 @@
         for d in range(layers):
             go(remote(both.at[other, d], pair.at[d], pair_send.at[i, d], pair_sem.at[i, d], partner))
 
-    arrays = ((in_ref, got_in_ref), (down_ref, got_down_ref))
-
-    def mine(a, owner):
-        n = arrays[a][1].shape[1]
-        return arrays[a][0].at[pl.ds(owner * n, n), :]
-
-    def half(a, expert, p):
-        cols = arrays[a][0].shape[1]
-        return arrays[a][1].at[expert, :, pl.ds(pl.multiple_of(p * cols, 128), cols)]
-
-    for a in range(2):
-        load(mine(a, ctx), half(a, z, core))
-
-    def hand_back(p):
-        for s in (2, 1, 3, 0) if layers == 4 else range(layers):
-            if s + p == 0:
-                continue
-            zz, pp = (z + s) % layers, (core + p) % 2
-            for a in range(2):
-                go(
-                    remote(
-                        mine(a, zz * 2 + pp),
-                        half(a, z, core),
-                        half_send.at[a, s * 2 + p],
-                        half_sem.at[a, ctx],
-                        place(zz, pp, exp),
-                    )
-                )
-
     outer_product(q_both, slice(0, head_cols), first_ref, grad_q_ref[...])
     pair_up(1, q_both, q_pair)
     width = middle_ref.shape[1]
@@ -1174,9 +1235,10 @@
     pair_sums(1, q_own, q_pair, q_near)
     pair_sums(0, late_own, late_pair, late_near)
     kv_line.middle()
+    hand_back(0, False)
+    hand_back(1, True)
+    hand_back(1, False)
     kv_line.finish()
-
-    hand_back(0)
 
     projected[:, :head_cols] = grad_q_ref[...]
     projected[:, head_cols:] = kv_own[z]
@@ -1217,6 +1279,14 @@
     k_own = k_both.at[core]
     pair_sums(2, k_own, k_pair, k_near)
 
+    @pl.loop(0, depth // tile)
+    def _(i):
+        at = pl.ds(pl.multiple_of(i * tile, tile), tile)
+        total = base_ref[:, at]
+        for k in range(2):
+            total = total + gates_ref[:, k : k + 1] * dot(picks_ref[k], returned_ref[:, at])
+        block_ref[:, at] = total.astype(BF16)
+
     late_line = line_of(0, late_own, late_up, late_down)
     q_line = line_of(1, q_own, q_up, q_down)
     k_line = line_of(2, k_own, k_up, k_down)
@@ -1233,12 +1303,13 @@
     q_line.finish()
     d_qkv_ref[:, :head_cols] = q_both[core, z, mine_rows, :].astype(F32)
     late_line.finish()
-    d_late_ref[...] = late_both[core, z, mine_rows, :].astype(F32)
+    last = late_both[core, z, mine_rows, :].astype(F32)
+    d_out_ref[...] = last[:, :width]
+    d_aux_ref[:, AUX:] = last[:, width:]
     k_line.finish()
-    hand_back(1)
     last = k_both[core, z, mine_rows, :].astype(F32)
     d_qkv_ref[:, head_cols:] = last[:, :kv_cols]
-    d_aux_ref[...] = last[:, kv_cols:]
+    d_aux_ref[:, :AUX] = last[:, kv_cols:]
 
     for source in range(2 * layers):
         for a in range(2):
@@ -1273,6 +1344,10 @@
     second,
     grad_logits,
     gain_moe,
+    base,
+    returned,
+    picks,
+    gates,
     grad_in,
     grad_down,
     layers,
@@ -1298,14 +1373,15 @@
         functools.partial(finish_kernel, layers),
         out_shape=(
             jax.ShapeDtypeStruct((count, depth), BF16),
+            jax.ShapeDtypeStruct((count, depth), BF16),
             jax.ShapeDtypeStruct((rows, qkv_cols), F32),
-            jax.ShapeDtypeStruct((rows, depth + AUX), F32),
-            jax.ShapeDtypeStruct((rows, AUX), F32),
+            jax.ShapeDtypeStruct((rows, depth), F32),
+            jax.ShapeDtypeStruct((rows, 2 * AUX), F32),
             jax.ShapeDtypeStruct((layers, n_in, 2 * grad_in.shape[1]), BF16),
             jax.ShapeDtypeStruct((layers, n_down, 2 * grad_down.shape[1]), BF16),
         ),
-        in_specs=[any_space] + [vmem] * 5 + [any_space] + [vmem] * 4 + [any_space] * 2,
-        out_specs=(vmem,) * 4 + (any_space,) * 2,
+        in_specs=[any_space] + [vmem] * 5 + [any_space] + [vmem] * 8 + [any_space] * 2,
+        out_specs=(vmem,) * 5 + (any_space,) * 2,
         scratch_shapes=[
             pltpu.VMEM((depth // 2, qkv_cols), BF16),
             pltpu.VMEM((count, qkv_cols), BF16),
@@ -1317,16 +1393,18 @@
         + sums(grad_kv.shape[1] + AUX)
         + [
             dma((2 * layers + 3,)),
-            dma((3, layers)),
-            dma((3, layers)),
+            dma((layers,)),
+            dma((layers,)),
+            dma((2, layers, 2)),
+            dma((2, layers, 2)),
             dma((2, 2 * layers)),
             dma((2, 2 * layers)),
             dma((3, layers)),
             dma((3, layers)),
             dma((3, 3, layers)),
             dma((3, 3, layers)),
-            dma((3, 2, layers)),
-            dma((3, 2, layers)),
+            dma((3, 2, layers, 1)),
+            dma((3, 2, layers, 1)),
         ],
         compiler_params=pltpu.CompilerParams(
             collective_id=1, has_side_effects=True, vmem_limit_bytes=60 * 2**20
@@ -1344,9 +1422,41 @@
         second,
         grad_logits,
         gain_moe,
+        base,
+        returned,
+        picks,
+        gates,
         grad_in,
         grad_down,
     )
+
+
+def settle_kernel(*refs):
+    count = len(refs) // 2
+    for src, dst in zip(refs[:count], refs[count:]):
+        dst[...] = src[...].astype(dst.dtype)
+
+
+def settle(arrays, steps):
+    def spec(array):
+        if array.ndim == 2 and array.shape[0] % (16 * steps) == 0:
+            return pl.BlockSpec((array.shape[0] // steps, array.shape[1]), lambda i: (i, 0))
+        if array.ndim == 3 and array.shape[1] % (16 * steps) == 0:
+            return pl.BlockSpec(
+                (array.shape[0], array.shape[1] // steps, array.shape[2]), lambda i: (0, i, 0)
+            )
+        return pl.BlockSpec(array.shape, lambda i: (0,) * array.ndim)
+
+    specs = [spec(array) for array, _ in arrays]
+    return pl.pallas_call(
+        settle_kernel,
+        grid=(steps,),
+        out_shape=[jax.ShapeDtypeStruct(array.shape, dtype) for array, dtype in arrays],
+        in_specs=specs,
+        out_specs=specs,
+        compiler_params=pltpu.CompilerParams(vmem_limit_bytes=60 * 2**20),
+        name="settle",
+    )(*[array for array, _ in arrays])
 
 
 CTX = ("le", "rep", "core")
@@ -1544,10 +1654,8 @@
         lengths, block_order, mine, projected, kv, grad_attended, lse, exact
     )
     grad_queries, grad_kv, returned = lax.optimization_barrier((grad_queries, grad_kv, returned))
-    picked = [dot(p, returned) for p in pick_hot]
-    block_out = (middle + gates[:, 0:1] * picked[0] + gates[:, 1:2] * picked[1]).astype(BF16)
     if special:
-        grad_inputs, sum_qkv, sum_late, sum_aux, sum_in, sum_down = finish(
+        block_out, grad_inputs, sum_qkv, sum_out, sum_aux, sum_in, sum_down = finish(
             grad_kv,
             grad_queries,
             first,
@@ -1559,9 +1667,24 @@
             second,
             jnp.pad(grad_logits, ((0, 0), (1, AUX - 1 - EXPERTS))),
             grad_gain_second[None, :],
+            middle,
+            returned,
+            jnp.stack(pick_hot),
+            gates,
             grad_in,
             grad_down,
             exp_local,
+        )
+        block_out, grad_inputs, sum_qkv, sum_out, sum_in, sum_down = settle(
+            (
+                (block_out, BF16),
+                (grad_inputs, BF16),
+                (sum_qkv, F32),
+                (sum_out, F32),
+                (sum_in, F32),
+                (sum_down, F32),
+            ),
+            4,
         )
     else:
         grad_router = dot(second, grad_logits, ((0,), (0,)))
@@ -1583,7 +1706,10 @@
         last = jnp.pad(grad_gain_first[:, None], ((0, 0), (0, AUX - 1)))
         part = jnp.concatenate([grad_qkv.astype(BF16), last.astype(BF16), late], axis=1)
         total = lax.psum_scatter(part, ALL, scatter_dimension=0, tiled=True).astype(F32)
-        sum_qkv, sum_aux, sum_late = total[:, :cols], total[:, cols : cols + AUX], total[:, cols + AUX :]
+        sum_qkv, sum_out = total[:, :cols], total[:, cols + AUX : cols + AUX + D]
+        sum_aux = jnp.concatenate([total[:, cols : cols + AUX], total[:, cols + AUX + D :]], axis=1)
+        picked = [dot(p, returned) for p in pick_hot]
+        block_out = (middle + gates[:, 0:1] * picked[0] + gates[:, 1:2] * picked[1]).astype(BF16)
 
         def to_rows(half, rows):
             width = half.shape[1]
@@ -1600,9 +1726,9 @@
         grad_inputs[None],
         sum_aux[:, 0],
         sum_qkv,
-        sum_late[:, :D],
-        sum_late[:, D],
-        sum_late[:, D + 1 : D + 1 + EXPERTS],
+        sum_out,
+        sum_aux[:, AUX],
+        sum_aux[:, AUX + 1 : AUX + 1 + EXPERTS],
         sum_in.astype(F32),
         sum_down.astype(F32),
     )

time: 643 us -> 601 us (0.935)
  Pallas kernels: 504 us -> 466 us
  waiting for transfers between devices: 35.4 us -> 51.7 us
    pallas_call x1, Pallas kernels: 179 us -> 161 us  [finish(): pl.pallas_call(functools.partial(finish_kernel, layers), out_shape=(jax.S...]
    all_to_all x2, waiting for transfers between devices: 35.4 us -> 51.7 us  [to_experts(): lax.all_to_all(rows.reshape((EXPERTS, CAP) + rows.shape[1:]), OWNERS, spl...]
    pallas_call x1, Pallas kernels: 163 us -> 150 us  [front(): pl.pallas_call(functools.partial(front_kernel, layers), out_shape=(jax.Sh...]
    pallas_call x1, Pallas kernels: 24.3 us -> 13.5 us  [attend_back(): pl.pallas_call(functools.partial(attend_back_kernel, lengths.shape[1]), o...]
    pallas_call x1, Pallas kernels: 19.1 us -> 8.62 us  [attend(): pl.pallas_call(functools.partial(attend_kernel, lengths.shape[1]), out_sh...]
    pallas_call x0 -> x1, Pallas kernels: none -> 7.84 us  [settle(): pl.pallas_call(settle_kernel, grid=(steps,), out_shape=[jax.ShapeDtypeStr...]
    dot_general x10 -> x8, matrix products: 26.8 us -> 20.6 us  [dot(): return lax.dot_general(a, b, (dims, ((), ())), preferred_element_type=F32)]
  transfers between devices with their start and end apart: 2 -> 2, of which waited for: 2 -> 2; matrix products, arithmetic and copies ran while one was open for 4% -> 5% of each run, Pallas kernels for 7% -> 4%
where the time goes in v5:
time: 601 us; the launch traced here: 592 us
  Pallas kernels  466 us (78%)
  waiting for transfers between devices  51.7 us (9%)
  starting transfers between devices  33.8 us (6%)
  matrix products  20.6 us (3%)
  local copies, waits for them, and re-layouts  11.9 us (2%)
  other arithmetic  6.06 us (1%)
    pallas_call x1, Pallas kernels, finish(): pl.pallas_call(functools.partial(finish_kernel, layers), out_shape=(jax.S...  161 us
    pallas_call x1, Pallas kernels, front(): pl.pallas_call(functools.partial(front_kernel, layers), out_shape=(jax.Sh...  150 us
    pallas_call x1, Pallas kernels, experts(): pl.pallas_call(functools.partial(experts_kernel, layers), out_shape=(jax....  125 us
    all_to_all x2, waiting for transfers between devices, to_experts(): lax.all_to_all(rows.reshape((EXPERTS, CAP) + rows.shape[1:]), OWNERS, spl...  51.7 us
    all_to_all x2, starting transfers between devices, to_experts(): lax.all_to_all(rows.reshape((EXPERTS, CAP) + rows.shape[1:]), OWNERS, spl...  33.8 us
    dot_general x8, matrix products, dot(): return lax.dot_general(a, b, (dims, ((), ())), preferred_element_type=F32)  20.6 us
    pallas_call x1, Pallas kernels, attend_back(): pl.pallas_call(functools.partial(attend_back_kernel, lengths.shape[1]), o...  13.5 us
  transfers between devices with their start and end apart: 2, of which 2 were waited for; matrix products, arithmetic and copies ran while one was open for 5% of the time, Pallas kernels for 4%

profile of v5, /device:TPU:8, one launch (start us, length us, event | category | flops | bytes accessed | tf_op | source)
XLA Modules:
  0.0 591.5 jit_solution(2920224329123972958)
XLA Ops:
  0.7 0.9 copy.72
  2.9 2.2 convolution_convert_fusion.1
  5.2 149.7 %front.1 = (bf16[1536,4224]{1,0:T(8,128)(2,1)}, bf16[1536,2048]{1,0:T(8,128)(2,1)}, bf16[1024,1536]{1,0:T(8,128)(2,1)}, bf16[256,1536]{1,0:T(8,128)(2,1)S(1)}, b...) custom-call(bf16[48,4224]{1,0:T(8,128)(2,1)S(1)} %pad_maximum_fusion.shard_ref, f32[4,192,2048]{2,1,0:T(8,128)} %in_ref.1, ...), custom_call_target="tpu_custom_call" | custom-call | tf_op jit(solution)/shard_map/front/pallas_call | solution.py:598
  154.9 0.9 copy-done.3
  155.8 18.1 %all-to-all-start = ((bf16[16,48,1536]{2,1,0:T(8,128)(2,1)}), bf16[16,48,1536]{2,1,0:T(8,128)(2,1)}, u32[]{:S(2)}, u32[]{:S(2)}) async-start(bf16[16,48,1536]{2,1,0:T(8,128)(2,1)} %bitcast.32), calls=%async_computation | async-start | bytes 4718592 | tf_op jit(solution)/shard_map/all_to_all | solution.py:1532
  174.0 1.6 convert_reduce_fusion
  175.6 8.6 %attend.1 = (f32[256,1536]{1,0:T(8,128)S(1)}, bf16[256,1536]{1,0:T(8,128)(2,1)S(1)}, f32[2,8,384]{2,1,0:T(8,128)S(1)}) custom-call(s32[1,3]{1,0:T(1,128)S(1)} %copy-done.6, s32[1,16]{1,0:T(1,128)S(1)} %copy-done.7, s32[1]{0:T(128)} %bitcast.mine_ref, bf16[256,2560]{1,0:T(8,128)(2,1)S(1)} %get-tuple-element.43.q_ref, bf16[2048,1024]{1,0:T(8,128)(2,1)} %get-tuple-element.45.kv_ref), custom_call_target="tpu_custom_call" | custom-call | flops 10000000000 | bytes 10000000 | tf_op jit(solution)/shard_map/attend/pallas_call | solution.py:137
  184.3 4.7 multiply_reduce_fusion.2
  189.6 1.7 fusion.29
  192.3 2.2 convolution_convert_fusion
  194.5 31.3 %all-to-all-done.grads_ref = bf16[16,48,1536]{2,1,0:T(8,128)(2,1)} async-done(((bf16[16,48,1536]{2,1,0:T(8,128)(2,1)}), bf16[16,48,1536]{2,1,0:T(8,128)(2,1)}, u32[]{:S(2)}, u32[]{:S(2)}) %all-to-all-start) | async-done | bytes 2359328 | tf_op jit(solution)/shard_map/all_to_all | solution.py:1532
  225.7 0.6 broadcast_in_dim.91.gates_ref
  226.4 124.9 %experts.1 = (bf16[16,48,1536]{2,1,0:T(8,128)(2,1)}, bf16[16,48,1536]{2,1,0:T(8,128)(2,1)}, f32[16,8,128]{2,1,0:T(8,128)}, bf16[1536,1024]{1,0:T(8,128)(2,1)}, bf16[1024,768]{1,0:T(8,128)(2,1)}) custom-call(bf16[16,48,1536]{2,1,0:T(8,128)(2,1)} %bitcast.31, f32[16,8,128]{2,1,0:T(8,128)} %broadcast_in_dim.91.gates_ref, ...), custom_call_target="tpu_custom_call" | custom-call | tf_op jit(solution)/shard_map/experts/pallas_call | solution.py:868
  351.2 15.6 %all-to-all-start.1 = ((bf16[16,48,1536]{2,1,0:T(8,128)(2,1)}), bf16[16,48,1536]{2,1,0:T(8,128)(2,1)S(1)}, u32[]{:S(2)}, u32[]{:S(2)}) async-start(bf16[16,48,1536]{2,1,0:T(8,128)(2,1)} %get-tuple-element.57), calls=%async_computation.1 | async-start | bytes 4718592 | tf_op jit(solution)/shard_map/all_to_all | solution.py:1532
  366.9 0.6 reshape.232.gain_ref
  367.8 1.0 add_convert_fusion.picks_ref
  368.8 0.9 slice_reduce_fusion.6
  370.6 0.7 fusion.43
  371.4 0.7 select_reduce_fusion.2
  372.2 2.6 fusion.19
  374.9 1.7 multiply_reduce_fusion
  376.6 0.6 broadcast_in_dim.95.gain_moe_ref
  377.2 0.7 pad.15.logits_ref
  378.4 5.2 fusion.7.grad_ref
  383.6 13.5 %attend_back.1 = (bf16[256,1536]{1,0:T(8,128)(2,1)}, bf16[2048,1024]{1,0:T(8,128)(2,1)}) custom-call(s32[1,3]{1,0:T(1,128)} %lengths_ref.3, s32[1,16]{1,0:T(1,128)} %order_ref.3, s32[1]{0:T(128)} %bitcast.mine_ref, bf16[256,2560]{1,0:T(8,128)(2,1)} %copy-done.2, bf16[2048,1024]{1,0:T(8,128)(2,1)} %get-tuple-element.45.kv_ref, ...), custom_call_target="tpu_custom_call" | custom-call | flops 1000000000 | bytes 1000000 | tf_op jit(solution)/shard_map/attend_back/pallas_call | solution.py:249
  397.1 20.5 %all-to-all-done.1 = bf16[16,48,1536]{2,1,0:T(8,128)(2,1)S(1)} async-done(((bf16[16,48,1536]{2,1,0:T(8,128)(2,1)}), bf16[16,48,1536]{2,1,0:T(8,128)(2,1)S(1)}, u32[]{:S(2)}, u32[]{:S(2)}) %all-to-all-start.1) | async-done | bytes 2359328 | tf_op jit(solution)/shard_map/all_to_all | solution.py:1532
  417.5 1.4 copy-done.11
  418.9 161.4 %finish.1 = (bf16[256,1536]{1,0:T(8,128)(2,1)}, bf16[256,1536]{1,0:T(8,128)(2,1)}, f32[48,2560]{1,0:T(8,128)}, f32[48,1536]{1,0:T(8,128)}, f32[48,256]{1,0:T(8,1...) custom-call(bf16[2048,1024]{1,0:T(8,128)(2,1)} %get-tuple-element.58.grad_kv_ref, ...), custom_call_target="tpu_custom_call" | custom-call | tf_op jit(solution)/shard_map/finish/pallas_call | solution.py:1372
  580.4 0.8 slice.53
  581.2 1.4 slice_reduce_fusion.4
  582.6 0.7 copy.80
  583.2 7.8 %settle.1 = (bf16[256,1536]{1,0:T(8,128)(2,1)}, bf16[256,1536]{1,0:T(8,128)(2,1)}, f32[48,2560]{1,0:T(8,128)}, f32[48,1536]{1,0:T(8,128)}, f32[4,192,2048]{2,1,0:T(8,128)}, /*index=5*/f32[4,128,1536]{2,1,0:T(8,128)}) custom-call(bf16[256,1536]{1,0:T(8,128)(2,1)} %get-tuple-element.64.refs_0_, bf16[256,1536]{1,0:T(8,128)(2,1)} %get-tuple-element.65.refs_1_, ...), custom_call_target="tpu_custom_call" | custom-call | tf_op jit(solution)/shard_map/settle/pallas_call | solution.py:1451
  (86 shorter events, 4.7 us)
Async XLA Ops:
  0.6 1.8 copy-start.15
  0.7 1.8 copy-start.16
  0.7 1.9 copy-start.21
  0.7 2.0 copy-start.22
  0.7 2.1 copy-start.23
  0.7 2.2 copy-start.13
  2.9 2.3 copy-start
  154.9 0.9 copy-start.3
  155.8 19.8 %copy-start.2 = (bf16[256,2560]{1,0:T(8,128)(2,1)}, bf16[256,2560]{1,0:T(8,128)(2,1)S(1)}, u32[]{:S(2)}) copy-start(bf16[256,2560]{1,0:T(8,128)(2,1)S(1)} %get-tuple-element.43.q_ref) | copy-start | bytes 3932164
  155.8 19.8 %copy-start.6 = (s32[1,3]{1,0:T(1,128)S(1)}, s32[1,3]{1,0:T(1,128)}, u32[]{:S(2)}) copy-start(s32[1,3]{1,0:T(1,128)} %lengths_ref.3) | copy-start | bytes 40
  155.8 19.8 %copy-start.7 = (s32[1,16]{1,0:T(1,128)S(1)}, s32[1,16]{1,0:T(1,128)}, u32[]{:S(2)}) copy-start(s32[1,16]{1,0:T(1,128)} %order_ref.3) | copy-start | bytes 196
  155.8 70.0 %all-to-all-start = ((bf16[16,48,1536]{2,1,0:T(8,128)(2,1)}), bf16[16,48,1536]{2,1,0:T(8,128)(2,1)}, u32[]{:S(2)}, u32[]{:S(2)}) async-start(bf16[16,48,1536]{2,1,0:T(8,128)(2,1)} %bitcast.32), calls=%async_computation | async-start | bytes 4718592 | tf_op jit(solution)/shard_map/all_to_all | solution.py:1532
  174.0 17.3 %copy-start.17 = (s32[256,2]{0,1:T(2,128)}, s32[256,2]{0,1:T(2,128)S(1)}, u32[]{:S(2)}) copy-start(s32[256,2]{0,1:T(2,128)S(1)} %copy.74) | copy-start | bytes 6148
  184.2 4.7 copy-start.1
  184.2 4.7 copy-start.4
  184.2 4.7 copy-start.5
  188.9 2.4 copy-start.8
  189.0 0.6 copy-start.18
  189.6 4.9 copy-start.10
  191.5 178.7 %copy-start.20 = (f32[256]{0:T(256)}, f32[256]{0:T(256)S(1)}, u32[]{:S(2)}) copy-start(f32[256]{0:T(256)S(1)} %get-tuple-element.143) | copy-start | bytes 3076
  191.7 2.7 copy-start.14
  351.2 66.3 %all-to-all-start.1 = ((bf16[16,48,1536]{2,1,0:T(8,128)(2,1)}), bf16[16,48,1536]{2,1,0:T(8,128)(2,1)S(1)}, u32[]{:S(2)}, u32[]{:S(2)}) async-start(bf16[16,48,1536]{2,1,0:T(8,128)(2,1)} %get-tuple-element.57), calls=%async_computation.1 | async-start | bytes 4718592 | tf_op jit(solution)/shard_map/all_to_all | solution.py:1532
  372.2 2.7 copy-start.9
  372.2 2.7 copy-start.19
  378.4 5.2 copy-start.12
  417.5 1.4 copy-start.11

commit v6 on v5

--- a/solution.py
+++ b/solution.py
@@ -39,10 +39,11 @@
     return (lane >= HEAD) if half else (lane < HEAD)
 
 
-def head_tiles(ref, rows, group, scale):
+def head_tiles(ref, rows, pair, scale):
     tiles = []
-    for i in range(GROUP):
-        head = group * GROUP + i
+    for i in range(2 * GROUP):
+        head = pair * 2 * GROUP + i
+        group = head // GROUP
         tile = ref[rows, (head // 2) * 128 : (head // 2 + 1) * 128].astype(F32)
         if head % 2 != group % 2:
             tile = pltpu.roll(tile, HEAD, 1)
@@ -61,7 +62,7 @@
         start = jnp.where(query_pos >= bound, bound, start)
     key_pos = key_block * BLK + lax.broadcasted_iota(jnp.int32, (BLK, BLK), 0)
     one = ((key_pos >= start) & (key_pos <= query_pos)).astype(jnp.int32)
-    return jnp.concatenate([one] * GROUP, axis=1) > 0
+    return jnp.concatenate([one] * (2 * GROUP), axis=1) > 0
 
 
 def first_row_start(lengths_ref, query_block, parts):
@@ -74,15 +75,17 @@
 
 
 def attend_kernel(
-    parts, lengths_ref, order_ref, mine_ref, q_ref, kv_ref, exact_ref, out_ref, lse_ref, q_s, m_s, acc_s
+    parts, lengths_ref, order_ref, mine_ref, q_ref, kv_ref, exact_ref, out_ref, lse_ref, q_s, m_s, sum_s, acc_s
 ):
     width = KV_HEADS * HEAD
+    wide = 2 * GROUP * BLK
     for qb in range(q_ref.shape[0] // BLK):
         rows = pl.ds(qb * BLK, BLK)
-        for g in range(KV_HEADS):
-            q_s[g] = head_tiles(q_ref, rows, g, HEAD**-0.5)
-            m_s[g] = jnp.full((8, GROUP * BLK), start_max, F32)
-            acc_s[g] = jnp.zeros((BLK, GROUP * BLK), F32)
+        for pair in range(KV_HEADS // 2):
+            q_s[pair] = head_tiles(q_ref, rows, pair, HEAD**-0.5)
+            m_s[pair] = jnp.full((8, wide), start_max, F32)
+            sum_s[pair] = jnp.zeros((8, wide), F32)
+            acc_s[pair] = jnp.zeros((BLK, wide), F32)
         query_block = order_ref[0, mine_ref[0] + qb]
         first = first_row_start(lengths_ref, query_block, parts)
 
@@ -94,32 +97,30 @@
             def _():
                 seen = block_visibility(lengths_ref, query_block, key_block, parts)
                 key_rows = pl.ds(kb * BLK, BLK)
-                for g in range(KV_HEADS):
-                    lanes = pl.ds((g // 2) * 128, 128)
-                    keys = kv_ref[key_rows, lanes]
-                    values = kv_ref[key_rows, pl.ds(width + (g // 2) * 128, 128)]
-                    values = jnp.where(lane_half(values.shape, g % 2), values, jnp.ones_like(values))
-                    scores = dot(keys, q_s[g], ((1,), (1,)))
+                for pair in range(KV_HEADS // 2):
+                    keys = kv_ref[key_rows, pl.ds(pair * 128, 128)]
+                    values = kv_ref[key_rows, pl.ds(width + pair * 128, 128)]
+                    scores = dot(keys, q_s[pair], ((1,), (1,)))
                     scores = jnp.where(seen, scores, far_negative)
-                    old = m_s[g, 0:1, :]
+                    old = m_s[pair, 0:1, :]
                     new = jnp.maximum(old, jnp.max(scores, axis=0, keepdims=True))
                     weights = jnp.exp(scores - new)
-                    acc_s[g] = acc_s[g] * jnp.exp(old - new) + dot(
-                        values, weights.astype(BF16), ((0,), (0,))
+                    factor = jnp.exp(old - new)
+                    sum_s[pair, 0:1, :] = sum_s[pair, 0:1, :] * factor + jnp.sum(
+                        weights, axis=0, keepdims=True
                     )
-                    m_s[g, 0:1, :] = new
+                    acc_s[pair] = acc_s[pair] * factor + dot(values, weights.astype(BF16), ((0,), (0,)))
+                    m_s[pair, 0:1, :] = new
 
         tiles = []
-        for g in range(KV_HEADS):
-            acc = acc_s[g]
-            at = (1 - g % 2) * HEAD
-            total = acc[at : at + 1, :]
-            lse_ref[qb, g : g + 1, :] = m_s[g, 0:1, :] + jnp.log(total)
-            acc = acc / total
-            for i in range(GROUP):
-                head = g * GROUP + i
+        for pair in range(KV_HEADS // 2):
+            total = sum_s[pair, 0:1, :]
+            lse_ref[qb, pair : pair + 1, :] = m_s[pair, 0:1, :] + jnp.log(total)
+            acc = acc_s[pair] / total
+            for i in range(2 * GROUP):
+                head = pair * 2 * GROUP + i
                 tile = jnp.transpose(acc[:, i * BLK : (i + 1) * BLK])
-                if head % 2 != g % 2:
+                if head % 2 != (head // GROUP) % 2:
                     tile = pltpu.roll(tile, HEAD, 1)
                 tiles.append(tile)
                 if head % 2 == 1:
@@ -133,20 +134,22 @@
     rows = projected.shape[0]
     smem = pl.BlockSpec(memory_space=pltpu.SMEM)
     vmem = pl.BlockSpec(memory_space=pltpu.VMEM)
-    wide = GROUP * BLK
+    wide = 2 * GROUP * BLK
+    pairs = KV_HEADS // 2
     return pl.pallas_call(
         functools.partial(attend_kernel, lengths.shape[1]),
         out_shape=(
             jax.ShapeDtypeStruct((rows, HEADS * HEAD), F32),
             jax.ShapeDtypeStruct((rows, HEADS * HEAD), BF16),
-            jax.ShapeDtypeStruct((rows // BLK, KV_HEADS, wide), F32),
+            jax.ShapeDtypeStruct((rows // BLK, pairs, wide), F32),
         ),
         in_specs=[smem, smem, smem, vmem, vmem],
         out_specs=(vmem, vmem, vmem),
         scratch_shapes=[
-            pltpu.VMEM((KV_HEADS, wide, 128), BF16),
-            pltpu.VMEM((KV_HEADS, 8, wide), F32),
-            pltpu.VMEM((KV_HEADS, BLK, wide), F32),
+            pltpu.VMEM((pairs, wide, 128), BF16),
+            pltpu.VMEM((pairs, 8, wide), F32),
+            pltpu.VMEM((pairs, 8, wide), F32),
+            pltpu.VMEM((pairs, BLK, wide), F32),
         ],
         compiler_params=pltpu.CompilerParams(vmem_limit_bytes=48 * 2**20),
         cost_estimate=pl.CostEstimate(flops=10**10, bytes_accessed=10**7, transcendentals=10**7),
@@ -180,17 +183,17 @@
 
     for qb in range(q_ref.shape[0] // BLK):
         rows = pl.ds(qb * BLK, BLK)
-        for g in range(KV_HEADS):
-            q_s[g] = head_tiles(q_ref, rows, g, HEAD**-0.5)
-            g_s[g] = head_tiles(grad_ref, rows, g, 1.0)
-            dq_s[g] = jnp.zeros((GROUP * BLK, 128), F32)
-            for i in range(GROUP):
-                head = g * GROUP + i
+        for pair in range(KV_HEADS // 2):
+            q_s[pair] = head_tiles(q_ref, rows, pair, HEAD**-0.5)
+            g_s[pair] = head_tiles(grad_ref, rows, pair, 1.0)
+            dq_s[pair] = jnp.zeros((2 * GROUP * BLK, 128), F32)
+            for i in range(2 * GROUP):
+                head = pair * 2 * GROUP + i
                 exact = exact_ref[rows, (head // 2) * 128 : (head // 2 + 1) * 128]
-                if head % 2 != g % 2:
+                if head % 2 != (head // GROUP) % 2:
                     exact = pltpu.roll(exact, HEAD, 1)
-                product = exact * g_s[g, i * BLK : (i + 1) * BLK, :].astype(F32)
-                delta_s[g : g + 1, i * BLK : (i + 1) * BLK] = jnp.sum(
+                product = exact * g_s[pair, i * BLK : (i + 1) * BLK, :].astype(F32)
+                delta_s[pair : pair + 1, i * BLK : (i + 1) * BLK] = jnp.sum(
                     jnp.transpose(product), axis=0, keepdims=True
                 )
         query_block = order_ref[0, mine_ref[0] + qb]
@@ -209,26 +212,21 @@
                     value_lanes = pl.ds(width + pair * 128, 128)
                     keys = kv_ref[key_rows, key_lanes]
                     values = kv_ref[key_rows, value_lanes]
-                    grad_keys = dkv_s[key_rows, key_lanes]
-                    grad_values = dkv_s[key_rows, value_lanes]
-                    for g in (2 * pair, 2 * pair + 1):
-                        scores = dot(keys, q_s[g], ((1,), (1,)))
-                        scores = jnp.where(seen, scores, far_negative)
-                        probs = jnp.exp(scores - lse_ref[qb, g : g + 1, :])
-                        grad_probs = dot(values, g_s[g], ((1,), (1,)))
-                        grad_scores = (probs * (grad_probs - delta_s[g : g + 1, :])).astype(BF16)
-                        grad_values = grad_values + dot(probs.astype(BF16), g_s[g])
-                        grad_keys = grad_keys + dot(grad_scores, q_s[g])
-                        dq_s[g] += dot(grad_scores, keys, ((0,), (0,)))
-                    dkv_s[key_rows, key_lanes] = grad_keys
-                    dkv_s[key_rows, value_lanes] = grad_values
+                    scores = dot(keys, q_s[pair], ((1,), (1,)))
+                    scores = jnp.where(seen, scores, far_negative)
+                    probs = jnp.exp(scores - lse_ref[qb, pair : pair + 1, :])
+                    grad_probs = dot(values, g_s[pair], ((1,), (1,)))
+                    grad_scores = (probs * (grad_probs - delta_s[pair : pair + 1, :])).astype(BF16)
+                    dkv_s[key_rows, value_lanes] += dot(probs.astype(BF16), g_s[pair])
+                    dkv_s[key_rows, key_lanes] += dot(grad_scores, q_s[pair])
+                    dq_s[pair] += dot(grad_scores, keys, ((0,), (0,)))
 
         tiles = []
-        for g in range(KV_HEADS):
-            for i in range(GROUP):
-                head = g * GROUP + i
-                tile = dq_s[g, i * BLK : (i + 1) * BLK, :] * HEAD**-0.5
-                if head % 2 != g % 2:
+        for pair in range(KV_HEADS // 2):
+            for i in range(2 * GROUP):
+                head = pair * 2 * GROUP + i
+                tile = dq_s[pair, i * BLK : (i + 1) * BLK, :] * HEAD**-0.5
+                if head % 2 != (head // GROUP) % 2:
                     tile = pltpu.roll(tile, HEAD, 1)
                 tiles.append(tile)
                 if head % 2 == 1:
@@ -245,7 +243,8 @@
     rows = projected.shape[0]
     smem = pl.BlockSpec(memory_space=pltpu.SMEM)
     vmem = pl.BlockSpec(memory_space=pltpu.VMEM)
-    wide = GROUP * BLK
+    wide = 2 * GROUP * BLK
+    pairs = KV_HEADS // 2
     return pl.pallas_call(
         functools.partial(attend_back_kernel, lengths.shape[1]),
         out_shape=(
@@ -255,10 +254,10 @@
         in_specs=[smem, smem, smem, vmem, vmem, vmem, vmem, vmem],
         out_specs=(vmem, vmem),
         scratch_shapes=[
-            pltpu.VMEM((KV_HEADS, wide, 128), BF16),
-            pltpu.VMEM((KV_HEADS, wide, 128), BF16),
-            pltpu.VMEM((KV_HEADS, wide), F32),
-            pltpu.VMEM((KV_HEADS, wide, 128), F32),
+            pltpu.VMEM((pairs, wide, 128), BF16),
+            pltpu.VMEM((pairs, wide, 128), BF16),
+            pltpu.VMEM((pairs, wide), F32),
+            pltpu.VMEM((pairs, wide, 128), F32),
             pltpu.VMEM(kv.shape, F32),
         ],
         compiler_params=pltpu.CompilerParams(vmem_limit_bytes=56 * 2**20),
@@ -293,9 +292,13 @@
     )
 
 
-def between(z, layers, offset):
-    low = layers // 2 - 1
-    return ((z == low) & (offset == 1)) | ((z == low + 1) & (offset == layers - 1))
+def near_to_far(z):
+    first_half = z < 2
+    return [z, z + 1 - 2 * (z % 2), jnp.where(first_half, 3, 0), jnp.where(first_half, 2, 1)]
+
+
+def between(z, zz):
+    return ((z == 1) & (zz == 2)) | ((z == 2) & (zz == 1))
 
 
 def meet(devices):
@@ -342,8 +345,8 @@
     x, y = x_of(exp), y_of(exp)
     ctx = z * 2 + core
     rows = shard_ref.shape[0]
-    offsets = (2, 1, 3, 0)
-    order = [(z + s) % layers for s in offsets]
+    own_layer, mate, farthest, middle = near_to_far(z)
+    order = [mate, farthest, middle, own_layer]
     wides = ((in_ref, in_wide), (down_ref, down_wide))
     halves = ((in_half, w_in_ref), (down_half, w_down_ref))
 
@@ -417,11 +420,14 @@
     def layer(k):
         return jnp.where(z < layers // 2, k, layers - 1 - k)
 
+    def ahead(zz):
+        return between(z, zz)
+
     def hand_out(a, early):
         for s, zz in enumerate(order):
-            across = between(z, layers, offsets[s])
+            across = ahead(zz)
             for p in range(2):
-                if offsets[s] + p == 0:
+                if s == layers - 1 and p == 0:
                     continue
                 pp = (core + p) % 2
                 copy = remote(
@@ -685,16 +691,10 @@
     ]
     for load in loads:
         load.start()
-    first_half = z < layers // 2
-    by_distance = [
-        z,
-        z + 1 - 2 * (z % 2),
-        jnp.where(first_half, 2, 1),
-        jnp.where(first_half, 3, 0),
-    ]
+    own_layer, mate, farthest, middle = near_to_far(z)
     peers = [
         (zz, (exp + t) % columns)
-        for s, zz in enumerate(by_distance[::-1])
+        for s, zz in enumerate([mate, farthest, middle, own_layer])
         for t in range(columns)
         if not (s == layers - 1 and t == 0)
     ]
@@ -725,7 +725,7 @@
     def tiles(i):
         return pl.ds(pl.multiple_of(i * tile, tile), tile)
 
-    for k, zz in enumerate(by_distance):
+    for k, zz in enumerate([own_layer, mate, farthest, middle]):
         rows = pl.ds(k * chunk, chunk)
         for ee in range(columns):
             source = ee * layers + zz
@@ -1063,6 +1063,7 @@
     above, below = place(z + 1, core, exp), place(z - 1, core, exp)
     x, y = x_of(exp), y_of(exp)
     mates = (x, y, y_of(x))
+    own_layer, mate, farthest, middle = near_to_far(z)
     ctx = z * 2 + core
     rows = d_qkv_ref.shape[0]
     count = tokens_ref.shape[0]
@@ -1118,12 +1119,12 @@
         load(mine(a, ctx), half(a, z, core))
 
     def hand_back(a, early):
-        for s in (2, 1, 3, 0):
-            across = between(z, layers, s)
+        for s, zz in enumerate([mate, farthest, middle, own_layer]):
+            across = between(z, zz)
             for p in range(2):
-                if s + p == 0:
+                if s == layers - 1 and p == 0:
                     continue
-                zz, pp = (z + s) % layers, (core + p) % 2
+                pp = (core + p) % 2
                 copy = remote(
                     mine(a, zz * 2 + pp),
                     half(a, z, core),

time: 601 us -> 580 us (0.965)
  waiting for transfers between devices: 51.7 us -> 27.3 us
  Pallas kernels: 466 us -> 480 us
  starting transfers between devices: 33.8 us -> 27 us
    all_to_all x2, waiting for transfers between devices: 51.7 us -> 27.3 us  [to_experts(): lax.all_to_all(rows.reshape((EXPERTS, CAP) + rows.shape[1:]), OWNERS, spl...]
    pallas_call x1, Pallas kernels: 13.5 us -> 25.1 us  [attend_back(): pl.pallas_call(functools.partial(attend_back_kernel, lengths.shape[1]), o...]
    pallas_call x1, Pallas kernels: 8.62 us -> 19.8 us  [attend(): pl.pallas_call(functools.partial(attend_kernel, lengths.shape[1]), out_sh...]
    pallas_call x1, Pallas kernels: 125 us -> 117 us  [experts(): pl.pallas_call(functools.partial(experts_kernel, layers), out_shape=(jax....]
    all_to_all x2, starting transfers between devices: 33.8 us -> 27 us  [to_experts(): lax.all_to_all(rows.reshape((EXPERTS, CAP) + rows.shape[1:]), OWNERS, spl...]
  transfers between devices with their start and end apart: 2 -> 2, of which waited for: 2 -> 2; matrix products, arithmetic and copies ran while one was open for 5% -> 5% of each run, Pallas kernels for 4% -> 8%
where the time goes in v6:
time: 580 us; the launch traced here: 575 us
  Pallas kernels  480 us (83%)
  waiting for transfers between devices  27.3 us (5%)
  starting transfers between devices  27 us (5%)
  matrix products  20.6 us (4%)
  local copies, waits for them, and re-layouts  11.9 us (2%)
  other arithmetic  6.06 us (1%)
    pallas_call x1, Pallas kernels, finish(): pl.pallas_call(functools.partial(finish_kernel, layers), out_shape=(jax.S...  161 us
    pallas_call x1, Pallas kernels, front(): pl.pallas_call(functools.partial(front_kernel, layers), out_shape=(jax.Sh...  150 us
    pallas_call x1, Pallas kernels, experts(): pl.pallas_call(functools.partial(experts_kernel, layers), out_shape=(jax....  117 us
    all_to_all x2, waiting for transfers between devices, to_experts(): lax.all_to_all(rows.reshape((EXPERTS, CAP) + rows.shape[1:]), OWNERS, spl...  27.3 us
    all_to_all x2, starting transfers between devices, to_experts(): lax.all_to_all(rows.reshape((EXPERTS, CAP) + rows.shape[1:]), OWNERS, spl...  27 us
    pallas_call x1, Pallas kernels, attend_back(): pl.pallas_call(functools.partial(attend_back_kernel, lengths.shape[1]), o...  25.1 us
    dot_general x8, matrix products, dot(): return lax.dot_general(a, b, (dims, ((), ())), preferred_element_type=F32)  20.6 us
    pallas_call x1, Pallas kernels, attend(): pl.pallas_call(functools.partial(attend_kernel, lengths.shape[1]), out_sh...  19.8 us
  transfers between devices with their start and end apart: 2, of which 2 were waited for; matrix products, arithmetic and copies ran while one was open for 5% of the time, Pallas kernels for 8%

profile of v6, /device:TPU:8, one launch (start us, length us, event | category | flops | bytes accessed | tf_op | source)
XLA Modules:
  0.0 574.8 jit_solution(14364292018715718089)
XLA Ops:
  0.7 0.9 copy.72
  2.9 2.2 convolution_convert_fusion.1
  5.2 149.7 %front.1 = (bf16[1536,4224]{1,0:T(8,128)(2,1)}, bf16[1536,2048]{1,0:T(8,128)(2,1)}, bf16[1024,1536]{1,0:T(8,128)(2,1)}, bf16[256,1536]{1,0:T(8,128)(2,1)S(1)}, b...) custom-call(bf16[48,4224]{1,0:T(8,128)(2,1)S(1)} %pad_maximum_fusion.shard_ref, f32[4,192,2048]{2,1,0:T(8,128)} %in_ref.1, ...), custom_call_target="tpu_custom_call" | custom-call | tf_op jit(solution)/shard_map/front/pallas_call | solution.py:604
  155.0 0.9 copy-done.3
  155.8 18.1 %all-to-all-start = ((bf16[16,48,1536]{2,1,0:T(8,128)(2,1)}), bf16[16,48,1536]{2,1,0:T(8,128)(2,1)}, u32[]{:S(2)}, u32[]{:S(2)}) async-start(bf16[16,48,1536]{2,1,0:T(8,128)(2,1)} %bitcast.32), calls=%async_computation | async-start | bytes 4718592 | tf_op jit(solution)/shard_map/all_to_all | solution.py:1533
  174.1 1.6 convert_reduce_fusion
  175.7 19.8 %attend.1 = (f32[256,1536]{1,0:T(8,128)S(1)}, bf16[256,1536]{1,0:T(8,128)(2,1)S(1)}, f32[2,4,768]{2,1,0:T(4,128)S(1)}) custom-call(s32[1,3]{1,0:T(1,128)S(1)} %copy-done.6, s32[1,16]{1,0:T(1,128)S(1)} %copy-done.7, s32[1]{0:T(128)} %bitcast.mine_ref, bf16[256,2560]{1,0:T(8,128)(2,1)S(1)} %get-tuple-element.43.q_ref, bf16[2048,1024]{1,0:T(8,128)(2,1)} %get-tuple-element.45.kv_ref), custom_call_target="tpu_custom_call" | custom-call | flops 10000000000 | bytes 10000000 | tf_op jit(solution)/shard_map/attend/pallas_call | solution.py:139
  195.5 4.7 multiply_reduce_fusion.2
  200.8 1.7 fusion.29
  203.5 2.2 convolution_convert_fusion
  205.7 20.1 %all-to-all-done.grads_ref = bf16[16,48,1536]{2,1,0:T(8,128)(2,1)} async-done(((bf16[16,48,1536]{2,1,0:T(8,128)(2,1)}), bf16[16,48,1536]{2,1,0:T(8,128)(2,1)}, u32[]{:S(2)}, u32[]{:S(2)}) %all-to-all-start) | async-done | bytes 2359328 | tf_op jit(solution)/shard_map/all_to_all | solution.py:1533
  225.8 0.6 broadcast_in_dim.91.gates_ref
  226.5 116.6 %experts.1 = (bf16[16,48,1536]{2,1,0:T(8,128)(2,1)}, bf16[16,48,1536]{2,1,0:T(8,128)(2,1)}, f32[16,8,128]{2,1,0:T(8,128)}, bf16[1536,1024]{1,0:T(8,128)(2,1)}, bf16[1024,768]{1,0:T(8,128)(2,1)}) custom-call(bf16[16,48,1536]{2,1,0:T(8,128)(2,1)} %bitcast.31, f32[16,8,128]{2,1,0:T(8,128)} %broadcast_in_dim.91.gates_ref, ...), custom_call_target="tpu_custom_call" | custom-call | tf_op jit(solution)/shard_map/experts/pallas_call | solution.py:868
  343.0 8.8 %all-to-all-start.1 = ((bf16[16,48,1536]{2,1,0:T(8,128)(2,1)}), bf16[16,48,1536]{2,1,0:T(8,128)(2,1)S(1)}, u32[]{:S(2)}, u32[]{:S(2)}) async-start(bf16[16,48,1536]{2,1,0:T(8,128)(2,1)} %get-tuple-element.57), calls=%async_computation.1 | async-start | bytes 4718592 | tf_op jit(solution)/shard_map/all_to_all | solution.py:1533
  351.9 0.6 reshape.232.gain_ref
  352.8 1.0 add_convert_fusion.picks_ref
  353.7 0.9 slice_reduce_fusion.6
  355.5 0.7 fusion.43
  356.4 0.7 select_reduce_fusion.2
  357.2 2.6 fusion.19
  359.9 1.7 multiply_reduce_fusion
  361.6 0.6 broadcast_in_dim.95.gain_moe_ref
  362.2 0.7 pad.15.logits_ref
  363.4 5.2 fusion.7.grad_ref
  368.6 25.1 %attend_back.1 = (bf16[256,1536]{1,0:T(8,128)(2,1)}, bf16[2048,1024]{1,0:T(8,128)(2,1)}) custom-call(s32[1,3]{1,0:T(1,128)} %lengths_ref.3, s32[1,16]{1,0:T(1,128)} %order_ref.3, s32[1]{0:T(128)} %bitcast.mine_ref, bf16[256,2560]{1,0:T(8,128)(2,1)} %copy-done.2, bf16[2048,1024]{1,0:T(8,128)(2,1)} %get-tuple-element.45.kv_ref, ...), custom_call_target="tpu_custom_call" | custom-call | flops 1000000000 | bytes 1000000 | tf_op jit(solution)/shard_map/attend_back/pallas_call | solution.py:248
  393.6 7.2 %all-to-all-done.1 = bf16[16,48,1536]{2,1,0:T(8,128)(2,1)S(1)} async-done(((bf16[16,48,1536]{2,1,0:T(8,128)(2,1)}), bf16[16,48,1536]{2,1,0:T(8,128)(2,1)S(1)}, u32[]{:S(2)}, u32[]{:S(2)}) %all-to-all-start.1) | async-done | bytes 2359328 | tf_op jit(solution)/shard_map/all_to_all | solution.py:1533
  400.8 1.4 copy-done.11
  402.2 161.4 %finish.1 = (bf16[256,1536]{1,0:T(8,128)(2,1)}, bf16[256,1536]{1,0:T(8,128)(2,1)}, f32[48,2560]{1,0:T(8,128)}, f32[48,1536]{1,0:T(8,128)}, f32[48,256]{1,0:T(8,1...) custom-call(bf16[2048,1024]{1,0:T(8,128)(2,1)} %get-tuple-element.58.grad_kv_ref, ...), custom_call_target="tpu_custom_call" | custom-call | tf_op jit(solution)/shard_map/finish/pallas_call | solution.py:1373
  563.6 0.8 slice.53
  564.4 1.4 slice_reduce_fusion.4
  565.8 0.7 copy.80
  566.5 7.8 %settle.1 = (bf16[256,1536]{1,0:T(8,128)(2,1)}, bf16[256,1536]{1,0:T(8,128)(2,1)}, f32[48,2560]{1,0:T(8,128)}, f32[48,1536]{1,0:T(8,128)}, f32[4,192,2048]{2,1,0:T(8,128)}, /*index=5*/f32[4,128,1536]{2,1,0:T(8,128)}) custom-call(bf16[256,1536]{1,0:T(8,128)(2,1)} %get-tuple-element.64.refs_0_, bf16[256,1536]{1,0:T(8,128)(2,1)} %get-tuple-element.65.refs_1_, ...), custom_call_target="tpu_custom_call" | custom-call | tf_op jit(solution)/shard_map/settle/pallas_call | solution.py:1452
  (86 shorter events, 4.7 us)
Async XLA Ops:
  0.6 1.8 copy-start.15
  0.7 1.8 copy-start.16
  0.7 1.9 copy-start.21
  0.7 2.0 copy-start.22
  0.7 2.1 copy-start.23
  0.7 2.2 copy-start.13
  2.9 2.3 copy-start
  154.9 0.9 copy-start.3
  155.8 19.8 %copy-start.2 = (bf16[256,2560]{1,0:T(8,128)(2,1)}, bf16[256,2560]{1,0:T(8,128)(2,1)S(1)}, u32[]{:S(2)}) copy-start(bf16[256,2560]{1,0:T(8,128)(2,1)S(1)} %get-tuple-element.43.q_ref) | copy-start | bytes 3932164
  155.8 19.8 %copy-start.6 = (s32[1,3]{1,0:T(1,128)S(1)}, s32[1,3]{1,0:T(1,128)}, u32[]{:S(2)}) copy-start(s32[1,3]{1,0:T(1,128)} %lengths_ref.3) | copy-start | bytes 40
  155.8 19.8 %copy-start.7 = (s32[1,16]{1,0:T(1,128)S(1)}, s32[1,16]{1,0:T(1,128)}, u32[]{:S(2)}) copy-start(s32[1,16]{1,0:T(1,128)} %order_ref.3) | copy-start | bytes 196
  155.8 70.0 %all-to-all-start = ((bf16[16,48,1536]{2,1,0:T(8,128)(2,1)}), bf16[16,48,1536]{2,1,0:T(8,128)(2,1)}, u32[]{:S(2)}, u32[]{:S(2)}) async-start(bf16[16,48,1536]{2,1,0:T(8,128)(2,1)} %bitcast.32), calls=%async_computation | async-start | bytes 4718592 | tf_op jit(solution)/shard_map/all_to_all | solution.py:1533
  174.1 28.5 %copy-start.17 = (s32[256,2]{0,1:T(2,128)}, s32[256,2]{0,1:T(2,128)S(1)}, u32[]{:S(2)}) copy-start(s32[256,2]{0,1:T(2,128)S(1)} %copy.74) | copy-start | bytes 6148
  195.5 4.7 copy-start.1
  195.5 4.7 copy-start.4
  195.5 4.7 copy-start.5
  200.2 2.4 copy-start.8
  200.2 0.6 copy-start.18
  200.8 4.9 copy-start.10
  202.7 152.5 %copy-start.20 = (f32[256]{0:T(256)}, f32[256]{0:T(256)S(1)}, u32[]{:S(2)}) copy-start(f32[256]{0:T(256)S(1)} %get-tuple-element.143) | copy-start | bytes 3076
  203.0 2.7 copy-start.14
  343.0 57.7 %all-to-all-start.1 = ((bf16[16,48,1536]{2,1,0:T(8,128)(2,1)}), bf16[16,48,1536]{2,1,0:T(8,128)(2,1)S(1)}, u32[]{:S(2)}, u32[]{:S(2)}) async-start(bf16[16,48,1536]{2,1,0:T(8,128)(2,1)} %get-tuple-element.57), calls=%async_computation.1 | async-start | bytes 4718592 | tf_op jit(solution)/shard_map/all_to_all | solution.py:1533
  357.2 2.7 copy-start.9
  357.2 2.7 copy-start.19
  363.4 5.2 copy-start.12
  400.8 1.4 copy-start.11
